TPU v7x, 32 devices: a whole 2x2x4 slice. The times are simulated.
32 devices in a mesh: gx: 8 (over y, x, core), gy: 4 (over z).
Axes of the slice: x: 2, y: 2, z: 4, core: 2. Of those that a mesh axis runs over, the one named last changes fastest.
Arguments:
- right_side: float32 [128, 64, 128], P('gx', 'gy'), may hold values from -24 to 24
- material: int32 [128, 64, 128], P('gx', 'gy'), may hold values from 0 to 15
- conductivity: float32 [16], replicated, may hold values from 0.2 to 5
Outputs:
- solution_field: float32 [128, 64, 128], P('gx', 'gy')
All inputs are finite; a program needn't handle non-finite values.
Results may differ from a plain program's by a relative error of at most 0.0001.
Values sent between devices are 32-bit elements; how exact they have to be, the bound alone decides.
No kernel may reach another device: no remote copies, remote signals or barrier semaphores. Data moves between devices by JAX's collectives and lax.ppermute only.
A program may use at most 64 MiB of HBM per device.

v0:
```python
import jax
import jax.numpy as jnp
from jax import lax
from jax.sharding import PartitionSpec as P

CYCLES = 2
COARSE_SWEEPS = 6


OMEGA = 0.8


def extended(x, sides, width):
    for axis, dim in sides:
        devices, length = (lax.axis_size(axis), x.shape[dim])
        up = [(i, (i + 1) % devices) for i in range(devices - 1)]
        down = [(j, i) for i, j in up]
        last = lax.slice_in_dim(x, length - width, length, axis=dim)
        first = lax.slice_in_dim(x, 0, width, axis=dim)
        before = lax.ppermute(last, axis, up)
        after = lax.ppermute(first, axis, down)
        x = jnp.concatenate([before, x, after], axis=dim)
    return x


def partner(block, axis, apart):
    count = lax.axis_size(axis)
    route = []
    for low in range(count):
        high = low | 1 << apart
        if high != low and high < count:
            route += [(low, high), (high, low)]
    return lax.ppermute(block, axis, route)


def neighbours(padded):
    return (
        padded[2:, 1:-1, 1:-1],
        padded[:-2, 1:-1, 1:-1],
        padded[1:-1, 2:, 1:-1],
        padded[1:-1, :-2, 1:-1],
        padded[1:-1, 1:-1, 2:],
        padded[1:-1, 1:-1, :-2],
    )


def face_set(padded_k, scale):
    centre = padded_k[1:-1, 1:-1, 1:-1]
    faces = tuple((0.5 * scale * (centre + other) for other in neighbours(padded_k)))
    total = faces[0] + faces[1] + faces[2] + faces[3] + faces[4] + faces[5]
    return (faces, total)


def apply_operator(padded_field, faces, total):
    result = total * padded_field[1:-1, 1:-1, 1:-1]
    for weight, other in zip(faces, neighbours(padded_field)):
        result = result - weight * other
    return result


def restrict(field):
    sx, sy, sz = field.shape
    return field.reshape(sx // 2, 2, sy // 2, 2, sz // 2, 2).mean(axis=(1, 3, 5))


def prolong(field):
    return jnp.repeat(jnp.repeat(jnp.repeat(field, 2, 0), 2, 1), 2, 2)


def field_pad(field):
    rimmed = extended(field, (("gx", 0), ("gy", 1)), 1)
    return jnp.pad(rimmed, ((0, 0), (0, 0), (1, 1)))


def conduct_pad(cond):
    rimmed = extended(cond, (("gx", 0), ("gy", 1)), 1)
    return jnp.pad(rimmed, ((0, 0), (0, 0), (1, 1)))


def merge_blocks(block):
    for bit in range(lax.axis_size("gx").bit_length() - 1):
        other = partner(block, "gx", bit)
        upper = lax.axis_index("gx") >> bit & 1 == 1
        block = jnp.where(
            upper, jnp.concatenate([other, block], 0), jnp.concatenate([block, other], 0)
        )
    for bit in range(lax.axis_size("gy").bit_length() - 1):
        other = partner(block, "gy", bit)
        upper = lax.axis_index("gy") >> bit & 1 == 1
        block = jnp.where(
            upper, jnp.concatenate([other, block], 1), jnp.concatenate([block, other], 1)
        )
    return block


def coarse_solve(coarse_right, coarse_level):
    cfaces, ctotal = coarse_level
    whole = merge_blocks(coarse_right)
    correction = OMEGA * whole / ctotal
    for sweep in range(COARSE_SWEEPS - 1):
        correction = (
            correction
            + OMEGA * (whole - apply_operator(jnp.pad(correction, 1), cfaces, ctotal)) / ctotal
        )
    bx, by, bz = coarse_right.shape
    start_x = lax.axis_index("gx") * bx
    start_y = lax.axis_index("gy") * by
    return lax.dynamic_slice(correction, (start_x, start_y, jnp.int32(0)), (bx, by, bz))


def cycle(levels, coarse_level, level, field, right, first):
    faces, total = levels[level]
    if first:
        field = OMEGA * right / total
    else:
        field = field + OMEGA * (right - apply_operator(field_pad(field), faces, total)) / total
    resid = right - apply_operator(field_pad(field), faces, total)
    coarse_right = restrict(resid)
    if level == 2:
        correction = coarse_solve(coarse_right, coarse_level)
    else:
        correction = cycle(levels, coarse_level, level + 1, None, coarse_right, True)
    field = field + prolong(correction)
    field = field + OMEGA * (right - apply_operator(field_pad(field), faces, total)) / total
    return field


def local(right_side, material, conductivity):
    cond = jnp.zeros(material.shape, jnp.float32)
    for which in range(conductivity.shape[0]):
        cond = jnp.where(material == which, conductivity[which], cond)
    conds = [cond]
    for level in range(3):
        conds.append(restrict(conds[-1]))
    levels = [face_set(conduct_pad(conds[level]), 0.25**level) for level in range(3)]
    coarse_cond = merge_blocks(restrict(conds[2]))
    coarse_level = face_set(jnp.pad(coarse_cond, 1), 0.25**3)
    field = jnp.zeros_like(right_side)
    for turn in range(CYCLES):
        field = cycle(levels, coarse_level, 0, field, right_side, turn == 0)
    return field


def solution(mesh):
    return jax.shard_map(
        local,
        mesh=mesh,
        in_specs=(P("gx", "gy", None), P("gx", "gy", None), P()),
        out_specs=P("gx", "gy", None),
        check_vma=False,
    )
```

profile of v0, /device:TPU:0, one launch (start us, length us, event | category | flops | bytes accessed | tf_op | source)
XLA Modules:
  0.0 339.7 jit_solution(12958650821471358652)
XLA Ops:
  2.0 11.0 %select_select_fusion = f32[16,16,128]{2,1,0:T(8,128)S(1)} fusion(s32[16,16,128]{2,1,0:T(8,128)} %param.4, f32[]{:T(128)} %bitcast.15, f32[]{:T(128)} %bitcast.14, f32[]{:T(128)} %bitcast.13, f32[]{:T(128)} %bitcast.12, f32[]{:T(128)} %bitcast.11, f32[]{:T(128)} %bitcast.10, f32[]{:T(128)} %bitcast.9, f32[]{:T(128)} %bitcast.8, f32[]{:T(128)} %bitcast.7, ...), kind=kLoop, calls=%fused_computation.229 | loop fusion | flops 1048576 | bytes 262208 | tf_op jit(solution)/shard_map/jit(_where)/select_n | solution.py:131
  16.7 9.8 %reshape.84 = f32[8,2,8,2,64,2]{5,4,3,2,1,0:T(8,128)} reshape(f32[16,16,128]{2,1,0:T(8,128)S(1)} %select_select_fusion) | data formatting | bytes 262144 | tf_op jit(solution)/shard_map/reshape | solution.py:63
  26.5 4.0 %reduce_sum.82 = f32[8,8,64]{2,1,0:T(8,128)S(1)} reduce(f32[8,2,8,2,64,2]{5,4,3,2,1,0:T(8,128)} %reshape.84, f32[]{:T(128)} %constant.24.clone.1), dimensions={1,3,5}, to_apply=%region_1.2 | reduce | flops 28672 | bytes 147460 | tf_op jit(solution)/shard_map/reduce_sum | solution.py:63
  30.6 5.1 %collective-permute-start.9 = (f32[1,8,64]{2,1,0:T(8,128)S(1)}, f32[1,8,64]{2,1,0:T(8,128)S(1)}, u32[]{:S(2)}, u32[]{:S(2)}) collective-permute-start(f32[1,8,64]{2,1,0:T(8,128)S(1)} %get-tuple-element.78), channel_id=1, source_target_pairs={{0,4},{4,8},{8,12},{12,16},{16,20},{20,24},{24,28},{1,5},{5,9},{9,... | collective-permute-start | bytes 6152 | tf_op jit(solution)/shard_map/ppermute | solution.py:20
  44.7 4.6 %collective-permute-start.17 = (f32[1,4,32]{2,1,0:T(4,128)S(1)}, f32[1,4,32]{2,1,0:T(4,128)S(1)}, u32[]{:S(2)}, u32[]{:S(2)}) collective-permute-start(f32[1,4,32]{2,1,0:T(4,128)S(1)} %get-tuple-element.99), channel_id=1, source_target_pairs={{0,4},{4,8},{8,12},{12,16},{16,20},{20,24},{24,28},{1,5},{5,9},{9,... | collective-permute-start | bytes 1544 | tf_op jit(solution)/shard_map/ppermute | solution.py:20
  55.1 4.5 %collective-permute-start.11 = (f32[10,1,64]{2,1,0:T(1,128)S(1)}, f32[10,1,64]{2,1,0:T(1,128)S(1)}, u32[]{:S(2)}, u32[]{:S(2)}) collective-permute-start(f32[10,1,64]{2,1,0:T(1,128)S(1)} %get-tuple-element.68), channel_id=1, source_target_pairs={{0,1},{1,2},{2,3},{4,5},{5,6},{6,7},{8,9},{9,10},{10,11},{12,13},{... | collective-permute-start | bytes 7688 | tf_op jit(solution)/shard_map/ppermute | solution.py:20
  61.1 5.2 %collective-permute-start.7 = (f32[18,1,128]{2,1,0:T(1,128)S(1)}, f32[18,1,128]{2,1,0:T(1,128)S(1)}, u32[]{:S(2)}, u32[]{:S(2)}) collective-permute-start(f32[18,1,128]{2,1,0:T(1,128)S(1)} %get-tuple-element.38), channel_id=1, source_target_pairs={{0,1},{1,2},{2,3},{4,5},{5,6},{6,7},{8,9},{9,10},{10,11},{12,13},{... | collective-permute-start | bytes 27656 | tf_op jit(solution)/shard_map/ppermute | solution.py:20
  67.7 4.1 %collective-permute-done.6 = f32[18,1,128]{2,1,0:T(1,128)S(1)} collective-permute-done((f32[18,1,128]{2,1,0:T(1,128)S(1)}, f32[18,1,128]{2,1,0:T(1,128)S(1)}, u32[]{:S(2)}, u32[]{:S(2)}) %collective-permute-start.6) | collective-permute-done | bytes 9248 | tf_op jit(solution)/shard_map/ppermute | solution.py:21
  72.3 9.8 %reshape.83 = f32[8,2,8,2,64,2]{5,4,3,2,1,0:T(8,128)} reshape(f32[16,16,128]{2,1,0:T(8,128)S(1)} %fusion.55) | data formatting | bytes 262144 | tf_op jit(solution)/shard_map/reshape | solution.py:63
  82.1 4.0 %reduce_sum.81 = f32[8,8,64]{2,1,0:T(8,128)S(1)} reduce(f32[8,2,8,2,64,2]{5,4,3,2,1,0:T(8,128)} %reshape.83, f32[]{:T(128)} %constant.24.clone.1), dimensions={1,3,5}, to_apply=%region_0.1 | reduce | flops 28672 | bytes 147460 | tf_op jit(solution)/shard_map/reduce_sum | solution.py:63
  90.8 3.5 %collective-permute-start.19 = (f32[6,1,32]{2,1,0:T(1,128)S(1)}, f32[6,1,32]{2,1,0:T(1,128)S(1)}, u32[]{:S(2)}, u32[]{:S(2)}) collective-permute-start(f32[6,1,32]{2,1,0:T(1,128)S(1)} %get-tuple-element.88), channel_id=1, source_target_pairs={{0,1},{1,2},{2,3},{4,5},{5,6},{6,7},{8,9},{9,10},{10,11},{12,13},{... | collective-permute-start | bytes 2312 | tf_op jit(solution)/shard_map/ppermute | solution.py:20
  95.8 4.4 %collective-permute-start.15 = (f32[10,1,64]{2,1,0:T(1,128)S(1)}, f32[10,1,64]{2,1,0:T(1,128)S(1)}, u32[]{:S(2)}, u32[]{:S(2)}) collective-permute-start(f32[10,1,64]{2,1,0:T(1,128)S(1)} %get-tuple-element.66), channel_id=1, source_target_pairs={{0,1},{1,2},{2,3},{4,5},{5,6},{6,7},{8,9},{9,10},{10,11},{12,13},{... | collective-permute-start | bytes 7688 | tf_op jit(solution)/shard_map/ppermute | solution.py:20
  101.6 4.1 %collective-permute-done.14 = f32[10,1,64]{2,1,0:T(1,128)S(1)} collective-permute-done((f32[10,1,64]{2,1,0:T(1,128)S(1)}, f32[10,1,64]{2,1,0:T(1,128)S(1)}, u32[]{:S(2)}, u32[]{:S(2)}) %collective-permute-start.14) | collective-permute-done | bytes 2592 | tf_op jit(solution)/shard_map/ppermute | solution.py:21
  107.3 4.3 %collective-permute-start.21 = (f32[1,4,32]{2,1,0:T(4,128)S(1)}, f32[1,4,32]{2,1,0:T(4,128)S(1)}, u32[]{:S(2)}, u32[]{:S(2)}) collective-permute-start(f32[1,4,32]{2,1,0:T(4,128)S(1)} %get-tuple-element.96), channel_id=1, source_target_pairs={{0,4},{4,8},{8,12},{12,16},{16,20},{20,24},{24,28},{1,5},{5,9},{9,... | collective-permute-start | bytes 1544 | tf_op jit(solution)/shard_map/ppermute | solution.py:20
  112.9 5.0 %collective-permute-done.20 = f32[1,4,32]{2,1,0:T(4,128)S(1)} collective-permute-done((f32[1,4,32]{2,1,0:T(4,128)S(1)}, f32[1,4,32]{2,1,0:T(4,128)S(1)}, u32[]{:S(2)}, u32[]{:S(2)}) %collective-permute-start.20) | collective-permute-done | bytes 544 | tf_op jit(solution)/shard_map/ppermute | solution.py:21
  122.7 4.2 %collective-permute-done.22 = f32[6,1,32]{2,1,0:T(1,128)S(1)} collective-permute-done((f32[6,1,32]{2,1,0:T(1,128)S(1)}, f32[6,1,32]{2,1,0:T(1,128)S(1)}, u32[]{:S(2)}, u32[]{:S(2)}) %collective-permute-start.22) | collective-permute-done | bytes 800 | tf_op jit(solution)/shard_map/ppermute | solution.py:21
  158.0 4.2 %collective-permute-done.36 = f32[6,1,32]{2,1,0:T(1,128)S(1)} collective-permute-done((f32[6,1,32]{2,1,0:T(1,128)S(1)}, f32[6,1,32]{2,1,0:T(1,128)S(1)}, u32[]{:S(2)}, u32[]{:S(2)}) %collective-permute-start.36) | collective-permute-done | bytes 800 | tf_op jit(solution)/shard_map/ppermute | solution.py:21
  174.4 4.0 %collective-permute-done.40 = f32[10,1,64]{2,1,0:T(1,128)S(1)} collective-permute-done((f32[10,1,64]{2,1,0:T(1,128)S(1)}, f32[10,1,64]{2,1,0:T(1,128)S(1)}, u32[]{:S(2)}, u32[]{:S(2)}) %collective-permute-start.40) | collective-permute-done | bytes 2592 | tf_op jit(solution)/shard_map/ppermute | solution.py:21
  190.0 4.2 %collective-permute-done.44 = f32[18,1,128]{2,1,0:T(1,128)S(1)} collective-permute-done((f32[18,1,128]{2,1,0:T(1,128)S(1)}, f32[18,1,128]{2,1,0:T(1,128)S(1)}, u32[]{:S(2)}, u32[]{:S(2)}) %collective-permute-start.44) | collective-permute-done | bytes 9248 | tf_op jit(solution)/shard_map/ppermute | solution.py:21
  205.5 4.2 %collective-permute-done.48 = f32[18,1,128]{2,1,0:T(1,128)S(1)} collective-permute-done((f32[18,1,128]{2,1,0:T(1,128)S(1)}, f32[18,1,128]{2,1,0:T(1,128)S(1)}, u32[]{:S(2)}, u32[]{:S(2)}) %collective-permute-start.48) | collective-permute-done | bytes 9248 | tf_op jit(solution)/shard_map/ppermute | solution.py:21
  221.3 4.2 %collective-permute-done.52 = f32[18,1,128]{2,1,0:T(1,128)S(1)} collective-permute-done((f32[18,1,128]{2,1,0:T(1,128)S(1)}, f32[18,1,128]{2,1,0:T(1,128)S(1)}, u32[]{:S(2)}, u32[]{:S(2)}) %collective-permute-start.52) | collective-permute-done | bytes 9248 | tf_op jit(solution)/shard_map/ppermute | solution.py:21
  226.0 9.8 %reshape.96 = f32[8,2,8,2,64,2]{5,4,3,2,1,0:T(8,128)} reshape(f32[16,16,128]{2,1,0:T(8,128)S(1)} %fusion.16) | data formatting | bytes 262144 | tf_op jit(solution)/shard_map/reshape | solution.py:63
  235.8 4.0 %reduce_sum.87 = f32[8,8,64]{2,1,0:T(8,128)S(1)} reduce(f32[8,2,8,2,64,2]{5,4,3,2,1,0:T(8,128)} %reshape.96, f32[]{:T(128)} %constant.24.clone.1), dimensions={1,3,5}, to_apply=%region_6.7 | reduce | flops 28672 | bytes 147460 | tf_op jit(solution)/shard_map/reduce_sum | solution.py:63
  250.9 4.2 %collective-permute-done.56 = f32[10,1,64]{2,1,0:T(1,128)S(1)} collective-permute-done((f32[10,1,64]{2,1,0:T(1,128)S(1)}, f32[10,1,64]{2,1,0:T(1,128)S(1)}, u32[]{:S(2)}, u32[]{:S(2)}) %collective-permute-start.56) | collective-permute-done | bytes 2592 | tf_op jit(solution)/shard_map/ppermute | solution.py:21
  267.7 4.2 %collective-permute-done.60 = f32[6,1,32]{2,1,0:T(1,128)S(1)} collective-permute-done((f32[6,1,32]{2,1,0:T(1,128)S(1)}, f32[6,1,32]{2,1,0:T(1,128)S(1)}, u32[]{:S(2)}, u32[]{:S(2)}) %collective-permute-start.60) | collective-permute-done | bytes 800 | tf_op jit(solution)/shard_map/ppermute | solution.py:21
  274.4 3.7 %collective-permute-start.63 = (f32[4,2,16]{2,1,0:T(2,128)S(1)}, f32[4,2,16]{2,1,0:T(2,128)S(1)}, u32[]{:S(2)}, u32[]{:S(2)}) collective-permute-start(f32[4,2,16]{2,1,0:T(2,128)S(1)} %maximum_select_fusion.14), channel_id=1, source_target_pairs={{0,8},{8,0},{4,12},{12,4},{16,24},{24,16},{20,28},{28,20},{1,9},{9... | collective-permute-start | bytes 1544 | tf_op jit(solution)/shard_map/ppermute | solution.py:33
  283.8 3.7 %collective-permute-done.65 = f32[16,2,16]{2,1,0:T(2,128)S(1)} collective-permute-done((f32[16,2,16]{2,1,0:T(2,128)S(1)}, f32[16,2,16]{2,1,0:T(2,128)S(1)}, u32[]{:S(2)}, u32[]{:S(2)}) %collective-permute-start.65) | collective-permute-done | bytes 2080 | tf_op jit(solution)/shard_map/ppermute | solution.py:33
  287.6 4.8 %collective-permute-done.66 = f32[16,4,16]{2,1,0:T(4,128)S(1)} collective-permute-done((f32[16,4,16]{2,1,0:T(4,128)S(1)}, f32[16,4,16]{2,1,0:T(4,128)S(1)}, u32[]{:S(2)}, u32[]{:S(2)}) %collective-permute-start.66) | collective-permute-done | bytes 4128 | tf_op jit(solution)/shard_map/ppermute | solution.py:33
  296.0 4.0 %collective-permute-done.67 = f32[1,4,32]{2,1,0:T(4,128)S(1)} collective-permute-done((f32[1,4,32]{2,1,0:T(4,128)S(1)}, f32[1,4,32]{2,1,0:T(4,128)S(1)}, u32[]{:S(2)}, u32[]{:S(2)}) %collective-permute-start.67) | collective-permute-done | bytes 544 | tf_op jit(solution)/shard_map/ppermute | solution.py:21
  303.4 4.2 %collective-permute-done.69 = f32[6,1,32]{2,1,0:T(1,128)S(1)} collective-permute-done((f32[6,1,32]{2,1,0:T(1,128)S(1)}, f32[6,1,32]{2,1,0:T(1,128)S(1)}, u32[]{:S(2)}, u32[]{:S(2)}) %collective-permute-start.69) | collective-permute-done | bytes 800 | tf_op jit(solution)/shard_map/ppermute | solution.py:21
  318.3 4.2 %collective-permute-done.73 = f32[10,1,64]{2,1,0:T(1,128)S(1)} collective-permute-done((f32[10,1,64]{2,1,0:T(1,128)S(1)}, f32[10,1,64]{2,1,0:T(1,128)S(1)}, u32[]{:S(2)}, u32[]{:S(2)}) %collective-permute-start.73) | collective-permute-done | bytes 2592 | tf_op jit(solution)/shard_map/ppermute | solution.py:21
  334.3 4.2 %collective-permute-done.77 = f32[18,1,128]{2,1,0:T(1,128)S(1)} collective-permute-done((f32[18,1,128]{2,1,0:T(1,128)S(1)}, f32[18,1,128]{2,1,0:T(1,128)S(1)}, u32[]{:S(2)}, u32[]{:S(2)}) %collective-permute-start.77) | collective-permute-done | bytes 9248 | tf_op jit(solution)/shard_map/ppermute | solution.py:21
  (286 shorter events, 178.9 us)
Async XLA Ops:
  12.9 26.9 %collective-permute-start.1 = (f32[1,16,128]{2,1,0:T(8,128)S(1)}, f32[1,16,128]{2,1,0:T(8,128)S(1)}, u32[]{:S(2)}, u32[]{:S(2)}) collective-permute-start(f32[1,16,128]{2,1,0:T(8,128)S(1)} %get-tuple-element.52), channel_id=1, source_target_pairs={{0,4},{4,8},{8,12},{12,16},{16,20},{20,24},{24,28},{1,5},{5,9},{9,... | collective-permute-start | bytes 24584 | tf_op jit(solution)/shard_map/ppermute | solution.py:20
  15.3 24.5 %collective-permute-start = (f32[1,16,128]{2,1,0:T(8,128)S(1)}, f32[1,16,128]{2,1,0:T(8,128)S(1)}, u32[]{:S(2)}, u32[]{:S(2)}) collective-permute-start(f32[1,16,128]{2,1,0:T(8,128)S(1)} %get-tuple-element.53), channel_id=1, source_target_pairs={{4,0},{8,4},{12,8},{16,12},{20,16},{24,20},{28,24},{5,1},{9,5},{13... | collective-permute-start | bytes 24584 | tf_op jit(solution)/shard_map/ppermute | solution.py:21
  30.6 21.3 %collective-permute-start.9 = (f32[1,8,64]{2,1,0:T(8,128)S(1)}, f32[1,8,64]{2,1,0:T(8,128)S(1)}, u32[]{:S(2)}, u32[]{:S(2)}) collective-permute-start(f32[1,8,64]{2,1,0:T(8,128)S(1)} %get-tuple-element.78), channel_id=1, source_target_pairs={{0,4},{4,8},{8,12},{12,16},{16,20},{20,24},{24,28},{1,5},{5,9},{9,... | collective-permute-start | bytes 6152 | tf_op jit(solution)/shard_map/ppermute | solution.py:20
  35.7 18.1 %collective-permute-start.8 = (f32[1,8,64]{2,1,0:T(8,128)S(1)}, f32[1,8,64]{2,1,0:T(8,128)S(1)}, u32[]{:S(2)}, u32[]{:S(2)}) collective-permute-start(f32[1,8,64]{2,1,0:T(8,128)S(1)} %get-tuple-element.79), channel_id=1, source_target_pairs={{4,0},{8,4},{12,8},{16,12},{20,16},{24,20},{28,24},{5,1},{9,5},{13... | collective-permute-start | bytes 6152 | tf_op jit(solution)/shard_map/ppermute | solution.py:21
  38.3 52.5 %collective-permute-start.16 = (f32[1,4,32]{2,1,0:T(4,128)S(1)}, f32[1,4,32]{2,1,0:T(4,128)S(1)}, u32[]{:S(2)}, u32[]{:S(2)}) collective-permute-start(f32[1,4,32]{2,1,0:T(4,128)S(1)} %get-tuple-element.98), channel_id=1, source_target_pairs={{4,0},{8,4},{12,8},{16,12},{20,16},{24,20},{28,24},{5,1},{9,5},{13... | collective-permute-start | bytes 1544 | tf_op jit(solution)/shard_map/ppermute | solution.py:21
  43.3 6.0 %collective-permute-start.2 = (f32[18,1,128]{2,1,0:T(1,128)S(1)}, f32[18,1,128]{2,1,0:T(1,128)S(1)}, u32[]{:S(2)}, u32[]{:S(2)}) collective-permute-start(f32[18,1,128]{2,1,0:T(1,128)S(1)} %get-tuple-element.41), channel_id=1, source_target_pairs={{1,0},{2,1},{3,2},{5,4},{6,5},{7,6},{9,8},{10,9},{11,10},{13,12},{... | collective-permute-start | bytes 27656 | tf_op jit(solution)/shard_map/ppermute | solution.py:21
  44.7 46.1 %collective-permute-start.17 = (f32[1,4,32]{2,1,0:T(4,128)S(1)}, f32[1,4,32]{2,1,0:T(4,128)S(1)}, u32[]{:S(2)}, u32[]{:S(2)}) collective-permute-start(f32[1,4,32]{2,1,0:T(4,128)S(1)} %get-tuple-element.99), channel_id=1, source_target_pairs={{0,4},{4,8},{8,12},{12,16},{16,20},{20,24},{24,28},{1,5},{5,9},{9,... | collective-permute-start | bytes 1544 | tf_op jit(solution)/shard_map/ppermute | solution.py:20
  49.3 78.9 %collective-permute-start.29 = (f32[2,2,16]{2,1,0:T(2,128)S(1)}, f32[2,2,16]{2,1,0:T(2,128)S(1)}, u32[]{:S(2)}, u32[]{:S(2)}) collective-permute-start(f32[2,2,16]{2,1,0:T(2,128)S(1)} %broadcast_multiply_fusion.3), channel_id=1, source_target_pairs={{0,4},{4,0},{8,12},{12,8},{16,20},{20,16},{24,28},{28,24},{1,5},{5... | collective-permute-start | bytes 776 | tf_op jit(solution)/shard_map/ppermute | solution.py:33
  53.8 6.0 %collective-permute-start.4 = (f32[1,16,128]{2,1,0:T(8,128)S(1)}, f32[1,16,128]{2,1,0:T(8,128)S(1)}, u32[]{:S(2)}, u32[]{:S(2)}) collective-permute-start(f32[1,16,128]{2,1,0:T(8,128)S(1)} %get-tuple-element.51), channel_id=1, source_target_pairs={{4,0},{8,4},{12,8},{16,12},{20,16},{24,20},{28,24},{5,1},{9,5},{13... | collective-permute-start | bytes 24584 | tf_op jit(solution)/shard_map/ppermute | solution.py:21
  55.1 5.9 %collective-permute-start.11 = (f32[10,1,64]{2,1,0:T(1,128)S(1)}, f32[10,1,64]{2,1,0:T(1,128)S(1)}, u32[]{:S(2)}, u32[]{:S(2)}) collective-permute-start(f32[10,1,64]{2,1,0:T(1,128)S(1)} %get-tuple-element.68), channel_id=1, source_target_pairs={{0,1},{1,2},{2,3},{4,5},{5,6},{6,7},{8,9},{9,10},{10,11},{12,13},{... | collective-permute-start | bytes 7688 | tf_op jit(solution)/shard_map/ppermute | solution.py:20
  59.8 6.5 %collective-permute-start.10 = (f32[10,1,64]{2,1,0:T(1,128)S(1)}, f32[10,1,64]{2,1,0:T(1,128)S(1)}, u32[]{:S(2)}, u32[]{:S(2)}) collective-permute-start(f32[10,1,64]{2,1,0:T(1,128)S(1)} %get-tuple-element.69), channel_id=1, source_target_pairs={{1,0},{2,1},{3,2},{5,4},{6,5},{7,6},{9,8},{10,9},{11,10},{13,12},{... | collective-permute-start | bytes 7688 | tf_op jit(solution)/shard_map/ppermute | solution.py:21
  61.1 6.6 %collective-permute-start.7 = (f32[18,1,128]{2,1,0:T(1,128)S(1)}, f32[18,1,128]{2,1,0:T(1,128)S(1)}, u32[]{:S(2)}, u32[]{:S(2)}) collective-permute-start(f32[18,1,128]{2,1,0:T(1,128)S(1)} %get-tuple-element.38), channel_id=1, source_target_pairs={{0,1},{1,2},{2,3},{4,5},{5,6},{6,7},{8,9},{9,10},{10,11},{12,13},{... | collective-permute-start | bytes 27656 | tf_op jit(solution)/shard_map/ppermute | solution.py:20
  66.2 5.6 %collective-permute-start.6 = (f32[18,1,128]{2,1,0:T(1,128)S(1)}, f32[18,1,128]{2,1,0:T(1,128)S(1)}, u32[]{:S(2)}, u32[]{:S(2)}) collective-permute-start(f32[18,1,128]{2,1,0:T(1,128)S(1)} %get-tuple-element.39), channel_id=1, source_target_pairs={{1,0},{2,1},{3,2},{5,4},{6,5},{7,6},{9,8},{10,9},{11,10},{13,12},{... | collective-permute-start | bytes 27656 | tf_op jit(solution)/shard_map/ppermute | solution.py:21
  86.2 9.4 %collective-permute-start.13 = (f32[1,8,64]{2,1,0:T(8,128)S(1)}, f32[1,8,64]{2,1,0:T(8,128)S(1)}, u32[]{:S(2)}, u32[]{:S(2)}) collective-permute-start(f32[1,8,64]{2,1,0:T(8,128)S(1)} %get-tuple-element.76), channel_id=1, source_target_pairs={{0,4},{4,8},{8,12},{12,16},{16,20},{20,24},{24,28},{1,5},{5,9},{9,... | collective-permute-start | bytes 6152 | tf_op jit(solution)/shard_map/ppermute | solution.py:20
  89.5 6.3 %collective-permute-start.12 = (f32[1,8,64]{2,1,0:T(8,128)S(1)}, f32[1,8,64]{2,1,0:T(8,128)S(1)}, u32[]{:S(2)}, u32[]{:S(2)}) collective-permute-start(f32[1,8,64]{2,1,0:T(8,128)S(1)} %get-tuple-element.77), channel_id=1, source_target_pairs={{4,0},{8,4},{12,8},{16,12},{20,16},{24,20},{28,24},{5,1},{9,5},{13... | collective-permute-start | bytes 6152 | tf_op jit(solution)/shard_map/ppermute | solution.py:21
  90.8 10.7 %collective-permute-start.19 = (f32[6,1,32]{2,1,0:T(1,128)S(1)}, f32[6,1,32]{2,1,0:T(1,128)S(1)}, u32[]{:S(2)}, u32[]{:S(2)}) collective-permute-start(f32[6,1,32]{2,1,0:T(1,128)S(1)} %get-tuple-element.88), channel_id=1, source_target_pairs={{0,1},{1,2},{2,3},{4,5},{5,6},{6,7},{8,9},{9,10},{10,11},{12,13},{... | collective-permute-start | bytes 2312 | tf_op jit(solution)/shard_map/ppermute | solution.py:20
  94.3 7.2 %collective-permute-start.18 = (f32[6,1,32]{2,1,0:T(1,128)S(1)}, f32[6,1,32]{2,1,0:T(1,128)S(1)}, u32[]{:S(2)}, u32[]{:S(2)}) collective-permute-start(f32[6,1,32]{2,1,0:T(1,128)S(1)} %get-tuple-element.89), channel_id=1, source_target_pairs={{1,0},{2,1},{3,2},{5,4},{6,5},{7,6},{9,8},{10,9},{11,10},{13,12},{... | collective-permute-start | bytes 2312 | tf_op jit(solution)/shard_map/ppermute | solution.py:21
  95.8 5.8 %collective-permute-start.15 = (f32[10,1,64]{2,1,0:T(1,128)S(1)}, f32[10,1,64]{2,1,0:T(1,128)S(1)}, u32[]{:S(2)}, u32[]{:S(2)}) collective-permute-start(f32[10,1,64]{2,1,0:T(1,128)S(1)} %get-tuple-element.66), channel_id=1, source_target_pairs={{0,1},{1,2},{2,3},{4,5},{5,6},{6,7},{8,9},{9,10},{10,11},{12,13},{... | collective-permute-start | bytes 7688 | tf_op jit(solution)/shard_map/ppermute | solution.py:20
  100.2 5.5 %collective-permute-start.14 = (f32[10,1,64]{2,1,0:T(1,128)S(1)}, f32[10,1,64]{2,1,0:T(1,128)S(1)}, u32[]{:S(2)}, u32[]{:S(2)}) collective-permute-start(f32[10,1,64]{2,1,0:T(1,128)S(1)} %get-tuple-element.67), channel_id=1, source_target_pairs={{1,0},{2,1},{3,2},{5,4},{6,5},{7,6},{9,8},{10,9},{11,10},{13,12},{... | collective-permute-start | bytes 7688 | tf_op jit(solution)/shard_map/ppermute | solution.py:21
  107.3 5.6 %collective-permute-start.21 = (f32[1,4,32]{2,1,0:T(4,128)S(1)}, f32[1,4,32]{2,1,0:T(4,128)S(1)}, u32[]{:S(2)}, u32[]{:S(2)}) collective-permute-start(f32[1,4,32]{2,1,0:T(4,128)S(1)} %get-tuple-element.96), channel_id=1, source_target_pairs={{0,4},{4,8},{8,12},{12,16},{16,20},{20,24},{24,28},{1,5},{5,9},{9,... | collective-permute-start | bytes 1544 | tf_op jit(solution)/shard_map/ppermute | solution.py:20
  111.5 6.3 %collective-permute-start.20 = (f32[1,4,32]{2,1,0:T(4,128)S(1)}, f32[1,4,32]{2,1,0:T(4,128)S(1)}, u32[]{:S(2)}, u32[]{:S(2)}) collective-permute-start(f32[1,4,32]{2,1,0:T(4,128)S(1)} %get-tuple-element.97), channel_id=1, source_target_pairs={{4,0},{8,4},{12,8},{16,12},{20,16},{24,20},{28,24},{5,1},{9,5},{13... | collective-permute-start | bytes 1544 | tf_op jit(solution)/shard_map/ppermute | solution.py:21
  121.3 5.5 %collective-permute-start.22 = (f32[6,1,32]{2,1,0:T(1,128)S(1)}, f32[6,1,32]{2,1,0:T(1,128)S(1)}, u32[]{:S(2)}, u32[]{:S(2)}) collective-permute-start(f32[6,1,32]{2,1,0:T(1,128)S(1)} %get-tuple-element.87), channel_id=1, source_target_pairs={{1,0},{2,1},{3,2},{5,4},{6,5},{7,6},{9,8},{10,9},{11,10},{13,12},{... | collective-permute-start | bytes 2312 | tf_op jit(solution)/shard_map/ppermute | solution.py:21
  156.7 5.5 %collective-permute-start.36 = (f32[6,1,32]{2,1,0:T(1,128)S(1)}, f32[6,1,32]{2,1,0:T(1,128)S(1)}, u32[]{:S(2)}, u32[]{:S(2)}) collective-permute-start(f32[6,1,32]{2,1,0:T(1,128)S(1)} %get-tuple-element.85), channel_id=1, source_target_pairs={{1,0},{2,1},{3,2},{5,4},{6,5},{7,6},{9,8},{10,9},{11,10},{13,12},{... | collective-permute-start | bytes 2312 | tf_op jit(solution)/shard_map/ppermute | solution.py:21
  172.9 5.5 %collective-permute-start.40 = (f32[10,1,64]{2,1,0:T(1,128)S(1)}, f32[10,1,64]{2,1,0:T(1,128)S(1)}, u32[]{:S(2)}, u32[]{:S(2)}) collective-permute-start(f32[10,1,64]{2,1,0:T(1,128)S(1)} %get-tuple-element.65), channel_id=1, source_target_pairs={{1,0},{2,1},{3,2},{5,4},{6,5},{7,6},{9,8},{10,9},{11,10},{13,12},{... | collective-permute-start | bytes 7688 | tf_op jit(solution)/shard_map/ppermute | solution.py:21
  188.6 5.6 %collective-permute-start.44 = (f32[18,1,128]{2,1,0:T(1,128)S(1)}, f32[18,1,128]{2,1,0:T(1,128)S(1)}, u32[]{:S(2)}, u32[]{:S(2)}) collective-permute-start(f32[18,1,128]{2,1,0:T(1,128)S(1)} %get-tuple-element.37), channel_id=1, source_target_pairs={{1,0},{2,1},{3,2},{5,4},{6,5},{7,6},{9,8},{10,9},{11,10},{13,12},{... | collective-permute-start | bytes 27656 | tf_op jit(solution)/shard_map/ppermute | solution.py:21
  204.1 5.6 %collective-permute-start.48 = (f32[18,1,128]{2,1,0:T(1,128)S(1)}, f32[18,1,128]{2,1,0:T(1,128)S(1)}, u32[]{:S(2)}, u32[]{:S(2)}) collective-permute-start(f32[18,1,128]{2,1,0:T(1,128)S(1)} %get-tuple-element.35), channel_id=1, source_target_pairs={{1,0},{2,1},{3,2},{5,4},{6,5},{7,6},{9,8},{10,9},{11,10},{13,12},{... | collective-permute-start | bytes 27656 | tf_op jit(solution)/shard_map/ppermute | solution.py:21
  220.0 5.6 %collective-permute-start.52 = (f32[18,1,128]{2,1,0:T(1,128)S(1)}, f32[18,1,128]{2,1,0:T(1,128)S(1)}, u32[]{:S(2)}, u32[]{:S(2)}) collective-permute-start(f32[18,1,128]{2,1,0:T(1,128)S(1)} %get-tuple-element.33), channel_id=1, source_target_pairs={{1,0},{2,1},{3,2},{5,4},{6,5},{7,6},{9,8},{10,9},{11,10},{13,12},{... | collective-permute-start | bytes 27656 | tf_op jit(solution)/shard_map/ppermute | solution.py:21
  249.6 5.5 %collective-permute-start.56 = (f32[10,1,64]{2,1,0:T(1,128)S(1)}, f32[10,1,64]{2,1,0:T(1,128)S(1)}, u32[]{:S(2)}, u32[]{:S(2)}) collective-permute-start(f32[10,1,64]{2,1,0:T(1,128)S(1)} %get-tuple-element.63), channel_id=1, source_target_pairs={{1,0},{2,1},{3,2},{5,4},{6,5},{7,6},{9,8},{10,9},{11,10},{13,12},{... | collective-permute-start | bytes 7688 | tf_op jit(solution)/shard_map/ppermute | solution.py:21
  266.4 5.5 %collective-permute-start.60 = (f32[6,1,32]{2,1,0:T(1,128)S(1)}, f32[6,1,32]{2,1,0:T(1,128)S(1)}, u32[]{:S(2)}, u32[]{:S(2)}) collective-permute-start(f32[6,1,32]{2,1,0:T(1,128)S(1)} %get-tuple-element.83), channel_id=1, source_target_pairs={{1,0},{2,1},{3,2},{5,4},{6,5},{7,6},{9,8},{10,9},{11,10},{13,12},{... | collective-permute-start | bytes 2312 | tf_op jit(solution)/shard_map/ppermute | solution.py:21
  302.1 5.5 %collective-permute-start.69 = (f32[6,1,32]{2,1,0:T(1,128)S(1)}, f32[6,1,32]{2,1,0:T(1,128)S(1)}, u32[]{:S(2)}, u32[]{:S(2)}) collective-permute-start(f32[6,1,32]{2,1,0:T(1,128)S(1)} %get-tuple-element.81), channel_id=1, source_target_pairs={{1,0},{2,1},{3,2},{5,4},{6,5},{7,6},{9,8},{10,9},{11,10},{13,12},{... | collective-permute-start | bytes 2312 | tf_op jit(solution)/shard_map/ppermute | solution.py:21
  317.0 5.5 %collective-permute-start.73 = (f32[10,1,64]{2,1,0:T(1,128)S(1)}, f32[10,1,64]{2,1,0:T(1,128)S(1)}, u32[]{:S(2)}, u32[]{:S(2)}) collective-permute-start(f32[10,1,64]{2,1,0:T(1,128)S(1)} %get-tuple-element.61), channel_id=1, source_target_pairs={{1,0},{2,1},{3,2},{5,4},{6,5},{7,6},{9,8},{10,9},{11,10},{13,12},{... | collective-permute-start | bytes 7688 | tf_op jit(solution)/shard_map/ppermute | solution.py:21
  333.0 5.6 %collective-permute-start.77 = (f32[18,1,128]{2,1,0:T(1,128)S(1)}, f32[18,1,128]{2,1,0:T(1,128)S(1)}, u32[]{:S(2)}, u32[]{:S(2)}) collective-permute-start(f32[18,1,128]{2,1,0:T(1,128)S(1)} %get-tuple-element.31), channel_id=1, source_target_pairs={{1,0},{2,1},{3,2},{5,4},{6,5},{7,6},{9,8},{10,9},{11,10},{13,12},{... | collective-permute-start | bytes 27656 | tf_op jit(solution)/shard_map/ppermute | solution.py:21
  (48 other events, 226.0 us)
where the time goes:
time: 344 us; the launch traced here: 340 us
  starting transfers between devices  156 us (45%)
  waiting for transfers between devices  113 us (33%)
  local copies, waits for them, and re-layouts  37.6 us (11%)
  other arithmetic  31 us (9%)
    ppermute x32, starting transfers between devices, extended(): before = lax.ppermute(last, axis, up)  95.5 us
    ppermute x32, waiting for transfers between devices, extended(): after = lax.ppermute(first, axis, down)  90.1 us
    ppermute x32, starting transfers between devices, extended(): after = lax.ppermute(first, axis, down)  41.6 us
    reshape x7, local copies, waits for them, and re-layouts, restrict(): field.reshape(sx // 2, 2, sy // 2, 2, sz // 2, 2).mean(axis=(1, 3, 5))  31.8 us
    ppermute x15, waiting for transfers between devices, partner(): return lax.ppermute(block, axis, route)  23 us
    ppermute x15, starting transfers between devices, partner(): return lax.ppermute(block, axis, route)  18.9 us
    reduce_sum x9, other arithmetic, restrict(): field.reshape(sx // 2, 2, sy // 2, 2, sz // 2, 2).mean(axis=(1, 3, 5))  12.8 us
    select_n x1, other arithmetic, local(): cond = jnp.where(material == which, conductivity[which], cond)  11 us
  transfers between devices with their start and end apart: 79, of which 43 were waited for; matrix products, arithmetic and copies ran while one was open for 10% of the time, Pallas kernels for 0%

commit v1 on v0

v1 whole, which is shorter than its diff:
```python
import functools

import jax
import jax.numpy as jnp
from jax import lax
from jax.experimental import pallas as pl
from jax.experimental.pallas import tpu as pltpu
from jax.sharding import PartitionSpec as P

COARSE_SWEEPS = 6
OMEGA = 0.8
KEEP = 1.0 - OMEGA
HALO = 12
SLAB = 4
TRIM = 8
F32 = jnp.float32


def pair_exchange(to_low, to_high, axis):
    count = lax.axis_size(axis)
    odd = lax.axis_index(axis) % 2 == 1
    near = [(i, i ^ 1) for i in range(count) if i ^ 1 < count]
    far = [(i, i + 1) for i in range(1, count - 1, 2)]
    far = far + [(j, i) for i, j in far]
    from_near = lax.ppermute(jnp.where(odd, to_low, to_high), axis, near)
    from_far = lax.ppermute(jnp.where(odd, to_high, to_low), axis, far)
    return jnp.where(odd, from_near, from_far), jnp.where(odd, from_far, from_near)


def everywhere(copies):
    return lax.all_to_all(copies, ("gx", "gy"), 0, 0)


def roll(value, shift, axis):
    return pltpu.roll(value, shift % value.shape[axis], axis=axis)


def lanes_of(value):
    return lax.broadcasted_iota(jnp.int32, value.shape, value.ndim - 1)


def rows_of(value):
    return lax.broadcasted_iota(jnp.int32, value.shape, value.ndim - 2)


def pick_lanes(value, index):
    flat = value.reshape(-1, value.shape[-1])
    index = jnp.broadcast_to(index, flat.shape)
    return jnp.take_along_axis(flat, index, axis=1).reshape(value.shape)


def lane_row(width):
    return lax.broadcasted_iota(jnp.int32, (1, width), 1)


def add_partner(value, apart):
    return value + pick_lanes(value, lane_row(value.shape[-1]) ^ apart)


def local_faces(h, h_next, h_prev, step):
    width = h.shape[-1]
    lane = lanes_of(h)
    wx = h + h_next
    wy = h + roll(h, -1, 1)
    wz = h + jnp.where(lane < width - step, roll(h, -step, 2), 0.0)
    before = jnp.where(lane >= step, roll(h, step, 2), 0.0)
    total = wx + wy + wz + ((h + h_prev) + (h + roll(h, 1, 1)) + (h + before))
    return wx, wy, jnp.where(lane < width - step, wz, 0.0), total


def scaled_inverse(total, h):
    return jnp.where(h > 0.0, OMEGA / total, 0.0)


def local_spread(v, v_next, from_prev, wx, wy, wz, step):
    return (
        (wx * v_next + from_prev)
        + (wy * roll(v, -1, 1) + roll(wy * v, 1, 1))
        + (wz * roll(v, -step, 2) + roll(wz * v, step, 2))
    )


def shift_up(value):
    return jnp.concatenate([value[1:], jnp.zeros_like(value[:1])], axis=0)


def shift_down(value):
    return jnp.concatenate([jnp.zeros_like(value[:1]), value[:-1]], axis=0)


def next_x(value, step):
    turned = roll(value, -step, 2)
    return jnp.where(lanes_of(value) < value.shape[-1] - step, turned, shift_up(turned))


def prev_x(value, step):
    turned = roll(value, step, 2)
    return jnp.where(lanes_of(value) >= step, turned, shift_down(turned))


def whole_faces(h, span, xstep, zstep):
    in_span = lanes_of(h) % span
    row = rows_of(h)
    not_last_z, not_first_z = in_span < span - zstep, in_span >= zstep
    not_last_y, not_first_y = row < h.shape[1] - 1, row >= 1
    wx = h + next_x(h, xstep)
    wy = h + jnp.where(not_last_y, roll(h, -1, 1), 0.0)
    wz = h + jnp.where(not_last_z, roll(h, -zstep, 2), 0.0)
    back = h + prev_x(h, xstep)
    back = back + (h + jnp.where(not_first_y, roll(h, 1, 1), 0.0))
    back = back + (h + jnp.where(not_first_z, roll(h, zstep, 2), 0.0))
    total = wx + wy + wz + back
    return wx, jnp.where(not_last_y, wy, 0.0), jnp.where(not_last_z, wz, 0.0), OMEGA / total


def whole_spread(v, wx, wy, wz, xstep, zstep):
    return (
        (wx * next_x(v, xstep) + prev_x(wx * v, xstep))
        + (wy * roll(v, -1, 1) + roll(wy * v, 1, 1))
        + (wz * roll(v, -zstep, 2) + roll(wz * v, zstep, 2))
    )


def slabs(first, last, body, size=SLAB):
    def step(i, carry):
        body(first + i * size)
        return carry

    lax.fori_loop(0, (last - first) // size, step, 0)


def part(ref, start, size=SLAB, rows=slice(None)):
    return ref[pl.ds(start, size), rows, :]


def halve_rows(value, buffer):
    rows = value.shape[1]
    buffer[...] = value
    return buffer[:, pl.ds(0, rows // 2, stride=2), :] + buffer[:, pl.ds(1, rows // 2, stride=2), :]


def sum_blocks(value, buffer, step):
    pairs = value.reshape((value.shape[0] // 2, 2) + value.shape[1:])
    return add_partner(halve_rows(pairs[:, 0] + pairs[:, 1], buffer), step)


def double_rows(ref, start, size, value):
    rows = value.shape[1]
    ref[pl.ds(start, size), pl.ds(0, rows, stride=2), :] = value
    ref[pl.ds(start, size), pl.ds(1, rows, stride=2), :] = value


def pack_block(values, buffer):
    blocks, rows, width = values[0].shape
    span = width // blocks
    for n, value in enumerate(values):
        buffer[:, n * rows : (n + 1) * rows, :] = value
    used = rows * len(values)
    lane = lane_row(width)
    packed = None
    for x in range(blocks):
        picked = pick_lanes(buffer[x], (lane % span) * blocks)[:used]
        packed = picked if packed is None else jnp.where(lanes_of(picked) // span == x, picked, packed)
    return packed


def coarse_cycle(g2, level2, level3, buffer):
    wx2, wy2, wz2, inv2 = level2
    wx3, wy3, wz3, inv3 = level3
    width = g2.shape[-1]
    span = width // 4
    v2 = inv2 * g2
    r2 = KEEP * g2 + whole_spread(v2, wx2, wy2, wz2, span, 1)
    g3 = 0.125 * halve_rows(add_partner(add_partner(r2, 1), span), buffer)
    v3 = inv3 * g3
    for _ in range(COARSE_SWEEPS - 1):
        v3 = KEEP * v3 + inv3 * (g3 + whole_spread(v3, wx3, wy3, wz3, 2 * span, 2))
    double_rows(buffer, 0, v3.shape[0], v3)
    u2 = v2 + buffer[...]
    return KEEP * u2 + inv2 * (g2 + whole_spread(u2, wx2, wy2, wz2, span, 1))


def spread_out(e2, wide, doubled):
    count, rows, width = e2.shape
    block_rows = rows // lax.axis_size("gy")
    span = width // 4
    wide[...] = jnp.zeros(wide.shape, F32)
    wide[1 : count + 1, 8 : 8 + rows, :] = e2
    gx, gy = lax.axis_index("gx"), lax.axis_index("gy")
    near = wide[pl.ds(gx, 3), pl.ds(gy * block_rows + 8 - block_rows, 16), :]
    lane = lane_row(width)
    kept = 3 * block_rows
    for j in range(1, 11):
        value = pick_lanes(near[j // 4], (j % 4) * span + lane // 4)[:kept]
        doubled[j, pl.ds(0, kept, stride=2), :] = value
        doubled[j, pl.ds(1, kept, stride=2), :] = value


def first_kernel(
    ext, table,
    packed, wx0, wy0, wz0, inv0, tot0, v0, wx1, wy1, wz1, inv1, v1, g1,
    h0, h1, buf0, buf1, buf2, bufp,
):
    planes, rows, width = ext.shape[1:]
    planes1 = planes // 2
    zero = jnp.zeros((1, rows, width), F32)
    for ref in (h0, wx0, v0):
        ref[0:1] = zero
        ref[planes + 1 : planes + 2] = zero
    for ref in (h1, wx1, v1):
        ref[0:1] = zero[:, : rows // 2]
        ref[planes1 + 1 : planes1 + 2] = zero[:, : rows // 2]

    def look_up(i):
        which = part(ext.at[1], i).astype(jnp.int32).reshape(SLAB * rows, width)
        values = jnp.broadcast_to(table[...], which.shape)
        h0[pl.ds(i + 1, SLAB)] = jnp.take_along_axis(values, which, axis=1).reshape(SLAB, rows, width)

    slabs(0, planes, look_up)

    def faces0(i):
        h = part(h0, i + 1)
        wx, wy, wz, total = local_faces(h, part(h0, i + 2), part(h0, i), 1)
        inv = scaled_inverse(total, h)
        wx0[pl.ds(i + 1, SLAB)] = wx
        wy0[pl.ds(i, SLAB)] = wy
        wz0[pl.ds(i, SLAB)] = wz
        tot0[pl.ds(i, SLAB)] = total
        inv0[pl.ds(i, SLAB)] = inv
        v0[pl.ds(i + 1, SLAB)] = inv * part(ext.at[0], i)
        h1[pl.ds(i // 2 + 1, SLAB // 2)] = sum_blocks(h, buf0, 1) * (1.0 / 32.0)

    slabs(0, planes, faces0)

    def resid0(i):
        v = part(v0, i + 1)
        spread = local_spread(
            v, part(v0, i + 2), part(wx0, i) * part(v0, i),
            part(wx0, i + 1), part(wy0, i), part(wz0, i), 1,
        )
        r = KEEP * part(ext.at[0], i) + spread
        g1[pl.ds(i // 2, SLAB // 2)] = sum_blocks(r, buf0, 1) * 0.125

    slabs(0, planes, resid0)

    def faces1(i):
        h = part(h1, i + 1)
        wx, wy, wz, total = local_faces(h, part(h1, i + 2), part(h1, i), 2)
        inv = scaled_inverse(total, h)
        wx1[pl.ds(i + 1, SLAB)] = wx
        wy1[pl.ds(i, SLAB)] = wy
        wz1[pl.ds(i, SLAB)] = wz
        inv1[pl.ds(i, SLAB)] = inv
        v1[pl.ds(i + 1, SLAB)] = inv * part(g1, i)

    slabs(0, planes1, faces1)

    own = slice(8, 16)
    low = HALO // 2
    size = planes1 - HALO
    v = part(v1, low + 1, size)
    r1 = KEEP * part(g1, low, size) + local_spread(
        v, part(v1, low + 2, size), part(wx1, low, size) * part(v1, low, size),
        part(wx1, low + 1, size), part(wy1, low, size), part(wz1, low, size), 2,
    )
    g2 = sum_blocks(r1[:, own], buf1, 2) * 0.125
    h2 = sum_blocks(part(h1, low + 1, size, own), buf2, 2) * (1.0 / 32.0)
    chunk = pack_block([g2, h2], bufp)

    def copy_out(i, carry):
        packed[i] = chunk
        return carry

    lax.fori_loop(0, packed.shape[0], copy_out, 0)


def fine_down(v0, wx0, wy0, wz0, tot0, ext, g1, v1, wx1, wy1, wz1, inv1, buf0, buf1, bufp, rows):
    half = rows.start // 2

    def resid0(i):
        v = part(v0, i + 1)
        spread = local_spread(
            v, part(v0, i + 2), part(wx0, i, rows=rows) * part(v0, i),
            part(wx0, i + 1, rows=rows), part(wy0, i, rows=rows), part(wz0, i, rows=rows), 1,
        )
        r = (part(ext.at[0], i, rows=rows) - part(tot0, i, rows=rows) * v) + spread
        coarse = sum_blocks(r, buf0, 1) * 0.125
        g1[pl.ds(i // 2, SLAB // 2), half : half + coarse.shape[1], :] = coarse

    slabs(HALO - 4, ext.shape[1] - HALO + 4, resid0)
    low = HALO // 2
    size = ext.shape[1] // 2 - HALO
    v1[pl.ds(low - 1, size + 4)] = part(inv1, low - 2, size + 4) * part(g1, low - 2, size + 4)
    v = part(v1, low + 1, size)
    r1 = KEEP * part(g1, low, size) + local_spread(
        v, part(v1, low + 2, size), part(wx1, low, size) * part(v1, low, size),
        part(wx1, low + 1, size), part(wy1, low, size), part(wz1, low, size), 2,
    )
    g2 = sum_blocks(r1[:, 8:16], buf1, 2) * 0.125
    return pack_block([g2], bufp)


def level1_up(first, last, doubled, v1, g1, wx1, wy1, wz1, inv1, u1, e0):
    count = last - first + 2

    def correct(i):
        e = doubled[pl.ds(i // 2 + 1, SLAB // 2)]
        e = jnp.broadcast_to(e[:, None], (SLAB // 2, 2) + e.shape[1:]).reshape((SLAB,) + e.shape[1:])
        u1[pl.ds(i + 1, SLAB)] = part(v1, i + 1) + e

    start = (first - 1) // 2 * 2
    stop = start + -(-(first - 1 - start + count) // SLAB) * SLAB
    slabs(start, stop, correct)

    def sweep(i):
        u = part(u1, i + 1)
        spread = local_spread(
            u, part(u1, i + 2), part(wx1, i) * part(u1, i),
            part(wx1, i + 1), part(wy1, i), part(wz1, i), 2,
        )
        double_rows(e0, i, SLAB, KEEP * u + part(inv1, i) * (part(g1, i) + spread))

    slabs(first, last, sweep)


def second_kernel(
    got, ext, wx0, wy0, wz0, inv0, tot0, v0, wx1, wy1, wz1, inv1, v1, g1,
    packed, v0n, v1n, g1n, wx2, wy2, wz2, inv2, wx3, wy3, wz3, inv3,
    g2, h2, buf2, wide, doubled, u1, e0, u0, v0m, buf0, buf1, bufp,
):
    count, rows2, width = g2.shape
    gy_count = lax.axis_size("gy")
    block = rows2 // gy_count

    def unpack(i, carry):
        for y in range(gy_count):
            both = got[i * gy_count + y]
            g2[i, y * block : (y + 1) * block, :] = both[:block]
            h2[i, y * block : (y + 1) * block, :] = both[block:]
        return carry

    lax.fori_loop(0, count, unpack, 0)

    span = width // 4
    h = h2[...]
    level2 = whole_faces(h, span, span, 1)
    h3 = halve_rows(add_partner(add_partner(h, 1), span), buf2) * (1.0 / 32.0)
    level3 = whole_faces(h3, span, 2 * span, 2)
    for ref, value in zip((wx2, wy2, wz2, inv2, wx3, wy3, wz3, inv3), level2 + level3):
        ref[...] = value
    spread_out(coarse_cycle(g2[...], level2, level3, buf2), wide, doubled)

    planes = ext.shape[1]
    rows = slice(TRIM, ext.shape[2] - TRIM)
    level1_up(2, planes // 2 - 2, doubled, v1, g1, wx1, wy1, wz1, inv1, u1, e0)

    def correct(i):
        e = part(e0, i // 2, SLAB // 2, rows)
        e = jnp.broadcast_to(e[:, None], (SLAB // 2, 2) + e.shape[1:]).reshape((SLAB,) + e.shape[1:])
        u0[pl.ds(i + 1, SLAB)] = part(v0, i + 1, rows=rows) + e

    slabs(HALO - 8, planes - HALO + 8, correct)

    def sweep(source, target):
        def body(i):
            u = part(source, i + 1)
            spread = local_spread(
                u, part(source, i + 2), part(wx0, i, rows=rows) * part(source, i),
                part(wx0, i + 1, rows=rows), part(wy0, i, rows=rows), part(wz0, i, rows=rows), 1,
            )
            target[pl.ds(i + 1, SLAB)] = KEEP * u + part(inv0, i, rows=rows) * (
                part(ext.at[0], i, rows=rows) + spread
            )

        return body

    slabs(HALO - 6, planes - HALO + 6, sweep(u0, v0m))
    slabs(HALO - 6, planes - HALO + 6, sweep(v0m, v0n))
    g1n[...] = jnp.zeros(g1n.shape, F32)
    v1n[...] = jnp.zeros(v1n.shape, F32)
    chunk = fine_down(
        v0n, wx0, wy0, wz0, tot0, ext, g1n, v1n, wx1, wy1, wz1, inv1, buf0, buf1, bufp, rows
    )

    def copy_out(i, carry):
        packed[i] = chunk
        return carry

    lax.fori_loop(0, packed.shape[0], copy_out, 0)


def third_kernel(
    got, ext, wx0, wy0, wz0, inv0, v0, wx1, wy1, wz1, inv1, v1, g1,
    wx2, wy2, wz2, inv2, wx3, wy3, wz3, inv3,
    out,
    g2, buf2, wide, doubled, u1, e0, u0,
):
    count, rows2, width = g2.shape
    gy_count = lax.axis_size("gy")
    block = rows2 // gy_count

    def unpack(i, carry):
        for y in range(gy_count):
            g2[i, y * block : (y + 1) * block, :] = got[i * gy_count + y]
        return carry

    lax.fori_loop(0, count, unpack, 0)
    level2 = (wx2[...], wy2[...], wz2[...], inv2[...])
    level3 = (wx3[...], wy3[...], wz3[...], inv3[...])
    spread_out(coarse_cycle(g2[...], level2, level3, buf2), wide, doubled)

    planes = ext.shape[1]
    rows = slice(TRIM, ext.shape[2] - TRIM)
    level1_up(HALO // 2 - 2, planes // 2 - HALO // 2 + 2, doubled, v1, g1, wx1, wy1, wz1, inv1, u1, e0)

    def correct(i):
        e = part(e0, i // 2, SLAB // 2, rows)
        e = jnp.broadcast_to(e[:, None], (SLAB // 2, 2) + e.shape[1:]).reshape((SLAB,) + e.shape[1:])
        u0[pl.ds(i + 1, SLAB)] = part(v0, i + 1) + e

    slabs(HALO - 2, planes - HALO + 2, correct)
    own = slice(8, 8 + out.shape[1])

    def sweep(i):
        u = part(u0, i + 1)
        spread = local_spread(
            u, part(u0, i + 2), part(wx0, i, rows=rows) * part(u0, i),
            part(wx0, i + 1, rows=rows), part(wy0, i, rows=rows), part(wz0, i, rows=rows), 1,
        )
        result = KEEP * u + part(inv0, i, rows=rows) * (part(ext.at[0], i, rows=rows) + spread)
        out[pl.ds(i - HALO, SLAB)] = result[:, own]

    slabs(HALO, planes - HALO, sweep)


def kernel_call(body, outs, scratch, args):
    def size(shape):
        total = 4
        for length in shape:
            total *= length
        return total

    shapes = [a.shape for a in args] + list(outs) + list(scratch)
    limit = sum(size(s) for s in shapes) + (8 << 20)
    return pl.pallas_call(
        body,
        out_shape=[jax.ShapeDtypeStruct(s, F32) for s in outs],
        in_specs=[pl.BlockSpec(memory_space=pltpu.VMEM)] * len(args),
        out_specs=[pl.BlockSpec(memory_space=pltpu.VMEM)] * len(outs),
        scratch_shapes=[pltpu.VMEM(s, F32) for s in scratch],
        compiler_params=pltpu.CompilerParams(vmem_limit_bytes=limit),
    )(*args)


def local(right_side, material, conductivity):
    bx, by, bz = right_side.shape
    gx_count, gy_count = lax.axis_size("gx"), lax.axis_size("gy")
    devices = gx_count * gy_count

    block = jnp.stack([right_side, (material + 1).astype(F32)])
    below, above = pair_exchange(block, block, "gy")
    block = jnp.concatenate([below, block, above], axis=2)
    below, above = pair_exchange(block[:, :HALO], block[:, bx - HALO :], "gx")
    ext = jnp.concatenate([below, block, above], axis=1)
    table = jnp.pad(0.5 * conductivity, (1, bz - 1 - conductivity.shape[0]))[None]

    X, Y = bx + 2 * HALO, 3 * by
    X1, Y1 = X // 2, Y // 2
    T = Y - 2 * TRIM
    xb, yb = bx // 4, by // 4
    full0, pad0 = (X, Y, bz), (X + 2, Y, bz)
    full1, pad1 = (X1, Y1, bz), (X1 + 2, Y1, bz)
    packed, wx0, wy0, wz0, inv0, tot0, v0, wx1, wy1, wz1, inv1, v1, g1 = kernel_call(
        first_kernel,
        [(devices, 2 * yb, bz), pad0, full0, full0, full0, full0, pad0, pad1, full1, full1, full1, pad1, full1],
        [pad0, pad1, (SLAB // 2, Y, bz), (xb, 2 * yb, bz), (xb, 2 * yb, bz), (xb, 8, bz)],
        [ext, table],
    )
    got = everywhere(packed)
    level2 = (gx_count, gy_count * yb, bz)
    level3 = (gx_count, gy_count * yb // 2, bz)
    coarse_scratch = [
        level2, (gx_count + 2, gy_count * yb + 16, bz), (3 * xb, Y1, bz), pad1, (X1, Y, bz), (X + 2, T, bz),
    ]
    packed, v0, v1, g1, *levels = kernel_call(
        second_kernel,
        [(devices, yb, bz), (X + 2, T, bz), pad1, full1] + [level2] * 4 + [level3] * 4,
        [level2, level2] + coarse_scratch
        + [(X + 2, T, bz), (SLAB // 2, T, bz), (xb, 2 * yb, bz), (xb, 8, bz)],
        [got, ext, wx0, wy0, wz0, inv0, tot0, v0, wx1, wy1, wz1, inv1, v1, g1],
    )
    got = everywhere(packed)
    (out,) = kernel_call(
        third_kernel,
        [(bx, by, bz)],
        [level2] + coarse_scratch,
        [got, ext, wx0, wy0, wz0, inv0, v0, wx1, wy1, wz1, inv1, v1, g1] + levels,
    )
    return out


def solution(mesh):
    return jax.shard_map(
        local,
        mesh=mesh,
        in_specs=(P("gx", "gy", None), P("gx", "gy", None), P()),
        out_specs=P("gx", "gy", None),
        check_vma=False,
    )
```

time: 344 us -> 67.1 us (0.20); the launches traced: 340 us -> 66.9 us
  starting transfers between devices: 156 us -> 7.34 us
  waiting for transfers between devices: 113 us -> 7.22 us
  local copies, waits for them, and re-layouts: 37.6 us -> 0.08 us
  blocking collectives: 0 us -> 36.6 us
  other arithmetic: 31 us -> 2.28 us
  Pallas kernels: 0 us -> 13.3 us
    ppermute x79 -> x4, starting transfers between devices: 156 us -> 7.34 us  [the longest x2 5.97 us: pair_exchange(): from_near = lax.ppermute(jnp.where(odd, to_low, to_high), axis, near)]
    ppermute x79 -> x4, waiting for transfers between devices: 113 us -> 7.22 us  [the longest x2 7.21 us: pair_exchange(): from_near = lax.ppermute(jnp.where(odd, to_low, to_high), axis, near)]
    all_to_all x0 -> x2, blocking collectives: none -> 36.6 us  [everywhere(): return lax.all_to_all(copies, ('gx', 'gy'), 0, 0)]
    reshape x19 -> x0, local copies, waits for them, and re-layouts: 34 us -> none  [the longest x7 31.8 us: restrict(): field.reshape(sx // 2, 2, sy // 2, 2, sz // 2, 2).mean(axis=(1, 3, 5))]
    pallas_call x0 -> x3, Pallas kernels: none -> 13.3 us  [kernel_call(): pl.pallas_call(body, out_shape=[jax.ShapeDtypeStruct(s, F32) for s in out...]
    reduce_sum x9 -> x0, other arithmetic: 12.8 us -> none  [restrict(): field.reshape(sx // 2, 2, sy // 2, 2, sz // 2, 2).mean(axis=(1, 3, 5))]
    select_n x14 -> x3, other arithmetic: 11.2 us -> 0.22 us  [the longest x2 0.13 us: pair_exchange(): jnp.where(odd, from_near, from_far)]
  transfers between devices with their start and end apart: 79 -> 4, of which waited for: 43 -> 2; matrix products, arithmetic and copies ran while one was open for 10% -> 0% of each run, Pallas kernels for 0% -> 0%
where the time goes in v1:
time: 67.1 us; the launch traced here: 66.9 us
  blocking collectives  36.6 us (55%)
  Pallas kernels  13.3 us (20%)
  starting transfers between devices  7.34 us (11%)
  waiting for transfers between devices  7.22 us (11%)
  other arithmetic  2.28 us (3%)
    all_to_all x2, blocking collectives, everywhere(): return lax.all_to_all(copies, ('gx', 'gy'), 0, 0)  36.6 us
    pallas_call x3, Pallas kernels, kernel_call(): pl.pallas_call(body, out_shape=[jax.ShapeDtypeStruct(s, F32) for s in out...  13.3 us
    ppermute x2, waiting for transfers between devices, pair_exchange(): from_near = lax.ppermute(jnp.where(odd, to_low, to_high), axis, near)  7.21 us
    ppermute x2, starting transfers between devices, pair_exchange(): from_near = lax.ppermute(jnp.where(odd, to_low, to_high), axis, near)  5.97 us
    another operation x2, other arithmetic, local(): block = jnp.stack([right_side, (material + 1).astype(F32)])  1.88 us
    ppermute x2, starting transfers between devices, pair_exchange(): from_far = lax.ppermute(jnp.where(odd, to_high, to_low), axis, far)  1.38 us
  transfers between devices with their start and end apart: 4, of which 2 were waited for; matrix products, arithmetic and copies ran while one was open for 0% of the time, Pallas kernels for 0%

profile of v1, /device:TPU:0, one launch (start us, length us, event | category | flops | bytes accessed | tf_op | source)
XLA Modules:
  0.0 66.9 jit_solution(1525923768271492699)
XLA Ops:
  0.0 0.0 copy-start
  0.0 1.0 %convert_bitcast_fusion = f32[1,16,16,128]{3,2,1,0:T(8,128)S(1)} fusion(s32[16,16,128]{2,1,0:T(8,128)} %param.4), kind=kLoop, calls=%fused_computation.7 | loop fusion | flops 65536 | bytes 262144 | tf_op jit(solution)/shard_map/stack | solution.py:460
  1.0 0.9 %pad_maximum_fusion.2 = f32[2,16,16,128]{3,2,1,0:T(8,128)S(1)} fusion(f32[1,16,16,128]{3,2,1,0:T(8,128)S(1)} %convert_bitcast_fusion, f32[1,16,16,128]{3,2,1,0:T(8,128)} %bitcast.5), kind=kLoop, calls=%fused_computation.6 | loop fusion | flops 65536 | bytes 524288 | tf_op jit(solution)/shard_map/stack | solution.py:460
  1.9 0.7 %collective-permute-start.1 = (f32[2,16,16,128]{3,2,1,0:T(8,128)S(1)}, f32[2,16,16,128]{3,2,1,0:T(8,128)S(1)}, u32[]{:S(2)}, u32[]{:S(2)}) collective-permute-start(f32[2,16,16,128]{3,2,1,0:T(8,128)S(1)} %pad_maximum_fusion.2), channel_id=1, source_target_pairs={{1,2},{2,1},{5,6},{6,5},{9,10},{10,9},{13,14},{14,13},{17,18},{18,... | collective-permute-start | bytes 786440 | tf_op jit(solution)/shard_map/ppermute | solution.py:26
  2.6 5.9 %collective-permute-start = (f32[2,16,16,128]{3,2,1,0:T(8,128)S(1)}, f32[2,16,16,128]{3,2,1,0:T(8,128)S(1)}, u32[]{:S(2)}, u32[]{:S(2)}) collective-permute-start(f32[2,16,16,128]{3,2,1,0:T(8,128)S(1)} %pad_maximum_fusion.2), channel_id=1, source_target_pairs={{0,1},{1,0},{2,3},{3,2},{4,5},{5,4},{6,7},{7,6},{8,9},{9,8},{10,11... | collective-permute-start | bytes 786440 | tf_op jit(solution)/shard_map/ppermute | solution.py:25
  8.5 0.0 collective-permute-done.1
  8.5 6.0 %collective-permute-done = f32[2,16,16,128]{3,2,1,0:T(8,128)S(1)} collective-permute-done((f32[2,16,16,128]{3,2,1,0:T(8,128)S(1)}, f32[2,16,16,128]{3,2,1,0:T(8,128)S(1)}, u32[]{:S(2)}, u32[]{:S(2)}) %collective-permute-start) | collective-permute-done | bytes 262176 | tf_op jit(solution)/shard_map/ppermute | solution.py:25
  14.5 0.0 copy-done
  14.5 0.0 copy-start.1
  14.6 0.1 pad_maximum_fusion.1
  14.6 0.1 slice_select_fusion.1
  14.7 0.1 collective-permute-start.2
  14.8 0.7 %collective-permute-start.3 = (f32[2,12,48,128]{3,2,1,0:T(8,128)S(1)}, f32[2,12,48,128]{3,2,1,0:T(8,128)S(1)}, u32[]{:S(2)}, u32[]{:S(2)}) collective-permute-start(f32[2,12,48,128]{3,2,1,0:T(8,128)S(1)} %get-tuple-element.58), channel_id=1, source_target_pairs={{4,8},{12,16},{20,24},{8,4},{16,12},{24,20},{5,9},{13,17},{21,25},... | collective-permute-start | bytes 1769480 | tf_op jit(solution)/shard_map/ppermute | solution.py:26
  15.5 0.0 copy-done.1
  15.5 0.1 pad_bitcast_fusion.table
  15.6 1.2 %collective-permute-done.2 = f32[2,12,48,128]{3,2,1,0:T(8,128)S(1)} collective-permute-done((f32[2,12,48,128]{3,2,1,0:T(8,128)S(1)}, f32[2,12,48,128]{3,2,1,0:T(8,128)S(1)}, u32[]{:S(2)}, u32[]{:S(2)}) %collective-permute-start.2) | collective-permute-done | bytes 589856 | tf_op jit(solution)/shard_map/ppermute | solution.py:25
  16.8 0.0 collective-permute-done.3
  16.8 0.1 broadcast_select_fusion.1
  16.9 0.1 pad_maximum_fusion.ext
  17.0 5.8 %shard_map.37 = (f32[32,8,128]{2,1,0:T(8,128)S(1)}, f32[42,48,128]{2,1,0:T(8,128)S(1)}, f32[40,48,128]{2,1,0:T(8,128)S(1)}, f32[40,48,128]{2,1,0:T(8,128)S(1)}, ...) custom-call(f32[2,40,48,128]{3,2,1,0:T(8,128)S(1)} %pad_maximum_fusi, ...), custom_call_target="tpu_custom_call" | custom-call | tf_op jit(solution)/shard_map/pallas_call | solution.py:445
  22.8 27.4 %all_to_all.10.got = f32[32,8,128]{2,1,0:T(8,128)S(1)} all-to-all(f32[32,8,128]{2,1,0:T(8,128)S(1)} %get-tuple-element.30), channel_id=1, replica_groups=mesh['gx'=8,'gy'=4] {'gx','gy'}, dimensions={0} | all-to-all | bytes 262144 | tf_op jit(solution)/shard_map/all_to_all | solution.py:31
  50.2 5.0 %shard_map.38 = (f32[32,4,128]{2,1,0:T(4,128)S(1)}, f32[42,32,128]{2,1,0:T(8,128)S(1)}, f32[22,24,128]{2,1,0:T(8,128)S(1)}, f32[20,24,128]{2,1,0:T(8,128)S(1)}, ...) custom-call(f32[32,8,128]{2,1,0:T(8,128)S(1)} %all_to_all.10.got, ...), custom_call_target="tpu_custom_call" | custom-call | tf_op jit(solution)/shard_map/pallas_call | solution.py:445
  55.2 9.2 %all_to_all.11.got = f32[32,4,128]{2,1,0:T(4,128)S(1)} all-to-all(f32[32,4,128]{2,1,0:T(4,128)S(1)} %get-tuple-element.43), channel_id=1, replica_groups=mesh['gx'=8,'gy'=4] {'gx','gy'}, dimensions={0} | all-to-all | bytes 131072 | tf_op jit(solution)/shard_map/all_to_all | solution.py:31
  64.4 2.5 %shard_map.39 = f32[16,16,128]{2,1,0:T(8,128)} custom-call(f32[32,4,128]{2,1,0:T(4,128)S(1)} %all_to_all.11.got, f32[2,40,48,128]{3,2,1,0:T(8,128)S(1)} %pad_maximum_fusion.ext, f32[42,48,128]{2,1,0:T(8,128)S(1)} %get-tuple-element.31.wx0, f32[40,48,128]{2,1,0:T(8,128)S(1)} %get-tuple-element.32.wy0, f32[40,48,128]{2,1,0:T(8,128)S(1)} %get-tuple-element.33.wz0, ...), custom_call_target="tpu_custom_call" | custom-call | tf_op jit(solution)/shard_map/pallas_call | solution.py:445
  (2 shorter events, 0.0 us)
Async XLA Ops:
  0.0 14.5 %copy-start = (f32[16,16,128]{2,1,0:T(8,128)S(1)}, f32[16,16,128]{2,1,0:T(8,128)}, u32[]{:S(2)}) copy-start(f32[16,16,128]{2,1,0:T(8,128)} %param.3) | copy-start | bytes 393220
  1.9 6.6 %collective-permute-start.1 = (f32[2,16,16,128]{3,2,1,0:T(8,128)S(1)}, f32[2,16,16,128]{3,2,1,0:T(8,128)S(1)}, u32[]{:S(2)}, u32[]{:S(2)}) collective-permute-start(f32[2,16,16,128]{3,2,1,0:T(8,128)S(1)} %pad_maximum_fusion.2), channel_id=1, source_target_pairs={{1,2},{2,1},{5,6},{6,5},{9,10},{10,9},{13,14},{14,13},{17,18},{18,... | collective-permute-start | bytes 786440 | tf_op jit(solution)/shard_map/ppermute | solution.py:26
  2.6 11.9 %collective-permute-start = (f32[2,16,16,128]{3,2,1,0:T(8,128)S(1)}, f32[2,16,16,128]{3,2,1,0:T(8,128)S(1)}, u32[]{:S(2)}, u32[]{:S(2)}) collective-permute-start(f32[2,16,16,128]{3,2,1,0:T(8,128)S(1)} %pad_maximum_fusion.2), channel_id=1, source_target_pairs={{0,1},{1,0},{2,3},{3,2},{4,5},{5,4},{6,7},{7,6},{8,9},{9,8},{10,11... | collective-permute-start | bytes 786440 | tf_op jit(solution)/shard_map/ppermute | solution.py:25
  14.5 1.0 %copy-start.1 = (f32[16]{0:T(128)S(1)}, f32[16]{0:T(128)}, u32[]{:S(2)}) copy-start(f32[16]{0:T(128)} %param.5) | copy-start | bytes 196
  14.7 2.1 %collective-permute-start.2 = (f32[2,12,48,128]{3,2,1,0:T(8,128)S(1)}, f32[2,12,48,128]{3,2,1,0:T(8,128)S(1)}, u32[]{:S(2)}, u32[]{:S(2)}) collective-permute-start(f32[2,12,48,128]{3,2,1,0:T(8,128)S(1)} %get-tuple-element.57), channel_id=1, source_target_pairs={{0,4},{4,0},{8,12},{12,8},{16,20},{20,16},{24,28},{28,24},{1,5},{5... | collective-permute-start | bytes 1769480 | tf_op jit(solution)/shard_map/ppermute | solution.py:25
  14.8 2.0 %collective-permute-start.3 = (f32[2,12,48,128]{3,2,1,0:T(8,128)S(1)}, f32[2,12,48,128]{3,2,1,0:T(8,128)S(1)}, u32[]{:S(2)}, u32[]{:S(2)}) collective-permute-start(f32[2,12,48,128]{3,2,1,0:T(8,128)S(1)} %get-tuple-element.58), channel_id=1, source_target_pairs={{4,8},{12,16},{20,24},{8,4},{16,12},{24,20},{5,9},{13,17},{21,25},... | collective-permute-start | bytes 1769480 | tf_op jit(solution)/shard_map/ppermute | solution.py:26

commit v2 on v1

v2 whole, which is shorter than its diff:
```python
import jax
import jax.numpy as jnp
from jax import lax
from jax.experimental import pallas as pl
from jax.experimental.pallas import tpu as pltpu
from jax.sharding import PartitionSpec as P

COARSE_SWEEPS = 6
OMEGA = 0.8
KEEP = 1.0 - OMEGA
HALO = 12
NEAR = 8
FAR = HALO - NEAR
BASE = 8
F32 = jnp.float32


def near_partner(index, count):
    return index ^ 1 if index ^ 1 < count else index


def far_partner(index, count):
    return (index - 1 ^ 1) + 1


def route(axis, far):
    gx_count, gy_count = lax.axis_size("gx"), lax.axis_size("gy")
    pairs = []
    for x in range(gx_count):
        for y in range(gy_count):
            if axis == "gx":
                if not far:
                    a, b = near_partner(x, gx_count), y
                elif 0 < x < gx_count - 1:
                    a, b = far_partner(x, gx_count), y
                else:
                    a, b = x, near_partner(y, gy_count)
            else:
                if not far:
                    a, b = x, near_partner(y, gy_count)
                elif 0 < y < gy_count - 1:
                    a, b = x, far_partner(y, gy_count)
                else:
                    a, b = near_partner(x, gx_count), y
            pairs.append((x * gy_count + y, a * gy_count + b))
    return pairs


def trade(to_near, to_far, axis):
    from_far = lax.ppermute(to_far, ("gx", "gy"), route(axis, True))
    from_near = lax.ppermute(to_near, ("gx", "gy"), route(axis, False))
    return from_near, from_far


def everywhere(copies):
    return lax.all_to_all(copies, ("gx", "gy"), 0, 0)


def is_odd(axis):
    return lax.axis_index(axis) % 2 == 1


def has_below(axis):
    return lax.axis_index(axis) > 0


def has_above(axis):
    return lax.axis_index(axis) < lax.axis_size(axis) - 1


def below(near, far, axis):
    return jnp.where(has_below(axis), jnp.where(is_odd(axis), near, far), 0.0)


def above(near, far, axis):
    return jnp.where(has_above(axis), jnp.where(is_odd(axis), far, near), 0.0)


def roll(value, shift, axis):
    return pltpu.roll(value, shift % value.shape[axis], axis=axis)


def lanes_of(value):
    return lax.broadcasted_iota(jnp.int32, value.shape, value.ndim - 1)


def rows_of(value):
    return lax.broadcasted_iota(jnp.int32, value.shape, value.ndim - 2)


def lane_row(width):
    return lax.broadcasted_iota(jnp.int32, (1, width), 1)


def pick_lanes(value, index):
    flat = value.reshape(-1, value.shape[-1])
    index = jnp.broadcast_to(index, flat.shape)
    return jnp.take_along_axis(flat, index, axis=1).reshape(value.shape)


def add_partner(value, apart):
    return value + pick_lanes(value, lane_row(value.shape[-1]) ^ apart)


def shift_up(value):
    return jnp.concatenate([value[1:], jnp.zeros_like(value[:1])], axis=0)


def shift_down(value):
    return jnp.concatenate([jnp.zeros_like(value[:1]), value[:-1]], axis=0)


def next_x(value, step):
    turned = roll(value, -step, 2)
    return jnp.where(lanes_of(value) < value.shape[-1] - step, turned, shift_up(turned))


def prev_x(value, step):
    turned = roll(value, step, 2)
    return jnp.where(lanes_of(value) >= step, turned, shift_down(turned))


def whole_faces(h, span, xstep, zstep):
    in_span = lanes_of(h) % span
    row = rows_of(h)
    not_last_z, not_first_z = in_span < span - zstep, in_span >= zstep
    not_last_y, not_first_y = row < h.shape[1] - 1, row >= 1
    wx = h + next_x(h, xstep)
    wy = h + jnp.where(not_last_y, roll(h, -1, 1), 0.0)
    wz = h + jnp.where(not_last_z, roll(h, -zstep, 2), 0.0)
    back = h + prev_x(h, xstep)
    back = back + (h + jnp.where(not_first_y, roll(h, 1, 1), 0.0))
    back = back + (h + jnp.where(not_first_z, roll(h, zstep, 2), 0.0))
    total = wx + wy + wz + back
    return wx, jnp.where(not_last_y, wy, 0.0), jnp.where(not_last_z, wz, 0.0), OMEGA / total


def whole_spread(v, wx, wy, wz, xstep, zstep):
    return (
        (wx * next_x(v, xstep) + prev_x(wx * v, xstep))
        + (wy * roll(v, -1, 1) + roll(wy * v, 1, 1))
        + (wz * roll(v, -zstep, 2) + roll(wz * v, zstep, 2))
    )


def read(array, start, size, top, rows, dx=0, dy=0):
    ref, planes_off, rows_off = array
    return ref[pl.ds(start + planes_off + dx, size), pl.ds(top + rows_off + dy, rows), :]


def write(array, start, top, value):
    ref, planes_off, rows_off = array
    ref[pl.ds(start + planes_off, value.shape[0]), pl.ds(top + rows_off, value.shape[1]), :] = value


def slabs(first, last, size, body):
    if first + size == last:
        body(first)
        return

    def step(i, carry):
        body(first + i * size)
        return carry

    lax.fori_loop(0, (last - first) // size, step, 0)


def faces(h, window, step):
    here = read(h, *window)
    lane = lanes_of(here)
    width = here.shape[-1]
    not_last = lane < width - step
    wx = here + read(h, *window, dx=1)
    wy = here + read(h, *window, dy=1)
    wz = here + jnp.where(not_last, roll(here, -step, 2), 0.0)
    back = (here + read(h, *window, dx=-1)) + (here + read(h, *window, dy=-1))
    back = back + (here + jnp.where(lane >= step, roll(here, step, 2), 0.0))
    total = (wx + wy + wz) + back
    inverse = jnp.where(here > 0.0, OMEGA / total, 0.0)
    return here, wx, wy, jnp.where(not_last, wz, 0.0), total, inverse


def spread(v, weights, window, step):
    wx, wy, wz = weights
    here = read(v, *window)
    wz = read(wz, *window)
    return here, (
        (read(wx, *window) * read(v, *window, dx=1) + read(wx, *window, dx=-1) * read(v, *window, dx=-1))
        + (read(wy, *window) * read(v, *window, dy=1) + read(wy, *window, dy=-1) * read(v, *window, dy=-1))
        + (wz * roll(here, -step, 2) + roll(wz * here, step, 2))
    )


def halve_rows(value, buffer):
    count, rows, _ = value.shape
    buffer[0:count, 0:rows, :] = value
    return (
        buffer[0:count, pl.ds(0, rows // 2, stride=2), :] + buffer[0:count, pl.ds(1, rows // 2, stride=2), :]
    )


def sum_blocks(value, buffer, step):
    pairs = value.reshape((value.shape[0] // 2, 2) + value.shape[1:])
    return add_partner(halve_rows(pairs[:, 0] + pairs[:, 1], buffer), step)


def double_rows(ref, start, value):
    count, rows, _ = value.shape
    ref[pl.ds(start, count), pl.ds(0, rows, stride=2), :] = value
    ref[pl.ds(start, count), pl.ds(1, rows, stride=2), :] = value


def double_planes(value):
    wide = jnp.broadcast_to(value[:, None], (value.shape[0], 2) + value.shape[1:])
    return wide.reshape((2 * value.shape[0],) + value.shape[1:])


def pack_block(values, buffer):
    blocks, rows, width = values[0].shape
    span = width // blocks
    for n, value in enumerate(values):
        buffer[:, n * rows : (n + 1) * rows, :] = value
    used = rows * len(values)
    lane = lane_row(width)
    packed = None
    for x in range(blocks):
        picked = pick_lanes(buffer[x], (lane % span) * blocks)[:used]
        packed = picked if packed is None else jnp.where(lanes_of(picked) // span == x, picked, packed)
    return packed


def send_to_all(packed, chunk):
    def copy_out(i, carry):
        packed[i] = chunk
        return carry

    lax.fori_loop(0, packed.shape[0], copy_out, 0)


def coarse_cycle(g2, level2, level3, buffer):
    wx2, wy2, wz2, inv2 = level2
    wx3, wy3, wz3, inv3 = level3
    width = g2.shape[-1]
    span = width // 4
    v2 = inv2 * g2
    r2 = KEEP * g2 + whole_spread(v2, wx2, wy2, wz2, span, 1)
    g3 = 0.125 * halve_rows(add_partner(add_partner(r2, 1), span), buffer)
    v3 = inv3 * g3
    for _ in range(COARSE_SWEEPS - 1):
        v3 = KEEP * v3 + inv3 * (g3 + whole_spread(v3, wx3, wy3, wz3, 2 * span, 2))
    double_rows(buffer, 0, v3)
    u2 = v2 + buffer[...]
    return KEEP * u2 + inv2 * (g2 + whole_spread(u2, wx2, wy2, wz2, span, 1))


def spread_out(e2, wide, doubled, planes):
    count, rows, width = e2.shape
    block = rows // lax.axis_size("gy")
    span = width // 4
    wide[0:1] = jnp.zeros((1,) + wide.shape[1:], F32)
    wide[count + 1 : count + 2] = jnp.zeros((1,) + wide.shape[1:], F32)
    wide[1 : count + 1, 0:8, :] = jnp.zeros((count, 8, width), F32)
    wide[1 : count + 1, rows + 8 : rows + 16, :] = jnp.zeros((count, 8, width), F32)
    wide[1 : count + 1, 8 : 8 + rows, :] = e2
    gx, gy = lax.axis_index("gx"), lax.axis_index("gy")
    around = wide[pl.ds(gx, 3), pl.ds(gy * block + 8 - block, 16), :]
    lane = lane_row(width)
    kept = 3 * block
    for j in planes:
        value = pick_lanes(around[j // 4], (j % 4) * span + lane // 4)[:kept]
        doubled[j, pl.ds(0, kept, stride=2), :] = value
        doubled[j, pl.ds(1, kept, stride=2), :] = value


def row_starts(axis, block):
    odd = is_odd(axis)
    low = (0, NEAR)
    high = (block - NEAR, block - HALO)
    to_near = [jnp.where(odd, a, b) for a, b in zip(low, high)]
    to_far = [jnp.where(odd, b, a) for a, b in zip(low, high)]
    return to_near, to_far


def pack_rows(source, starts, first, last, target):
    count = source.shape[0]
    half = (last - first) // 2
    target[0:count] = source[:, pl.ds(starts[0], NEAR), :]
    target[count : count + half, 0:FAR, :] = source[first : first + half, pl.ds(starts[1], FAR), :]
    target[count : count + half, FAR:NEAR, :] = source[first + half : last, pl.ds(starts[1], FAR), :]


def unpack_rows(target, planes_off, top, bottom, count, first, last, near, far):
    half = (last - first) // 2
    for choose, at, edge in ((below, top - NEAR, top - HALO), (above, bottom, bottom + NEAR)):
        target[planes_off : planes_off + count, at : at + NEAR, :] = choose(near[0:count], far[0:count], "gy")
        strips = choose(near[count : count + half], far[count : count + half], "gy")
        target[planes_off + first : planes_off + first + half, edge : edge + FAR, :] = strips[:, 0:FAR]
        target[planes_off + first + half : planes_off + last, edge : edge + FAR, :] = strips[:, FAR:NEAR]


def start_kernel(right, material, cond, h, k_near, k_far, g_near, g_far, table):
    planes, rows, width = material.shape
    table[0:1, 0 : cond.shape[1]] = cond[...]
    which = material[...].reshape(planes * rows, width)
    values = jnp.broadcast_to(0.5 * table[0:1, :], which.shape)
    h[...] = jnp.take_along_axis(values, which, axis=1).reshape(material.shape)
    odd = is_odd("gx")
    k_near[...] = h[pl.ds(jnp.where(odd, 0, planes - HALO), HALO)]
    k_far[...] = h[pl.ds(jnp.where(odd, planes - HALO, 0), HALO)]
    to_near, to_far = row_starts("gy", rows)
    pack_rows(right, to_near, 0, planes, g_near)
    pack_rows(right, to_far, 0, planes, g_far)


def far_planes(planes):
    return HALO - FAR + 1, planes - HALO + FAR - 1


def k_kernel(h, near, far, wide, k_near, k_far):
    block = h.shape[0]
    wide[0:HALO] = below(near[...], far[...], "gx")
    wide[HALO : HALO + block] = h[...]
    wide[HALO + block :] = above(near[...], far[...], "gx")
    first, last = far_planes(wide.shape[0])
    to_near, to_far = row_starts("gy", h.shape[1])
    pack_rows(wide, to_near, first, last, k_near)
    pack_rows(wide, to_far, first, last, k_far)


def plane_strips(rows):
    strips, at = [], 0
    for distance in range(1, HALO):
        cut = (distance // 4) * 4
        tiles = (rows - 2 * cut) // 8
        strips.append((distance, cut, tiles, at))
        at += tiles
    return strips, at


def g_kernel(right, near, far, wide, g_near, g_far):
    block, rows, _ = right.shape
    top = BASE // 2
    wide[:, top + HALO : top + HALO + rows, :] = right[...]
    unpack_rows(wide, 0, top + HALO, top + HALO + rows, block, 0, block, near, far)
    odd = is_odd("gx")
    strips, _ = plane_strips(rows + 2 * HALO)
    for distance, cut, tiles, at in strips:
        low, high = distance - 1, block - distance
        for target, plane in ((g_near, jnp.where(odd, low, high)), (g_far, jnp.where(odd, high, low))):
            for tile in range(tiles):
                target[at + tile] = wide[plane, top + cut + 8 * tile : top + cut + 8 * tile + 8, :]


def first_kernel(
    k_wide, k_near, k_far, g_wide, g_near, g_far,
    packed, g0, wx0, wy0, wz0, inv0, tot0, v0, wx1, wy1, wz1, inv1, v1, g1,
    h0, h1, buf0, bufp,
):
    top = BASE // 2
    planes, rows, width = k_wide.shape
    own = slice(HALO, planes - HALO)
    h0[1 : planes + 1, top + HALO : top + HALO + rows, :] = k_wide[...]
    first, last = far_planes(planes)
    unpack_rows(h0, 1, top + HALO, top + HALO + rows, planes, first, last, k_near, k_far)
    g0[own] = g_wide[...]
    rows = rows + 2 * HALO
    strips, _ = plane_strips(rows)
    for distance, cut, tiles, at in strips:
        for choose, plane in ((below, HALO - distance), (above, planes - HALO - 1 + distance)):
            value = choose(g_near[at : at + tiles], g_far[at : at + tiles], "gx")
            g0[plane, top + cut : top + cut + 8 * tiles, :] = value.reshape(8 * tiles, width)

    aH0, aG0 = (h0, 1, top), (g0, 0, top)
    aWX0, aV0 = (wx0, 1, BASE), (v0, 1, BASE)
    aWY0, aWZ0, aINV0, aTOT0 = ((ref, 0, BASE) for ref in (wy0, wz0, inv0, tot0))
    aH1, aWX1, aV1 = (h1, 1, BASE), (wx1, 1, BASE), (v1, 1, BASE)
    aWY1, aWZ1, aINV1, aG1 = ((ref, 0, BASE) for ref in (wy1, wz1, inv1, g1))
    size = planes // 4

    def faces0(i):
        window = (i, size, 0, rows)
        here, wx, wy, wz, total, inverse = faces(aH0, window, 1)
        write(aWX0, i, 0, wx)
        write(aWY0, i, 0, wy)
        write(aWZ0, i, 0, wz)
        write(aTOT0, i, 0, total)
        write(aINV0, i, 0, inverse)
        write(aV0, i, 0, inverse * read(aG0, *window))
        write(aH1, i // 2, 0, sum_blocks(here, buf0, 1) * (1.0 / 32.0))

    slabs(0, planes, size, faces0)

    def resid0(i):
        window = (i, size, 0, rows)
        _, around = spread(aV0, (aWX0, aWY0, aWZ0), window, 1)
        write(aG1, i // 2, 0, sum_blocks(KEEP * read(aG0, *window) + around, buf0, 1) * 0.125)

    slabs(0, planes, size, resid0)

    planes1, rows1 = planes // 2, -(-rows // 16) * 8

    def faces1(i):
        window = (i, planes1, 0, rows1)
        _, wx, wy, wz, total, inverse = faces(aH1, window, 2)
        write(aWX1, i, 0, wx)
        write(aWY1, i, 0, wy)
        write(aWZ1, i, 0, wz)
        write(aINV1, i, 0, inverse)
        write(aV1, i, 0, inverse * read(aG1, *window))

    slabs(0, planes1, planes1, faces1)

    low = HALO // 2
    window = (low, planes1 - HALO, low, rows // 2 - HALO)
    _, around = spread(aV1, (aWX1, aWY1, aWZ1), window, 2)
    g2 = sum_blocks(KEEP * read(aG1, *window) + around, buf0, 2) * 0.125
    h2 = sum_blocks(read(aH1, *window), buf0, 2) * (1.0 / 32.0)
    send_to_all(packed, pack_block([g2, h2], bufp))


def second_kernel(
    got, g0, wx0, wy0, wz0, inv0, tot0, v0, wx1, wy1, wz1, inv1, v1, g1,
    packed, v0n, v1n, g1n, wx2, wy2, wz2, inv2, wx3, wy3, wz3, inv3,
    g2, h2, buf2, wide, doubled, u1, e0, u0, v0m, buf0, bufp,
):
    count, rows2, width = g2.shape
    gy_count = lax.axis_size("gy")
    block2 = rows2 // gy_count

    def unpack(i, carry):
        for y in range(gy_count):
            both = got[i * gy_count + y]
            g2[i, y * block2 : (y + 1) * block2, :] = both[:block2]
            h2[i, y * block2 : (y + 1) * block2, :] = both[block2:]
        return carry

    lax.fori_loop(0, count, unpack, 0)

    span = width // 4
    h = h2[...]
    level2 = whole_faces(h, span, span, 1)
    h3 = halve_rows(add_partner(add_partner(h, 1), span), buf2) * (1.0 / 32.0)
    level3 = whole_faces(h3, span, 2 * span, 2)
    for ref, value in zip((wx2, wy2, wz2, inv2, wx3, wy3, wz3, inv3), level2 + level3):
        ref[...] = value
    spread_out(coarse_cycle(g2[...], level2, level3, buf2), wide, doubled, range(1, 11))

    top = BASE // 2
    planes = g0.shape[0]
    block = planes - 2 * HALO
    aG0 = (g0, 0, top)
    w0 = (wx0, 1, BASE), (wy0, 0, BASE), (wz0, 0, BASE)
    aINV0, aTOT0, aV0 = (inv0, 0, BASE), (tot0, 0, BASE), (v0, 1, BASE)
    w1 = (wx1, 1, BASE), (wy1, 0, BASE), (wz1, 0, BASE)
    aINV1, aG1, aV1 = (inv1, 0, BASE), (g1, 0, BASE), (v1, 1, BASE)

    low, block1 = HALO // 2, block // 2
    aU1 = (u1, 1, BASE)
    window = (0, planes // 2, 0, planes // 4 // 8 * 8 + 16)
    e1 = doubled[1 : 1 + planes // 4, 2 : 2 + window[3], :]
    write(aU1, 0, 0, read(aV1, *window) + double_planes(e1))
    window = (low - 4, block1 + 8, low - 4, block1 + 8)
    here, around = spread(aU1, w1, window, 2)
    swept = KEEP * here + read(aINV1, *window) * (read(aG1, *window) + around)
    double_rows(e0, low - 4, swept)

    rows = block + 16
    aU0 = (u0, 1, BASE - (HALO - 7))
    aE0 = (e0, 0, -(2 * low - 8))
    aV0M = (v0m, 1, BASE - (HALO - 6))
    aV0N = (v0n, 1, BASE - (HALO - 5))
    size = (block + 16) // 4

    def correct(i):
        window = (i, size, HALO - 7, rows)
        e = double_planes(read(aE0, i // 2, size // 2, HALO - 7, rows))
        write(aU0, i, HALO - 7, read(aV0, *window) + e)

    slabs(HALO - 8, planes - HALO + 8, size, correct)

    def sweep(source, target, margin, size):
        def body(i):
            window = (i, size, HALO - margin, rows)
            here, around = spread(source, w0, window, 1)
            value = KEEP * here + read(aINV0, *window) * (read(aG0, *window) + around)
            write(target, i, HALO - margin, value)

        slabs(HALO - margin, planes - HALO + margin, size, body)

    sweep(aU0, aV0M, 6, (block + 12) // 2)
    sweep(aV0M, aV0N, 5, (block + 10) // 2)

    aG1N, aV1N = (g1n, 0, BASE - (low - 2)), (v1n, 1, BASE - (low - 2))
    size = (block + 8) // 2

    def resid(i):
        window = (i, size, HALO - 4, block + 8)
        here, around = spread(aV0N, w0, window, 1)
        r = (read(aG0, *window) - read(aTOT0, *window) * here) + around
        write(aG1N, i // 2, low - 2, sum_blocks(r, buf0, 1) * 0.125)

    slabs(HALO - 4, planes - HALO + 4, size, resid)

    window = (low - 2, block1 + 4, low - 2, block1 + 4)
    write(aV1N, low - 2, low - 2, read(aINV1, *window) * read(aG1N, *window))
    window = (low, block1, low, block1)
    _, around = spread(aV1N, w1, window, 2)
    send_to_all(packed, pack_block([sum_blocks(KEEP * read(aG1N, *window) + around, buf0, 2) * 0.125], bufp))


def third_kernel(
    got, g0, wx0, wy0, wz0, inv0, v0n, wx1, wy1, wz1, inv1, v1n, g1n,
    wx2, wy2, wz2, inv2, wx3, wy3, wz3, inv3,
    out,
    g2, buf2, wide, doubled, u1, e0, u0,
):
    count, rows2, width = g2.shape
    gy_count = lax.axis_size("gy")
    block2 = rows2 // gy_count

    def unpack(i, carry):
        for y in range(gy_count):
            g2[i, y * block2 : (y + 1) * block2, :] = got[i * gy_count + y]
        return carry

    lax.fori_loop(0, count, unpack, 0)
    level2 = (wx2[...], wy2[...], wz2[...], inv2[...])
    level3 = (wx3[...], wy3[...], wz3[...], inv3[...])
    spread_out(coarse_cycle(g2[...], level2, level3, buf2), wide, doubled, range(3, 9))

    top = BASE // 2
    planes = g0.shape[0]
    block = planes - 2 * HALO
    aG0, aINV0 = (g0, 0, top), (inv0, 0, BASE)
    w0 = (wx0, 1, BASE), (wy0, 0, BASE), (wz0, 0, BASE)
    w1 = (wx1, 1, BASE), (wy1, 0, BASE), (wz1, 0, BASE)
    low, block1 = HALO // 2, block // 2
    aINV1 = (inv1, 0, BASE)
    aG1N, aV1N = (g1n, 0, BASE - (low - 2)), (v1n, 1, BASE - (low - 2))
    aV0N = (v0n, 1, BASE - (HALO - 5))

    aU1 = (u1, 1, BASE - (low - 2))
    window = (low - 2, block1 + 4, low - 2, block1 + 4)
    e1 = doubled[low // 2 : low // 2 + block1 // 2 + 2, low : low + block1 + 4, :]
    write(aU1, low - 2, low - 2, read(aV1N, *window) + double_planes(e1))
    window = (low - 1, block1 + 2, low - 1, block1 + 2)
    here, around = spread(aU1, w1, window, 2)
    swept = KEEP * here + read(aINV1, *window) * (read(aG1N, *window) + around)
    double_rows(e0, low - 1, swept)

    aU0 = (u0, 1, BASE - (HALO - 1))
    aE0 = (e0, 0, -(2 * low - 2))
    size = (block + 4) // 2
    rows = block + 2

    def correct(i):
        window = (i, size, HALO - 1, rows)
        e = double_planes(read(aE0, i // 2, size // 2, HALO - 1, rows))
        write(aU0, i, HALO - 1, read(aV0N, *window) + e)

    slabs(HALO - 2, planes - HALO + 2, size, correct)

    def sweep(i):
        window = (i, size, HALO, block)
        here, around = spread(aU0, w0, window, 1)
        out[pl.ds(i - HALO, size)] = KEEP * here + read(aINV0, *window) * (read(aG0, *window) + around)

    size = block // 2
    slabs(HALO, planes - HALO, size, sweep)


def kernel_call(body, outs, scratch, args):
    def size(shape):
        total = 4
        for length in shape:
            total *= length
        return total

    shapes = [a.shape for a in args] + list(outs) + list(scratch)
    limit = sum(size(s) for s in shapes) + (8 << 20)
    return pl.pallas_call(
        body,
        out_shape=[jax.ShapeDtypeStruct(s, F32) for s in outs],
        in_specs=[pl.BlockSpec(memory_space=pltpu.VMEM)] * len(args),
        out_specs=[pl.BlockSpec(memory_space=pltpu.VMEM)] * len(outs),
        scratch_shapes=[pltpu.VMEM(s, F32) for s in scratch],
        compiler_params=pltpu.CompilerParams(vmem_limit_bytes=limit),
    )(*args)


def local(right_side, material, conductivity):
    bx, by, bz = right_side.shape
    gx_count, gy_count = lax.axis_size("gx"), lax.axis_size("gy")
    devices = gx_count * gy_count

    X, Y = bx + 2 * HALO, by + 2 * HALO
    YA = Y + BASE
    YB = Y + 2 * BASE
    X1, Y1 = X // 2, -(-Y // 16) * 8 + 2 * BASE
    xb, yb = bx // 4, by // 4

    strip = (bx + bx // 2, NEAR, bz)
    h, k_near, k_far, g_near, g_far = kernel_call(
        start_kernel,
        [(bx, by, bz), (HALO, by, bz), (HALO, by, bz), strip, strip],
        [(8, bz)],
        [right_side, material, conductivity[None]],
    )
    k_near, k_far = trade(k_near, k_far, "gx")
    g_near, g_far = trade(g_near, g_far, "gy")
    first, last = far_planes(X)
    strip = (X + (last - first) // 2, NEAR, bz)
    k_wide, k_near, k_far = kernel_call(
        k_kernel, [(X, by, bz), strip, strip], [], [h, k_near, k_far]
    )
    k_near, k_far = trade(k_near, k_far, "gy")
    strip = (plane_strips(Y)[1], 8, bz)
    g_wide, g_near, g_far = kernel_call(
        g_kernel, [(bx, YA, bz), strip, strip], [], [right_side, g_near, g_far]
    )
    g_near, g_far = trade(g_near, g_far, "gx")

    pad0, full0, pad1, full1 = (X + 2, YB, bz), (X, YB, bz), (X1 + 2, Y1, bz), (X1, Y1, bz)
    packed, g0, wx0, wy0, wz0, inv0, tot0, v0, wx1, wy1, wz1, inv1, v1, g1 = kernel_call(
        first_kernel,
        [(devices, 2 * yb, bz), (X, YA, bz), pad0, full0, full0, full0, full0, pad0]
        + [pad1, full1, full1, full1, pad1, full1],
        [(X + 2, YA, bz), pad1, (X // 4, Y, bz), (xb, 8, bz)],
        [k_wide, k_near, k_far, g_wide, g_near, g_far],
    )
    got = everywhere(packed)
    level2 = (gx_count, gy_count * yb, bz)
    level3 = (gx_count, gy_count * yb // 2, bz)
    coarse_scratch = [
        level2, (gx_count + 2, gy_count * yb + 16, bz), (3 * xb, 32, bz), pad1, (X1, by + 24, bz), pad0,
    ]
    packed, v0n, v1n, g1n, *levels = kernel_call(
        second_kernel,
        [(devices, yb, bz), pad0, pad1, full1] + [level2] * 4 + [level3] * 4,
        [level2, level2] + coarse_scratch + [pad0, (X // 4, Y, bz), (xb, 8, bz)],
        [got, g0, wx0, wy0, wz0, inv0, tot0, v0, wx1, wy1, wz1, inv1, v1, g1],
    )
    got = everywhere(packed)
    (out,) = kernel_call(
        third_kernel,
        [(bx, by, bz)],
        [level2] + coarse_scratch,
        [got, g0, wx0, wy0, wz0, inv0, v0n, wx1, wy1, wz1, inv1, v1n, g1n] + levels,
    )
    return out


def solution(mesh):
    return jax.shard_map(
        local,
        mesh=mesh,
        in_specs=(P("gx", "gy", None), P("gx", "gy", None), P()),
        out_specs=P("gx", "gy", None),
        check_vma=False,
    )
```

time: 67.1 us -> 50.6 us (0.75)
  blocking collectives: 36.6 us -> 22.9 us
  Pallas kernels: 13.3 us -> 8.95 us
  local copies, waits for them, and re-layouts: 0.08 us -> 3.37 us
  starting transfers between devices: 7.34 us -> 10.4 us
  waiting for transfers between devices: 7.22 us -> 4.71 us
  other arithmetic: 2.28 us -> 0 us
    all_to_all x2, blocking collectives: 36.6 us -> 22.9 us  [everywhere(): return lax.all_to_all(copies, ('gx', 'gy'), 0, 0)]
    pallas_call x3 -> x6, Pallas kernels: 13.3 us -> 8.95 us  [kernel_call(): pl.pallas_call(body, out_shape=[jax.ShapeDtypeStruct(s, F32) for s in out...]
    unnamed x4 -> x8, local copies, waits for them, and re-layouts: 0.01 us -> 3.37 us
    ppermute x4 -> x8, starting transfers between devices: 7.34 us -> 10.4 us  [the longest x4 6.71 us: trade(): from_far = lax.ppermute(to_far, ('gx', 'gy'), route(axis, True))]
    ppermute x4 -> x8, waiting for transfers between devices: 7.22 us -> 4.71 us  [the longest x4 4.7 us: trade(): from_far = lax.ppermute(to_far, ('gx', 'gy'), route(axis, True))]
    another operation x2 -> x0, other arithmetic: 1.88 us -> none  [local(): block = jnp.stack([right_side, (material + 1).astype(F32)])]
  transfers between devices with their start and end apart: 4 -> 8, of which waited for: 2 -> 2; matrix products, arithmetic and copies ran while one was open for 0% -> 0% of each run, Pallas kernels for 0% -> 0%
where the time goes in v2:
time: 50.6 us; the launch traced here: 50.4 us
  blocking collectives  22.9 us (45%)
  starting transfers between devices  10.4 us (21%)
  Pallas kernels  8.95 us (18%)
  waiting for transfers between devices  4.71 us (9%)
  local copies, waits for them, and re-layouts  3.37 us (7%)
    all_to_all x2, blocking collectives, everywhere(): return lax.all_to_all(copies, ('gx', 'gy'), 0, 0)  22.9 us
    pallas_call x6, Pallas kernels, kernel_call(): pl.pallas_call(body, out_shape=[jax.ShapeDtypeStruct(s, F32) for s in out...  8.95 us
    ppermute x4, starting transfers between devices, trade(): from_far = lax.ppermute(to_far, ('gx', 'gy'), route(axis, True))  6.71 us
    ppermute x4, waiting for transfers between devices, trade(): from_far = lax.ppermute(to_far, ('gx', 'gy'), route(axis, True))  4.7 us
    ppermute x4, starting transfers between devices, trade(): from_near = lax.ppermute(to_near, ('gx', 'gy'), route(axis, False))  3.65 us
    unnamed x8, local copies, waits for them, and re-layouts  3.37 us
  transfers between devices with their start and end apart: 8, of which 2 were waited for; matrix products, arithmetic and copies ran while one was open for 0% of the time, Pallas kernels for 0%

profile of v2, /device:TPU:0, one launch (start us, length us, event | category | flops | bytes accessed | tf_op | source)
XLA Modules:
  0.0 50.4 jit_solution(5443352041192583836)
XLA Ops:
  0.0 0.0 copy-start
  0.0 0.9 %copy-done = f32[16,16,128]{2,1,0:T(8,128)S(1)} copy-done((f32[16,16,128]{2,1,0:T(8,128)S(1)}, f32[16,16,128]{2,1,0:T(8,128)}, u32[]{:S(2)}) %copy-start) | copy-done | bytes 131096
  0.9 0.0 copy-start.2
  0.9 0.9 %copy-done.2 = s32[16,16,128]{2,1,0:T(8,128)S(1)} copy-done((s32[16,16,128]{2,1,0:T(8,128)S(1)}, s32[16,16,128]{2,1,0:T(8,128)}, u32[]{:S(2)}) %copy-start.2) | copy-done | bytes 131096
  1.8 0.0 copy-start.3
  1.8 0.7 %copy-done.3 = f32[16]{0:T(128)S(1)} copy-done((f32[16]{0:T(128)S(1)}, f32[16]{0:T(128)}, u32[]{:S(2)}) %copy-start.3) | copy-done | bytes 88
  2.5 0.2 shard_map.37
  2.7 0.5 collective-permute-start
  3.2 2.7 %collective-permute-start.1 = (f32[12,16,128]{2,1,0:T(8,128)S(1)}, f32[12,16,128]{2,1,0:T(8,128)S(1)}, u32[]{:S(2)}, u32[]{:S(2)}) collective-permute-start(f32[12,16,128]{2,1,0:T(8,128)S(1)} %get-tuple-element.44), channel_id=1, source_target_pairs={{0,1},{1,0},{2,3},{3,2},{4,8},{5,9},{6,10},{7,11},{8,4},{9,5},{10,... | collective-permute-start | bytes 294920 | tf_op jit(solution)/shard_map/ppermute | solution.py:50
  5.8 0.1 collective-permute-start.4
  5.9 1.2 %collective-permute-start.5 = (f32[24,8,128]{2,1,0:T(8,128)S(1)}, f32[24,8,128]{2,1,0:T(8,128)S(1)}, u32[]{:S(2)}, u32[]{:S(2)}) collective-permute-start(f32[24,8,128]{2,1,0:T(8,128)S(1)} %get-tuple-element.49), channel_id=1, source_target_pairs={{0,4},{1,2},{2,1},{3,7},{4,0},{5,6},{6,5},{7,3},{8,12},{9,10},{10,... | collective-permute-start | bytes 294920 | tf_op jit(solution)/shard_map/ppermute | solution.py:50
  7.2 0.0 collective-permute-done.near
  7.2 1.3 %collective-permute-done.1.far = f32[12,16,128]{2,1,0:T(8,128)S(1)} collective-permute-done((f32[12,16,128]{2,1,0:T(8,128)S(1)}, f32[12,16,128]{2,1,0:T(8,128)S(1)}, u32[]{:S(2)}, u32[]{:S(2)}) %collective-permute-start.1) | collective-permute-done | bytes 98336 | tf_op jit(solution)/shard_map/ppermute | solution.py:50
  8.4 0.1 shard_map.38
  8.5 2.6 %collective-permute-start.2 = (f32[51,8,128]{2,1,0:T(8,128)S(1)}, f32[51,8,128]{2,1,0:T(8,128)S(1)}, u32[]{:S(2)}, u32[]{:S(2)}) collective-permute-start(f32[51,8,128]{2,1,0:T(8,128)S(1)} %get-tuple-element.46), channel_id=1, source_target_pairs={{0,1},{1,0},{2,3},{3,2},{4,5},{5,4},{6,7},{7,6},{8,9},{9,8},{10,11... | collective-permute-start | bytes 626696 | tf_op jit(solution)/shard_map/ppermute | solution.py:51
  11.1 0.1 collective-permute-start.3
  11.2 0.0 collective-permute-done.4.near
  11.2 0.0 collective-permute-done.5.far
  11.2 0.0 copy-start.1
  11.2 0.9 %copy-done.1 = f32[16,16,128]{2,1,0:T(8,128)S(1)} copy-done((f32[16,16,128]{2,1,0:T(8,128)S(1)}, f32[16,16,128]{2,1,0:T(8,128)}, u32[]{:S(2)}) %copy-start.1) | copy-done | bytes 131096
  12.1 0.1 shard_map.39
  12.2 0.5 collective-permute-start.6
  12.7 2.7 %collective-permute-start.7 = (f32[43,8,128]{2,1,0:T(8,128)S(1)}, f32[43,8,128]{2,1,0:T(8,128)S(1)}, u32[]{:S(2)}, u32[]{:S(2)}) collective-permute-start(f32[43,8,128]{2,1,0:T(8,128)S(1)} %get-tuple-element.52), channel_id=1, source_target_pairs={{0,1},{1,0},{2,3},{3,2},{4,8},{5,9},{6,10},{7,11},{8,4},{9,5},{10,... | collective-permute-start | bytes 528392 | tf_op jit(solution)/shard_map/ppermute | solution.py:50
  15.4 0.0 collective-permute-done.6.g_near
  15.4 3.4 %collective-permute-done.7.g_far = f32[43,8,128]{2,1,0:T(8,128)S(1)} collective-permute-done((f32[43,8,128]{2,1,0:T(8,128)S(1)}, f32[43,8,128]{2,1,0:T(8,128)S(1)}, u32[]{:S(2)}, u32[]{:S(2)}) %collective-permute-start.7) | collective-permute-done | bytes 176160 | tf_op jit(solution)/shard_map/ppermute | solution.py:50
  18.8 0.0 collective-permute-done.2.k_near
  18.8 0.0 collective-permute-done.3.k_far
  18.8 2.8 %shard_map.40 = (f32[32,8,128]{2,1,0:T(8,128)S(1)}, f32[40,48,128]{2,1,0:T(8,128)S(1)}, f32[42,56,128]{2,1,0:T(8,128)S(1)}, f32[40,56,128]{2,1,0:T(8,128)S(1)}, ...) custom-call(f32[40,16,128]{2,1,0:T(8,128)S(1)} %get-tuple-element.45, ...), custom_call_target="tpu_custom_call" | custom-call | tf_op jit(solution)/shard_map/pallas_call | solution.py:581
  21.6 13.7 %all_to_all.10.got = f32[32,8,128]{2,1,0:T(8,128)S(1)} all-to-all(f32[32,8,128]{2,1,0:T(8,128)S(1)} %get-tuple-element.53), channel_id=1, replica_groups=mesh['gx'=8,'gy'=4] {'gx','gy'}, dimensions={0} | all-to-all | bytes 262144 | tf_op jit(solution)/shard_map/all_to_all | solution.py:56
  35.4 3.7 %shard_map.41 = (f32[32,4,128]{2,1,0:T(4,128)S(1)}, f32[42,56,128]{2,1,0:T(8,128)S(1)}, f32[22,40,128]{2,1,0:T(8,128)S(1)}, f32[20,40,128]{2,1,0:T(8,128)S(1)}, ...) custom-call(f32[32,8,128]{2,1,0:T(8,128)S(1)} %all_to_all.10.got, ...), custom_call_target="tpu_custom_call" | custom-call | tf_op jit(solution)/shard_map/pallas_call | solution.py:581
  39.1 9.2 %all_to_all.11.got = f32[32,4,128]{2,1,0:T(4,128)S(1)} all-to-all(f32[32,4,128]{2,1,0:T(4,128)S(1)} %get-tuple-element.67), channel_id=1, replica_groups=mesh['gx'=8,'gy'=4] {'gx','gy'}, dimensions={0} | all-to-all | bytes 131072 | tf_op jit(solution)/shard_map/all_to_all | solution.py:56
  48.3 2.1 %shard_map.42 = f32[16,16,128]{2,1,0:T(8,128)} custom-call(f32[32,4,128]{2,1,0:T(4,128)S(1)} %all_to_all.11.got, f32[40,48,128]{2,1,0:T(8,128)S(1)} %get-tuple-element.54.g0, f32[42,56,128]{2,1,0:T(8,128)S(1)} %get-tuple-element.55.wx0, f32[40,56,128]{2,1,0:T(8,128)S(1)} %get-tuple-element.56.wy0, f32[40,56,128]{2,1,0:T(8,128)S(1)} %get-tuple-element.57.wz0, ...), custom_call_target="tpu_custom_call" | custom-call | tf_op jit(solution)/shard_map/pallas_call | solution.py:581
Async XLA Ops:
  0.0 0.9 %copy-start = (f32[16,16,128]{2,1,0:T(8,128)S(1)}, f32[16,16,128]{2,1,0:T(8,128)}, u32[]{:S(2)}) copy-start(f32[16,16,128]{2,1,0:T(8,128)} %right.3) | copy-start | bytes 393220
  0.9 0.9 %copy-start.2 = (s32[16,16,128]{2,1,0:T(8,128)S(1)}, s32[16,16,128]{2,1,0:T(8,128)}, u32[]{:S(2)}) copy-start(s32[16,16,128]{2,1,0:T(8,128)} %material.1) | copy-start | bytes 393220
  1.8 0.7 %copy-start.3 = (f32[16]{0:T(128)S(1)}, f32[16]{0:T(128)}, u32[]{:S(2)}) copy-start(f32[16]{0:T(128)} %param.5) | copy-start | bytes 196
  2.7 4.5 %collective-permute-start = (f32[12,16,128]{2,1,0:T(8,128)S(1)}, f32[12,16,128]{2,1,0:T(8,128)S(1)}, u32[]{:S(2)}, u32[]{:S(2)}) collective-permute-start(f32[12,16,128]{2,1,0:T(8,128)S(1)} %get-tuple-element.43), channel_id=1, source_target_pairs={{0,4},{1,5},{2,6},{3,7},{4,0},{5,1},{6,2},{7,3},{8,12},{9,13},{10,... | collective-permute-start | bytes 294920 | tf_op jit(solution)/shard_map/ppermute | solution.py:51
  3.2 5.3 %collective-permute-start.1 = (f32[12,16,128]{2,1,0:T(8,128)S(1)}, f32[12,16,128]{2,1,0:T(8,128)S(1)}, u32[]{:S(2)}, u32[]{:S(2)}) collective-permute-start(f32[12,16,128]{2,1,0:T(8,128)S(1)} %get-tuple-element.44), channel_id=1, source_target_pairs={{0,1},{1,0},{2,3},{3,2},{4,8},{5,9},{6,10},{7,11},{8,4},{9,5},{10,... | collective-permute-start | bytes 294920 | tf_op jit(solution)/shard_map/ppermute | solution.py:50
  5.8 5.4 %collective-permute-start.4 = (f32[24,8,128]{2,1,0:T(8,128)S(1)}, f32[24,8,128]{2,1,0:T(8,128)S(1)}, u32[]{:S(2)}, u32[]{:S(2)}) collective-permute-start(f32[24,8,128]{2,1,0:T(8,128)S(1)} %get-tuple-element.48), channel_id=1, source_target_pairs={{0,1},{1,0},{2,3},{3,2},{4,5},{5,4},{6,7},{7,6},{8,9},{9,8},{10,11... | collective-permute-start | bytes 294920 | tf_op jit(solution)/shard_map/ppermute | solution.py:51
  5.9 5.3 %collective-permute-start.5 = (f32[24,8,128]{2,1,0:T(8,128)S(1)}, f32[24,8,128]{2,1,0:T(8,128)S(1)}, u32[]{:S(2)}, u32[]{:S(2)}) collective-permute-start(f32[24,8,128]{2,1,0:T(8,128)S(1)} %get-tuple-element.49), channel_id=1, source_target_pairs={{0,4},{1,2},{2,1},{3,7},{4,0},{5,6},{6,5},{7,3},{8,12},{9,10},{10,... | collective-permute-start | bytes 294920 | tf_op jit(solution)/shard_map/ppermute | solution.py:50
  8.5 10.3 %collective-permute-start.2 = (f32[51,8,128]{2,1,0:T(8,128)S(1)}, f32[51,8,128]{2,1,0:T(8,128)S(1)}, u32[]{:S(2)}, u32[]{:S(2)}) collective-permute-start(f32[51,8,128]{2,1,0:T(8,128)S(1)} %get-tuple-element.46), channel_id=1, source_target_pairs={{0,1},{1,0},{2,3},{3,2},{4,5},{5,4},{6,7},{7,6},{8,9},{9,8},{10,11... | collective-permute-start | bytes 626696 | tf_op jit(solution)/shard_map/ppermute | solution.py:51
  11.1 7.7 %collective-permute-start.3 = (f32[51,8,128]{2,1,0:T(8,128)S(1)}, f32[51,8,128]{2,1,0:T(8,128)S(1)}, u32[]{:S(2)}, u32[]{:S(2)}) collective-permute-start(f32[51,8,128]{2,1,0:T(8,128)S(1)} %get-tuple-element.47), channel_id=1, source_target_pairs={{0,4},{1,2},{2,1},{3,7},{4,0},{5,6},{6,5},{7,3},{8,12},{9,10},{10,... | collective-permute-start | bytes 626696 | tf_op jit(solution)/shard_map/ppermute | solution.py:50
  11.2 0.9 %copy-start.1 = (f32[16,16,128]{2,1,0:T(8,128)S(1)}, f32[16,16,128]{2,1,0:T(8,128)}, u32[]{:S(2)}) copy-start(f32[16,16,128]{2,1,0:T(8,128)} %right.3) | copy-start | bytes 393220
  12.2 3.2 %collective-permute-start.6 = (f32[43,8,128]{2,1,0:T(8,128)S(1)}, f32[43,8,128]{2,1,0:T(8,128)S(1)}, u32[]{:S(2)}, u32[]{:S(2)}) collective-permute-start(f32[43,8,128]{2,1,0:T(8,128)S(1)} %get-tuple-element.51), channel_id=1, source_target_pairs={{0,4},{1,5},{2,6},{3,7},{4,0},{5,1},{6,2},{7,3},{8,12},{9,13},{10,... | collective-permute-start | bytes 528392 | tf_op jit(solution)/shard_map/ppermute | solution.py:51
  12.7 6.2 %collective-permute-start.7 = (f32[43,8,128]{2,1,0:T(8,128)S(1)}, f32[43,8,128]{2,1,0:T(8,128)S(1)}, u32[]{:S(2)}, u32[]{:S(2)}) collective-permute-start(f32[43,8,128]{2,1,0:T(8,128)S(1)} %get-tuple-element.52), channel_id=1, source_target_pairs={{0,1},{1,0},{2,3},{3,2},{4,8},{5,9},{6,10},{7,11},{8,4},{9,5},{10,... | collective-permute-start | bytes 528392 | tf_op jit(solution)/shard_map/ppermute | solution.py:50

commit v3 on v2

--- a/solution.py
+++ b/solution.py
@@ -13,6 +13,7 @@
 FAR = HALO - NEAR
 BASE = 8
 F32 = jnp.float32
+START_LIMIT = int(53.25 * 2**20)
 
 
 def near_partner(index, count):
@@ -199,9 +200,13 @@
     )
 
 
+def halve_planes(value):
+    pairs = value.reshape((value.shape[0] // 2, 2) + value.shape[1:])
+    return pairs[:, 0] + pairs[:, 1]
+
+
 def sum_blocks(value, buffer, step):
-    pairs = value.reshape((value.shape[0] // 2, 2) + value.shape[1:])
-    return add_partner(halve_rows(pairs[:, 0] + pairs[:, 1], buffer), step)
+    return add_partner(halve_rows(halve_planes(value), buffer), step)
 
 
 def double_rows(ref, start, value):
@@ -230,11 +235,12 @@
 
 
 def send_to_all(packed, chunk):
-    def copy_out(i, carry):
-        packed[i] = chunk
-        return carry
-
-    lax.fori_loop(0, packed.shape[0], copy_out, 0)
+    copies = min(packed.shape[0], 32)
+
+    def copy_out(i):
+        packed[pl.ds(i, copies)] = jnp.broadcast_to(chunk[None], (copies,) + chunk.shape)
+
+    slabs(0, packed.shape[0], copies, copy_out)
 
 
 def coarse_cycle(g2, level2, level3, buffer):
@@ -298,18 +304,28 @@
         target[planes_off + first + half : planes_off + last, edge : edge + FAR, :] = strips[:, FAR:NEAR]
 
 
-def start_kernel(right, material, cond, h, k_near, k_far, g_near, g_far, table):
-    planes, rows, width = material.shape
+def start_kernel(
+    right_hbm, material_hbm, cond, h, right, k_near, k_far, g_near, g_far, material, table, arrived,
+):
+    planes, rows, width = h.shape
+    copies = [
+        pltpu.make_async_copy(right_hbm, right, arrived.at[0]),
+        pltpu.make_async_copy(material_hbm, material, arrived.at[1]),
+    ]
+    for copy in copies:
+        copy.start()
     table[0:1, 0 : cond.shape[1]] = cond[...]
+    copies[0].wait()
+    to_near, to_far = row_starts("gy", rows)
+    pack_rows(right, to_near, 0, planes, g_near)
+    pack_rows(right, to_far, 0, planes, g_far)
+    copies[1].wait()
     which = material[...].reshape(planes * rows, width)
     values = jnp.broadcast_to(0.5 * table[0:1, :], which.shape)
-    h[...] = jnp.take_along_axis(values, which, axis=1).reshape(material.shape)
+    h[...] = jnp.take_along_axis(values, which, axis=1).reshape(planes, rows, width)
     odd = is_odd("gx")
     k_near[...] = h[pl.ds(jnp.where(odd, 0, planes - HALO), HALO)]
     k_far[...] = h[pl.ds(jnp.where(odd, planes - HALO, 0), HALO)]
-    to_near, to_far = row_starts("gy", rows)
-    pack_rows(right, to_near, 0, planes, g_near)
-    pack_rows(right, to_far, 0, planes, g_far)
 
 
 def far_planes(planes):
@@ -375,7 +391,7 @@
     aWY0, aWZ0, aINV0, aTOT0 = ((ref, 0, BASE) for ref in (wy0, wz0, inv0, tot0))
     aH1, aWX1, aV1 = (h1, 1, BASE), (wx1, 1, BASE), (v1, 1, BASE)
     aWY1, aWZ1, aINV1, aG1 = ((ref, 0, BASE) for ref in (wy1, wz1, inv1, g1))
-    size = planes // 4
+    size = planes
 
     def faces0(i):
         window = (i, size, 0, rows)
@@ -386,16 +402,18 @@
         write(aTOT0, i, 0, total)
         write(aINV0, i, 0, inverse)
         write(aV0, i, 0, inverse * read(aG0, *window))
-        write(aH1, i // 2, 0, sum_blocks(here, buf0, 1) * (1.0 / 32.0))
 
     slabs(0, planes, size, faces0)
+    write(aH1, 0, 0, sum_blocks(read(aH0, 0, planes, 0, rows), buf0, 1) * (1.0 / 32.0))
 
     def resid0(i):
         window = (i, size, 0, rows)
         _, around = spread(aV0, (aWX0, aWY0, aWZ0), window, 1)
-        write(aG1, i // 2, 0, sum_blocks(KEEP * read(aG0, *window) + around, buf0, 1) * 0.125)
+        buf0[pl.ds(i // 2, size // 2)] = halve_planes(KEEP * read(aG0, *window) + around)
 
     slabs(0, planes, size, resid0)
+    r = buf0[:, pl.ds(0, rows // 2, stride=2), :] + buf0[:, pl.ds(1, rows // 2, stride=2), :]
+    write(aG1, 0, 0, add_partner(r, 1) * 0.125)
 
     planes1, rows1 = planes // 2, -(-rows // 16) * 8
 
@@ -469,7 +487,7 @@
     aE0 = (e0, 0, -(2 * low - 8))
     aV0M = (v0m, 1, BASE - (HALO - 6))
     aV0N = (v0n, 1, BASE - (HALO - 5))
-    size = (block + 16) // 4
+    size = block + 16
 
     def correct(i):
         window = (i, size, HALO - 7, rows)
@@ -487,19 +505,14 @@
 
         slabs(HALO - margin, planes - HALO + margin, size, body)
 
-    sweep(aU0, aV0M, 6, (block + 12) // 2)
-    sweep(aV0M, aV0N, 5, (block + 10) // 2)
+    sweep(aU0, aV0M, 6, block + 12)
+    sweep(aV0M, aV0N, 5, block + 10)
 
     aG1N, aV1N = (g1n, 0, BASE - (low - 2)), (v1n, 1, BASE - (low - 2))
-    size = (block + 8) // 2
-
-    def resid(i):
-        window = (i, size, HALO - 4, block + 8)
-        here, around = spread(aV0N, w0, window, 1)
-        r = (read(aG0, *window) - read(aTOT0, *window) * here) + around
-        write(aG1N, i // 2, low - 2, sum_blocks(r, buf0, 1) * 0.125)
-
-    slabs(HALO - 4, planes - HALO + 4, size, resid)
+    window = (HALO - 4, block + 8, HALO - 4, block + 8)
+    here, around = spread(aV0N, w0, window, 1)
+    r = (read(aG0, *window) - read(aTOT0, *window) * here) + around
+    write(aG1N, low - 2, low - 2, sum_blocks(r, buf0, 1) * 0.125)
 
     window = (low - 2, block1 + 4, low - 2, block1 + 4)
     write(aV1N, low - 2, low - 2, read(aINV1, *window) * read(aG1N, *window))
@@ -550,7 +563,7 @@
 
     aU0 = (u0, 1, BASE - (HALO - 1))
     aE0 = (e0, 0, -(2 * low - 2))
-    size = (block + 4) // 2
+    size = block + 4
     rows = block + 2
 
     def correct(i):
@@ -565,7 +578,7 @@
         here, around = spread(aU0, w0, window, 1)
         out[pl.ds(i - HALO, size)] = KEEP * here + read(aINV0, *window) * (read(aG0, *window) + around)
 
-    size = block // 2
+    size = block
     slabs(HALO, planes - HALO, size, sweep)
 
 
@@ -600,32 +613,39 @@
     xb, yb = bx // 4, by // 4
 
     strip = (bx + bx // 2, NEAR, bz)
-    h, k_near, k_far, g_near, g_far = kernel_call(
+    outs = [(bx, by, bz), (bx, by, bz), (HALO, by, bz), (HALO, by, bz), strip, strip]
+    h, right, k_near, k_far, g_near, g_far = pl.pallas_call(
         start_kernel,
-        [(bx, by, bz), (HALO, by, bz), (HALO, by, bz), strip, strip],
-        [(8, bz)],
-        [right_side, material, conductivity[None]],
-    )
+        out_shape=[jax.ShapeDtypeStruct(s, F32) for s in outs],
+        in_specs=[pl.BlockSpec(memory_space=pl.ANY)] * 2 + [pl.BlockSpec(memory_space=pltpu.VMEM)],
+        out_specs=[pl.BlockSpec(memory_space=pltpu.VMEM)] * len(outs),
+        scratch_shapes=[
+            pltpu.VMEM((bx, by, bz), jnp.int32),
+            pltpu.VMEM((8, bz), F32),
+            pltpu.SemaphoreType.DMA((2,)),
+        ],
+        compiler_params=pltpu.CompilerParams(vmem_limit_bytes=START_LIMIT),
+    )(right_side, material, conductivity[None])
     k_near, k_far = trade(k_near, k_far, "gx")
     g_near, g_far = trade(g_near, g_far, "gy")
+    strip = (plane_strips(Y)[1], 8, bz)
+    g_wide, g_near, g_far = kernel_call(
+        g_kernel, [(bx, YA, bz), strip, strip], [], [right, g_near, g_far]
+    )
     first, last = far_planes(X)
     strip = (X + (last - first) // 2, NEAR, bz)
     k_wide, k_near, k_far = kernel_call(
         k_kernel, [(X, by, bz), strip, strip], [], [h, k_near, k_far]
     )
+    g_near, g_far = trade(g_near, g_far, "gx")
     k_near, k_far = trade(k_near, k_far, "gy")
-    strip = (plane_strips(Y)[1], 8, bz)
-    g_wide, g_near, g_far = kernel_call(
-        g_kernel, [(bx, YA, bz), strip, strip], [], [right_side, g_near, g_far]
-    )
-    g_near, g_far = trade(g_near, g_far, "gx")
 
     pad0, full0, pad1, full1 = (X + 2, YB, bz), (X, YB, bz), (X1 + 2, Y1, bz), (X1, Y1, bz)
     packed, g0, wx0, wy0, wz0, inv0, tot0, v0, wx1, wy1, wz1, inv1, v1, g1 = kernel_call(
         first_kernel,
         [(devices, 2 * yb, bz), (X, YA, bz), pad0, full0, full0, full0, full0, pad0]
         + [pad1, full1, full1, full1, pad1, full1],
-        [(X + 2, YA, bz), pad1, (X // 4, Y, bz), (xb, 8, bz)],
+        [(X + 2, YA, bz), pad1, (X1, Y, bz), (xb, 8, bz)],
         [k_wide, k_near, k_far, g_wide, g_near, g_far],
     )
     got = everywhere(packed)
@@ -637,7 +657,7 @@
     packed, v0n, v1n, g1n, *levels = kernel_call(
         second_kernel,
         [(devices, yb, bz), pad0, pad1, full1] + [level2] * 4 + [level3] * 4,
-        [level2, level2] + coarse_scratch + [pad0, (X // 4, Y, bz), (xb, 8, bz)],
+        [level2, level2] + coarse_scratch + [pad0, (X1, Y, bz), (xb, 8, bz)],
         [got, g0, wx0, wy0, wz0, inv0, tot0, v0, wx1, wy1, wz1, inv1, v1, g1],
     )
     got = everywhere(packed)

time: 50.6 us -> 47.3 us (0.935)
  local copies, waits for them, and re-layouts: 3.37 us -> 0.65 us
  waiting for transfers between devices: 4.71 us -> 5.49 us
  blocking collectives: 22.9 us -> 22.2 us
  Pallas kernels: 8.95 us -> 8.43 us
    unnamed x8 -> x2, local copies, waits for them, and re-layouts: 3.37 us -> 0.65 us
    pallas_call x6 -> x5, Pallas kernels: 8.95 us -> 7.25 us  [kernel_call(): pl.pallas_call(body, out_shape=[jax.ShapeDtypeStruct(s, F32) for s in out...]
    pallas_call x0 -> x1, Pallas kernels: none -> 1.19 us  [local(): pl.pallas_call(start_kernel, out_shape=[jax.ShapeDtypeStruct(s, F32) for...]
    ppermute x4, waiting for transfers between devices: 4.7 us -> 5.47 us  [trade(): from_far = lax.ppermute(to_far, ('gx', 'gy'), route(axis, True))]
    all_to_all x2, blocking collectives: 22.9 us -> 22.2 us  [everywhere(): return lax.all_to_all(copies, ('gx', 'gy'), 0, 0)]
where the time goes in v3:
time: 47.3 us; the launch traced here: 47.1 us
  blocking collectives  22.2 us (47%)
  starting transfers between devices  10.4 us (22%)
  Pallas kernels  8.43 us (18%)
  waiting for transfers between devices  5.49 us (12%)
  local copies, waits for them, and re-layouts  0.65 us (1%)
    all_to_all x2, blocking collectives, everywhere(): return lax.all_to_all(copies, ('gx', 'gy'), 0, 0)  22.2 us
    pallas_call x5, Pallas kernels, kernel_call(): pl.pallas_call(body, out_shape=[jax.ShapeDtypeStruct(s, F32) for s in out...  7.25 us
    ppermute x4, starting transfers between devices, trade(): from_far = lax.ppermute(to_far, ('gx', 'gy'), route(axis, True))  6.71 us
    ppermute x4, waiting for transfers between devices, trade(): from_far = lax.ppermute(to_far, ('gx', 'gy'), route(axis, True))  5.47 us
    ppermute x4, starting transfers between devices, trade(): from_near = lax.ppermute(to_near, ('gx', 'gy'), route(axis, False))  3.66 us
    pallas_call x1, Pallas kernels, local(): pl.pallas_call(start_kernel, out_shape=[jax.ShapeDtypeStruct(s, F32) for...  1.19 us
  transfers between devices with their start and end apart: 8, of which 2 were waited for; matrix products, arithmetic and copies ran while one was open for 0% of the time, Pallas kernels for 0%

profile of v3, /device:TPU:0, one launch (start us, length us, event | category | flops | bytes accessed | tf_op | source)
XLA Modules:
  0.0 47.1 jit_solution(11105038864804795425)
XLA Ops:
  0.0 0.0 copy-start
  0.0 0.7 %copy-done = f32[16]{0:T(128)S(1)} copy-done((f32[16]{0:T(128)S(1)}, f32[16]{0:T(128)}, u32[]{:S(2)}) %copy-start) | copy-done | bytes 88
  0.7 1.2 %shard_map.37 = (f32[16,16,128]{2,1,0:T(8,128)S(1)}, f32[16,16,128]{2,1,0:T(8,128)S(1)}, f32[12,16,128]{2,1,0:T(8,128)S(1)}, f32[12,16,128]{2,1,0:T(8,128)S(1)},...) custom-call(f32[16,16,128]{2,1,0:T(8,128)} %right_hbm.1, s32[16,16,128]{2,1,0:T(8,128)} %material_hbm.1, ...), custom_call_target="tpu_custom_call" | custom-call | tf_op jit(solution)/shard_map/pallas_call | solution.py:617
  1.9 0.5 %collective-permute-start = (f32[12,16,128]{2,1,0:T(8,128)S(1)}, f32[12,16,128]{2,1,0:T(8,128)S(1)}, u32[]{:S(2)}, u32[]{:S(2)}) collective-permute-start(f32[12,16,128]{2,1,0:T(8,128)S(1)} %get-tuple-element.44), channel_id=1, source_target_pairs={{0,4},{1,5},{2,6},{3,7},{4,0},{5,1},{6,2},{7,3},{8,12},{9,13},{10,... | collective-permute-start | bytes 294920 | tf_op jit(solution)/shard_map/ppermute | solution.py:52
  2.4 2.7 %collective-permute-start.1 = (f32[12,16,128]{2,1,0:T(8,128)S(1)}, f32[12,16,128]{2,1,0:T(8,128)S(1)}, u32[]{:S(2)}, u32[]{:S(2)}) collective-permute-start(f32[12,16,128]{2,1,0:T(8,128)S(1)} %get-tuple-element.45), channel_id=1, source_target_pairs={{0,1},{1,0},{2,3},{3,2},{4,8},{5,9},{6,10},{7,11},{8,4},{9,5},{10,... | collective-permute-start | bytes 294920 | tf_op jit(solution)/shard_map/ppermute | solution.py:51
  5.0 0.1 collective-permute-start.4
  5.1 1.2 %collective-permute-start.5 = (f32[24,8,128]{2,1,0:T(8,128)S(1)}, f32[24,8,128]{2,1,0:T(8,128)S(1)}, u32[]{:S(2)}, u32[]{:S(2)}) collective-permute-start(f32[24,8,128]{2,1,0:T(8,128)S(1)} %get-tuple-element.51), channel_id=1, source_target_pairs={{0,4},{1,2},{2,1},{3,7},{4,0},{5,6},{6,5},{7,3},{8,12},{9,10},{10,... | collective-permute-start | bytes 294920 | tf_op jit(solution)/shard_map/ppermute | solution.py:51
  6.3 0.0 collective-permute-done.near
  6.4 1.3 %collective-permute-done.1.far = f32[12,16,128]{2,1,0:T(8,128)S(1)} collective-permute-done((f32[12,16,128]{2,1,0:T(8,128)S(1)}, f32[12,16,128]{2,1,0:T(8,128)S(1)}, u32[]{:S(2)}, u32[]{:S(2)}) %collective-permute-start.1) | collective-permute-done | bytes 98336 | tf_op jit(solution)/shard_map/ppermute | solution.py:51
  7.6 0.1 shard_map.38
  7.7 2.6 %collective-permute-start.2 = (f32[51,8,128]{2,1,0:T(8,128)S(1)}, f32[51,8,128]{2,1,0:T(8,128)S(1)}, u32[]{:S(2)}, u32[]{:S(2)}) collective-permute-start(f32[51,8,128]{2,1,0:T(8,128)S(1)} %get-tuple-element.47), channel_id=1, source_target_pairs={{0,1},{1,0},{2,3},{3,2},{4,5},{5,4},{6,7},{7,6},{8,9},{9,8},{10,11... | collective-permute-start | bytes 626696 | tf_op jit(solution)/shard_map/ppermute | solution.py:52
  10.3 0.1 collective-permute-start.3
  10.4 0.0 collective-permute-done.4.near
  10.4 0.0 collective-permute-done.5.far
  10.4 0.1 shard_map.39
  10.4 0.5 %collective-permute-start.6 = (f32[43,8,128]{2,1,0:T(8,128)S(1)}, f32[43,8,128]{2,1,0:T(8,128)S(1)}, u32[]{:S(2)}, u32[]{:S(2)}) collective-permute-start(f32[43,8,128]{2,1,0:T(8,128)S(1)} %get-tuple-element.53), channel_id=1, source_target_pairs={{0,4},{1,5},{2,6},{3,7},{4,0},{5,1},{6,2},{7,3},{8,12},{9,13},{10,... | collective-permute-start | bytes 528392 | tf_op jit(solution)/shard_map/ppermute | solution.py:52
  10.9 2.7 %collective-permute-start.7 = (f32[43,8,128]{2,1,0:T(8,128)S(1)}, f32[43,8,128]{2,1,0:T(8,128)S(1)}, u32[]{:S(2)}, u32[]{:S(2)}) collective-permute-start(f32[43,8,128]{2,1,0:T(8,128)S(1)} %get-tuple-element.54), channel_id=1, source_target_pairs={{0,1},{1,0},{2,3},{3,2},{4,8},{5,9},{6,10},{7,11},{8,4},{9,5},{10,... | collective-permute-start | bytes 528392 | tf_op jit(solution)/shard_map/ppermute | solution.py:51
  13.7 0.0 collective-permute-done.6.g_near
  13.7 4.2 %collective-permute-done.7.g_far = f32[43,8,128]{2,1,0:T(8,128)S(1)} collective-permute-done((f32[43,8,128]{2,1,0:T(8,128)S(1)}, f32[43,8,128]{2,1,0:T(8,128)S(1)}, u32[]{:S(2)}, u32[]{:S(2)}) %collective-permute-start.7) | collective-permute-done | bytes 176160 | tf_op jit(solution)/shard_map/ppermute | solution.py:51
  17.9 0.0 collective-permute-done.2.k_near
  17.9 0.0 collective-permute-done.3.k_far
  17.9 2.0 %shard_map.40 = (f32[32,8,128]{2,1,0:T(8,128)S(1)}, f32[40,48,128]{2,1,0:T(8,128)S(1)}, f32[42,56,128]{2,1,0:T(8,128)S(1)}, f32[40,56,128]{2,1,0:T(8,128)S(1)}, ...) custom-call(f32[40,16,128]{2,1,0:T(8,128)S(1)} %get-tuple-element.46, ...), custom_call_target="tpu_custom_call" | custom-call | tf_op jit(solution)/shard_map/pallas_call | solution.py:594
  19.9 13.0 %all_to_all.10.got = f32[32,8,128]{2,1,0:T(8,128)S(1)} all-to-all(f32[32,8,128]{2,1,0:T(8,128)S(1)} %get-tuple-element.55), channel_id=1, replica_groups=mesh['gx'=8,'gy'=4] {'gx','gy'}, dimensions={0} | all-to-all | bytes 262144 | tf_op jit(solution)/shard_map/all_to_all | solution.py:57
  32.8 3.1 %shard_map.41 = (f32[32,4,128]{2,1,0:T(4,128)S(1)}, f32[42,56,128]{2,1,0:T(8,128)S(1)}, f32[22,40,128]{2,1,0:T(8,128)S(1)}, f32[20,40,128]{2,1,0:T(8,128)S(1)}, ...) custom-call(f32[32,8,128]{2,1,0:T(8,128)S(1)} %all_to_all.10.got, ...), custom_call_target="tpu_custom_call" | custom-call | tf_op jit(solution)/shard_map/pallas_call | solution.py:594
  36.0 9.2 %all_to_all.11.got = f32[32,4,128]{2,1,0:T(4,128)S(1)} all-to-all(f32[32,4,128]{2,1,0:T(4,128)S(1)} %get-tuple-element.69), channel_id=1, replica_groups=mesh['gx'=8,'gy'=4] {'gx','gy'}, dimensions={0} | all-to-all | bytes 131072 | tf_op jit(solution)/shard_map/all_to_all | solution.py:57
  45.1 2.0 %shard_map.42 = f32[16,16,128]{2,1,0:T(8,128)} custom-call(f32[32,4,128]{2,1,0:T(4,128)S(1)} %all_to_all.11.got, f32[40,48,128]{2,1,0:T(8,128)S(1)} %get-tuple-element.56.g0, f32[42,56,128]{2,1,0:T(8,128)S(1)} %get-tuple-element.57.wx0, f32[40,56,128]{2,1,0:T(8,128)S(1)} %get-tuple-element.58.wy0, f32[40,56,128]{2,1,0:T(8,128)S(1)} %get-tuple-element.59.wz0, ...), custom_call_target="tpu_custom_call" | custom-call | tf_op jit(solution)/shard_map/pallas_call | solution.py:594
Async XLA Ops:
  0.0 0.7 %copy-start = (f32[16]{0:T(128)S(1)}, f32[16]{0:T(128)}, u32[]{:S(2)}) copy-start(f32[16]{0:T(128)} %param.5) | copy-start | bytes 196
  1.9 4.5 %collective-permute-start = (f32[12,16,128]{2,1,0:T(8,128)S(1)}, f32[12,16,128]{2,1,0:T(8,128)S(1)}, u32[]{:S(2)}, u32[]{:S(2)}) collective-permute-start(f32[12,16,128]{2,1,0:T(8,128)S(1)} %get-tuple-element.44), channel_id=1, source_target_pairs={{0,4},{1,5},{2,6},{3,7},{4,0},{5,1},{6,2},{7,3},{8,12},{9,13},{10,... | collective-permute-start | bytes 294920 | tf_op jit(solution)/shard_map/ppermute | solution.py:52
  2.4 5.3 %collective-permute-start.1 = (f32[12,16,128]{2,1,0:T(8,128)S(1)}, f32[12,16,128]{2,1,0:T(8,128)S(1)}, u32[]{:S(2)}, u32[]{:S(2)}) collective-permute-start(f32[12,16,128]{2,1,0:T(8,128)S(1)} %get-tuple-element.45), channel_id=1, source_target_pairs={{0,1},{1,0},{2,3},{3,2},{4,8},{5,9},{6,10},{7,11},{8,4},{9,5},{10,... | collective-permute-start | bytes 294920 | tf_op jit(solution)/shard_map/ppermute | solution.py:51
  5.0 5.4 %collective-permute-start.4 = (f32[24,8,128]{2,1,0:T(8,128)S(1)}, f32[24,8,128]{2,1,0:T(8,128)S(1)}, u32[]{:S(2)}, u32[]{:S(2)}) collective-permute-start(f32[24,8,128]{2,1,0:T(8,128)S(1)} %get-tuple-element.50), channel_id=1, source_target_pairs={{0,1},{1,0},{2,3},{3,2},{4,5},{5,4},{6,7},{7,6},{8,9},{9,8},{10,11... | collective-permute-start | bytes 294920 | tf_op jit(solution)/shard_map/ppermute | solution.py:52
  5.1 5.3 %collective-permute-start.5 = (f32[24,8,128]{2,1,0:T(8,128)S(1)}, f32[24,8,128]{2,1,0:T(8,128)S(1)}, u32[]{:S(2)}, u32[]{:S(2)}) collective-permute-start(f32[24,8,128]{2,1,0:T(8,128)S(1)} %get-tuple-element.51), channel_id=1, source_target_pairs={{0,4},{1,2},{2,1},{3,7},{4,0},{5,6},{6,5},{7,3},{8,12},{9,10},{10,... | collective-permute-start | bytes 294920 | tf_op jit(solution)/shard_map/ppermute | solution.py:51
  7.7 10.2 %collective-permute-start.2 = (f32[51,8,128]{2,1,0:T(8,128)S(1)}, f32[51,8,128]{2,1,0:T(8,128)S(1)}, u32[]{:S(2)}, u32[]{:S(2)}) collective-permute-start(f32[51,8,128]{2,1,0:T(8,128)S(1)} %get-tuple-element.47), channel_id=1, source_target_pairs={{0,1},{1,0},{2,3},{3,2},{4,5},{5,4},{6,7},{7,6},{8,9},{9,8},{10,11... | collective-permute-start | bytes 626696 | tf_op jit(solution)/shard_map/ppermute | solution.py:52
  10.3 7.6 %collective-permute-start.3 = (f32[51,8,128]{2,1,0:T(8,128)S(1)}, f32[51,8,128]{2,1,0:T(8,128)S(1)}, u32[]{:S(2)}, u32[]{:S(2)}) collective-permute-start(f32[51,8,128]{2,1,0:T(8,128)S(1)} %get-tuple-element.48), channel_id=1, source_target_pairs={{0,4},{1,2},{2,1},{3,7},{4,0},{5,6},{6,5},{7,3},{8,12},{9,10},{10,... | collective-permute-start | bytes 626696 | tf_op jit(solution)/shard_map/ppermute | solution.py:51
  10.4 3.2 %collective-permute-start.6 = (f32[43,8,128]{2,1,0:T(8,128)S(1)}, f32[43,8,128]{2,1,0:T(8,128)S(1)}, u32[]{:S(2)}, u32[]{:S(2)}) collective-permute-start(f32[43,8,128]{2,1,0:T(8,128)S(1)} %get-tuple-element.53), channel_id=1, source_target_pairs={{0,4},{1,5},{2,6},{3,7},{4,0},{5,1},{6,2},{7,3},{8,12},{9,13},{10,... | collective-permute-start | bytes 528392 | tf_op jit(solution)/shard_map/ppermute | solution.py:52
  10.9 6.9 %collective-permute-start.7 = (f32[43,8,128]{2,1,0:T(8,128)S(1)}, f32[43,8,128]{2,1,0:T(8,128)S(1)}, u32[]{:S(2)}, u32[]{:S(2)}) collective-permute-start(f32[43,8,128]{2,1,0:T(8,128)S(1)} %get-tuple-element.54), channel_id=1, source_target_pairs={{0,1},{1,0},{2,3},{3,2},{4,8},{5,9},{6,10},{7,11},{8,4},{9,5},{10,... | collective-permute-start | bytes 528392 | tf_op jit(solution)/shard_map/ppermute | solution.py:51

commit v4 on v3

--- a/solution.py
+++ b/solution.py
@@ -144,6 +144,23 @@
     )
 
 
+def coarse_faces(h, span, xstep, zstep):
+    wx, wy, wz, inverse = whole_faces(h, span, xstep, zstep)
+    return wx, prev_x(wx, xstep), wy, roll(wy, 1, 1), wz, roll(wz, zstep, 2), inverse
+
+
+def coarse_spread(v, wx, wx_back, wy, wy_back, wz, wz_back, zstep):
+    turned = roll(v, v.shape[-1] // 2, 2)
+    low = lanes_of(v) < v.shape[-1] // 2
+    after = jnp.where(low, turned, shift_up(turned))
+    before = jnp.where(low, shift_down(turned), turned)
+    return (
+        (wx * after + wx_back * before)
+        + (wy * roll(v, -1, 1) + wy_back * roll(v, 1, 1))
+        + (wz * roll(v, -zstep, 2) + wz_back * roll(v, zstep, 2))
+    )
+
+
 def read(array, start, size, top, rows, dx=0, dy=0):
     ref, planes_off, rows_off = array
     return ref[pl.ds(start + planes_off + dx, size), pl.ds(top + rows_off + dy, rows), :]
@@ -243,33 +260,45 @@
     slabs(0, packed.shape[0], copies, copy_out)
 
 
+def sum_whole_blocks(value, buffer):
+    halved = halve_rows(value, buffer)
+    lane = lane_row(value.shape[-1])
+    span = value.shape[-1] // 4
+    return (halved + pick_lanes(halved, lane ^ 1)) + (
+        pick_lanes(halved, lane ^ span) + pick_lanes(halved, lane ^ span ^ 1)
+    )
+
+
 def coarse_cycle(g2, level2, level3, buffer):
     wx2, wy2, wz2, inv2 = level2
-    wx3, wy3, wz3, inv3 = level3
-    width = g2.shape[-1]
-    span = width // 4
+    *w3, inv3 = level3
+    span = g2.shape[-1] // 4
     v2 = inv2 * g2
     r2 = KEEP * g2 + whole_spread(v2, wx2, wy2, wz2, span, 1)
-    g3 = 0.125 * halve_rows(add_partner(add_partner(r2, 1), span), buffer)
+    g3 = 0.125 * sum_whole_blocks(r2, buffer)
     v3 = inv3 * g3
     for _ in range(COARSE_SWEEPS - 1):
-        v3 = KEEP * v3 + inv3 * (g3 + whole_spread(v3, wx3, wy3, wz3, 2 * span, 2))
+        v3 = KEEP * v3 + inv3 * (g3 + coarse_spread(v3, *w3, 2))
     double_rows(buffer, 0, v3)
     u2 = v2 + buffer[...]
     return KEEP * u2 + inv2 * (g2 + whole_spread(u2, wx2, wy2, wz2, span, 1))
 
 
-def spread_out(e2, wide, doubled, planes):
+def spread_out(e2, wide, around, doubled, planes):
     count, rows, width = e2.shape
-    block = rows // lax.axis_size("gy")
+    blocks = lax.axis_size("gy")
+    block = rows // blocks
     span = width // 4
-    wide[0:1] = jnp.zeros((1,) + wide.shape[1:], F32)
-    wide[count + 1 : count + 2] = jnp.zeros((1,) + wide.shape[1:], F32)
-    wide[1 : count + 1, 0:8, :] = jnp.zeros((count, 8, width), F32)
-    wide[1 : count + 1, rows + 8 : rows + 16, :] = jnp.zeros((count, 8, width), F32)
-    wide[1 : count + 1, 8 : 8 + rows, :] = e2
+    for edge in (0, count + 1):
+        wide[edge] = jnp.zeros(wide.shape[1:], F32)
+    for edge in (0, blocks + 1):
+        wide[:, edge] = jnp.zeros((count + 2,) + wide.shape[2:], F32)
+    for y in range(blocks):
+        wide[1 : count + 1, y + 1] = e2[:, y * block : (y + 1) * block]
     gx, gy = lax.axis_index("gx"), lax.axis_index("gy")
-    around = wide[pl.ds(gx, 3), pl.ds(gy * block + 8 - block, 16), :]
+    for x in range(3):
+        for y in range(3):
+            around[x, y * block : (y + 1) * block, :] = wide[gx + x, gy + y]
     lane = lane_row(width)
     kept = 3 * block
     for j in planes:
@@ -280,73 +309,106 @@
 
 def row_starts(axis, block):
     odd = is_odd(axis)
-    low = (0, NEAR)
-    high = (block - NEAR, block - HALO)
+    low = (0, 0, NEAR)
+    high = (block - NEAR, block - FAR, block - HALO)
     to_near = [jnp.where(odd, a, b) for a, b in zip(low, high)]
     to_far = [jnp.where(odd, b, a) for a, b in zip(low, high)]
     return to_near, to_far
 
 
-def pack_rows(source, starts, first, last, target):
-    count = source.shape[0]
-    half = (last - first) // 2
-    target[0:count] = source[:, pl.ds(starts[0], NEAR), :]
-    target[count : count + half, 0:FAR, :] = source[first : first + half, pl.ds(starts[1], FAR), :]
-    target[count : count + half, FAR:NEAR, :] = source[first + half : last, pl.ds(starts[1], FAR), :]
-
-
-def unpack_rows(target, planes_off, top, bottom, count, first, last, near, far):
-    half = (last - first) // 2
-    for choose, at, edge in ((below, top - NEAR, top - HALO), (above, bottom, bottom + NEAR)):
-        target[planes_off : planes_off + count, at : at + NEAR, :] = choose(near[0:count], far[0:count], "gy")
-        strips = choose(near[count : count + half], far[count : count + half], "gy")
-        target[planes_off + first : planes_off + first + half, edge : edge + FAR, :] = strips[:, 0:FAR]
-        target[planes_off + first + half : planes_off + last, edge : edge + FAR, :] = strips[:, FAR:NEAR]
+def whole_strips(planes):
+    return (0, planes), (0, 0, 0), (0, planes // 2, planes // 2)
+
+
+def diamond_strips(planes):
+    full = (HALO - NEAR + 1, planes - HALO + NEAR - 1)
+    far = HALO - FAR + 1
+    half = planes // 2 - far
+    return full, (1, full[1], full[0] - 1), (far, far + half, half)
+
+
+def strip_tiles(strips):
+    (first, last), (_, _, edge), (_, _, half) = strips
+    return last - first + edge + half
+
+
+def pack_rows(source, starts, strips, target):
+    (first, last), *halves = strips
+    at = last - first
+    target[0:at] = source[first:last, pl.ds(starts[0], NEAR), :]
+    for start, (one, two, count) in zip(starts[1:], halves):
+        if count:
+            target[at : at + count, 0:FAR, :] = source[one : one + count, pl.ds(start, FAR), :]
+            target[at : at + count, FAR:NEAR, :] = source[two : two + count, pl.ds(start, FAR), :]
+        at += count
+
+
+def unpack_rows(target, planes_off, top, bottom, strips, near, far):
+    (first, last), *halves = strips
+    for choose, rows in ((below, (top - NEAR, top - FAR, top - HALO)), (above, (bottom, bottom, bottom + NEAR))):
+        at = last - first
+        target[planes_off + first : planes_off + last, rows[0] : rows[0] + NEAR, :] = choose(
+            near[0:at], far[0:at], "gy"
+        )
+        for row, (one, two, count) in zip(rows[1:], halves):
+            if count:
+                both = choose(near[at : at + count], far[at : at + count], "gy")
+                for plane, value in ((planes_off + one, both[:, 0:FAR]), (planes_off + two, both[:, FAR:NEAR])):
+                    target[plane : plane + count, row : row + FAR, :] = value
+            at += count
 
 
 def start_kernel(
-    right_hbm, material_hbm, cond, h, right, k_near, k_far, g_near, g_far, material, table, arrived,
+    right_hbm, material_hbm, right, material, k_near, k_far, g_near, g_far, arrived,
 ):
-    planes, rows, width = h.shape
+    planes, rows, _ = right.shape
     copies = [
-        pltpu.make_async_copy(right_hbm, right, arrived.at[0]),
-        pltpu.make_async_copy(material_hbm, material, arrived.at[1]),
+        pltpu.make_async_copy(material_hbm, material, arrived.at[0]),
+        pltpu.make_async_copy(right_hbm, right, arrived.at[1]),
     ]
     for copy in copies:
         copy.start()
-    table[0:1, 0 : cond.shape[1]] = cond[...]
     copies[0].wait()
+    odd = is_odd("gx")
+    k_near[...] = material[pl.ds(jnp.where(odd, 0, planes - HALO), HALO)]
+    k_far[...] = material[pl.ds(jnp.where(odd, planes - HALO, 0), HALO)]
+    copies[1].wait()
     to_near, to_far = row_starts("gy", rows)
-    pack_rows(right, to_near, 0, planes, g_near)
-    pack_rows(right, to_far, 0, planes, g_far)
-    copies[1].wait()
-    which = material[...].reshape(planes * rows, width)
-    values = jnp.broadcast_to(0.5 * table[0:1, :], which.shape)
-    h[...] = jnp.take_along_axis(values, which, axis=1).reshape(planes, rows, width)
-    odd = is_odd("gx")
-    k_near[...] = h[pl.ds(jnp.where(odd, 0, planes - HALO), HALO)]
-    k_far[...] = h[pl.ds(jnp.where(odd, planes - HALO, 0), HALO)]
-
-
-def far_planes(planes):
-    return HALO - FAR + 1, planes - HALO + FAR - 1
-
-
-def k_kernel(h, near, far, wide, k_near, k_far):
+    strips = whole_strips(planes)
+    pack_rows(right, to_near, strips, g_near)
+    pack_rows(right, to_far, strips, g_far)
+
+
+def table_kernel(cond, material, near, table, h, h_near):
+    table[...] = jnp.zeros(table.shape, F32)
+    table[0:1, 0 : cond.shape[1]] = 0.5 * cond[...]
+    h[...] = look_up(material[...], table)
+    h_near[...] = look_up(near[...], table)
+
+
+def look_up(ids, table):
+    planes, rows, width = ids.shape
+    ids = ids.reshape(planes * rows, width)
+    values = jnp.broadcast_to(table[0:1, :], ids.shape)
+    return jnp.take_along_axis(values, ids, axis=1).reshape(planes, rows, width)
+
+
+def k_kernel(h, h_near, far, table, wide, k_near, k_far):
     block = h.shape[0]
-    wide[0:HALO] = below(near[...], far[...], "gx")
+    h_far = look_up(far[...], table)
+    wide[0:HALO] = below(h_near[...], h_far, "gx")
     wide[HALO : HALO + block] = h[...]
-    wide[HALO + block :] = above(near[...], far[...], "gx")
-    first, last = far_planes(wide.shape[0])
-    to_near, to_far = row_starts("gy", h.shape[1])
-    pack_rows(wide, to_near, first, last, k_near)
-    pack_rows(wide, to_far, first, last, k_far)
+    wide[HALO + block :] = above(h_near[...], h_far, "gx")
+    strips = diamond_strips(wide.shape[0])
+    to_near, to_far = row_starts("gy", wide.shape[1])
+    pack_rows(wide, to_near, strips, k_near)
+    pack_rows(wide, to_far, strips, k_far)
 
 
 def plane_strips(rows):
     strips, at = [], 0
     for distance in range(1, HALO):
-        cut = (distance // 4) * 4
+        cut = HALO - -(-(HALO - 1 - distance) // 4) * 4
         tiles = (rows - 2 * cut) // 8
         strips.append((distance, cut, tiles, at))
         at += tiles
@@ -357,7 +419,7 @@
     block, rows, _ = right.shape
     top = BASE // 2
     wide[:, top + HALO : top + HALO + rows, :] = right[...]
-    unpack_rows(wide, 0, top + HALO, top + HALO + rows, block, 0, block, near, far)
+    unpack_rows(wide, 0, top + HALO, top + HALO + rows, whole_strips(block), near, far)
     odd = is_odd("gx")
     strips, _ = plane_strips(rows + 2 * HALO)
     for distance, cut, tiles, at in strips:
@@ -367,80 +429,72 @@
                 target[at + tile] = wide[plane, top + cut + 8 * tile : top + cut + 8 * tile + 8, :]
 
 
-def first_kernel(
-    k_wide, k_near, k_far, g_wide, g_near, g_far,
-    packed, g0, wx0, wy0, wz0, inv0, tot0, v0, wx1, wy1, wz1, inv1, v1, g1,
-    h0, h1, buf0, bufp,
+def faces_kernel(
+    k_wide, k_near, k_far,
+    wx0, wy0, wz0, inv0, tot0, wx1, wy1, wz1, inv1, h2,
+    h0, h1, buf0,
 ):
     top = BASE // 2
-    planes, rows, width = k_wide.shape
-    own = slice(HALO, planes - HALO)
+    planes, rows, _ = k_wide.shape
     h0[1 : planes + 1, top + HALO : top + HALO + rows, :] = k_wide[...]
-    first, last = far_planes(planes)
-    unpack_rows(h0, 1, top + HALO, top + HALO + rows, planes, first, last, k_near, k_far)
-    g0[own] = g_wide[...]
+    unpack_rows(h0, 1, top + HALO, top + HALO + rows, diamond_strips(planes), k_near, k_far)
     rows = rows + 2 * HALO
+
+    aH0, aWX0, aH1, aWX1 = (h0, 1, top), (wx0, 1, BASE), (h1, 1, BASE), (wx1, 1, BASE)
+    _, wx, wy, wz, total, inverse = faces(aH0, (0, planes, 0, rows), 1)
+    write(aWX0, 0, 0, wx)
+    for ref, value in ((wy0, wy), (wz0, wz), (tot0, total), (inv0, inverse)):
+        write((ref, 0, BASE), 0, 0, value)
+    write(aH1, 0, 0, sum_blocks(read(aH0, 0, planes, 0, rows), buf0, 1) * (1.0 / 32.0))
+
+    planes1, rows1 = planes // 2, -(-rows // 16) * 8
+    _, wx, wy, wz, _, inverse = faces(aH1, (0, planes1, 0, rows1), 2)
+    write(aWX1, 0, 0, wx)
+    for ref, value in ((wy1, wy), (wz1, wz), (inv1, inverse)):
+        write((ref, 0, BASE), 0, 0, value)
+    low = HALO // 2
+    own = read(aH1, low, planes1 - HALO, low, rows // 2 - HALO)
+    h2[...] = sum_blocks(own, buf0, 2) * (1.0 / 32.0)
+
+
+def first_kernel(
+    g_wide, g_near, g_far, wx0, wy0, wz0, inv0, wx1, wy1, wz1, inv1, h2,
+    packed, g0, v0, v1, g1,
+    buf0, bufp,
+):
+    top = BASE // 2
+    planes, _, width = g0.shape
+    block, rows = g_wide.shape[0], g_wide.shape[1] - BASE
+    g0[HALO : HALO + block] = g_wide[...]
     strips, _ = plane_strips(rows)
     for distance, cut, tiles, at in strips:
         for choose, plane in ((below, HALO - distance), (above, planes - HALO - 1 + distance)):
             value = choose(g_near[at : at + tiles], g_far[at : at + tiles], "gx")
             g0[plane, top + cut : top + cut + 8 * tiles, :] = value.reshape(8 * tiles, width)
 
-    aH0, aG0 = (h0, 1, top), (g0, 0, top)
-    aWX0, aV0 = (wx0, 1, BASE), (v0, 1, BASE)
-    aWY0, aWZ0, aINV0, aTOT0 = ((ref, 0, BASE) for ref in (wy0, wz0, inv0, tot0))
-    aH1, aWX1, aV1 = (h1, 1, BASE), (wx1, 1, BASE), (v1, 1, BASE)
-    aWY1, aWZ1, aINV1, aG1 = ((ref, 0, BASE) for ref in (wy1, wz1, inv1, g1))
-    size = planes
-
-    def faces0(i):
-        window = (i, size, 0, rows)
-        here, wx, wy, wz, total, inverse = faces(aH0, window, 1)
-        write(aWX0, i, 0, wx)
-        write(aWY0, i, 0, wy)
-        write(aWZ0, i, 0, wz)
-        write(aTOT0, i, 0, total)
-        write(aINV0, i, 0, inverse)
-        write(aV0, i, 0, inverse * read(aG0, *window))
-
-    slabs(0, planes, size, faces0)
-    write(aH1, 0, 0, sum_blocks(read(aH0, 0, planes, 0, rows), buf0, 1) * (1.0 / 32.0))
-
-    def resid0(i):
-        window = (i, size, 0, rows)
-        _, around = spread(aV0, (aWX0, aWY0, aWZ0), window, 1)
-        buf0[pl.ds(i // 2, size // 2)] = halve_planes(KEEP * read(aG0, *window) + around)
-
-    slabs(0, planes, size, resid0)
-    r = buf0[:, pl.ds(0, rows // 2, stride=2), :] + buf0[:, pl.ds(1, rows // 2, stride=2), :]
-    write(aG1, 0, 0, add_partner(r, 1) * 0.125)
+    aG0, aV0, aV1, aG1 = (g0, 0, top), (v0, 1, BASE), (v1, 1, BASE), (g1, 0, BASE)
+    w0 = (wx0, 1, BASE), (wy0, 0, BASE), (wz0, 0, BASE)
+    w1 = (wx1, 1, BASE), (wy1, 0, BASE), (wz1, 0, BASE)
+    window = (0, planes, 0, rows)
+    write(aV0, 0, 0, read((inv0, 0, BASE), *window) * read(aG0, *window))
+    _, around = spread(aV0, w0, window, 1)
+    write(aG1, 0, 0, sum_blocks(KEEP * read(aG0, *window) + around, buf0, 1) * 0.125)
 
     planes1, rows1 = planes // 2, -(-rows // 16) * 8
-
-    def faces1(i):
-        window = (i, planes1, 0, rows1)
-        _, wx, wy, wz, total, inverse = faces(aH1, window, 2)
-        write(aWX1, i, 0, wx)
-        write(aWY1, i, 0, wy)
-        write(aWZ1, i, 0, wz)
-        write(aINV1, i, 0, inverse)
-        write(aV1, i, 0, inverse * read(aG1, *window))
-
-    slabs(0, planes1, planes1, faces1)
-
+    window = (0, planes1, 0, rows1)
+    write(aV1, 0, 0, read((inv1, 0, BASE), *window) * read(aG1, *window))
     low = HALO // 2
     window = (low, planes1 - HALO, low, rows // 2 - HALO)
-    _, around = spread(aV1, (aWX1, aWY1, aWZ1), window, 2)
+    _, around = spread(aV1, w1, window, 2)
     g2 = sum_blocks(KEEP * read(aG1, *window) + around, buf0, 2) * 0.125
-    h2 = sum_blocks(read(aH1, *window), buf0, 2) * (1.0 / 32.0)
-    send_to_all(packed, pack_block([g2, h2], bufp))
+    send_to_all(packed, pack_block([g2, h2[...]], bufp))
 
 
 def second_kernel(
     got, g0, wx0, wy0, wz0, inv0, tot0, v0, wx1, wy1, wz1, inv1, v1, g1,
-    packed, v0n, v1n, g1n, wx2, wy2, wz2, inv2, wx3, wy3, wz3, inv3,
-    g2, h2, buf2, wide, doubled, u1, e0, u0, v0m, buf0, bufp,
+    packed, v0n, v1n, g1n, *rest,
 ):
+    levels, (g2, h2, buf2, wide, around, doubled, u1, e0, u0, v0m, buf0, bufp) = rest[:11], rest[11:]
     count, rows2, width = g2.shape
     gy_count = lax.axis_size("gy")
     block2 = rows2 // gy_count
@@ -457,11 +511,11 @@
     span = width // 4
     h = h2[...]
     level2 = whole_faces(h, span, span, 1)
-    h3 = halve_rows(add_partner(add_partner(h, 1), span), buf2) * (1.0 / 32.0)
-    level3 = whole_faces(h3, span, 2 * span, 2)
-    for ref, value in zip((wx2, wy2, wz2, inv2, wx3, wy3, wz3, inv3), level2 + level3):
+    h3 = sum_whole_blocks(h, buf2) * (1.0 / 32.0)
+    level3 = coarse_faces(h3, span, 2 * span, 2)
+    for ref, value in zip(levels, level2 + level3):
         ref[...] = value
-    spread_out(coarse_cycle(g2[...], level2, level3, buf2), wide, doubled, range(1, 11))
+    spread_out(coarse_cycle(g2[...], level2, level3, buf2), wide, around, doubled, range(1, 11))
 
     top = BASE // 2
     planes = g0.shape[0]
@@ -522,11 +576,9 @@
 
 
 def third_kernel(
-    got, g0, wx0, wy0, wz0, inv0, v0n, wx1, wy1, wz1, inv1, v1n, g1n,
-    wx2, wy2, wz2, inv2, wx3, wy3, wz3, inv3,
-    out,
-    g2, buf2, wide, doubled, u1, e0, u0,
+    got, g0, wx0, wy0, wz0, inv0, v0n, wx1, wy1, wz1, inv1, v1n, g1n, *rest,
 ):
+    levels, (out, g2, buf2, wide, around, doubled, u1, e0, u0) = rest[:11], rest[11:]
     count, rows2, width = g2.shape
     gy_count = lax.axis_size("gy")
     block2 = rows2 // gy_count
@@ -537,9 +589,8 @@
         return carry
 
     lax.fori_loop(0, count, unpack, 0)
-    level2 = (wx2[...], wy2[...], wz2[...], inv2[...])
-    level3 = (wx3[...], wy3[...], wz3[...], inv3[...])
-    spread_out(coarse_cycle(g2[...], level2, level3, buf2), wide, doubled, range(3, 9))
+    values = [ref[...] for ref in levels]
+    spread_out(coarse_cycle(g2[...], values[:4], values[4:], buf2), wide, around, doubled, range(3, 9))
 
     top = BASE // 2
     planes = g0.shape[0]
@@ -582,7 +633,7 @@
     slabs(HALO, planes - HALO, size, sweep)
 
 
-def kernel_call(body, outs, scratch, args):
+def kernel_call(body, outs, scratch, args, cost=None):
     def size(shape):
         total = 4
         for length in shape:
@@ -598,6 +649,7 @@
         out_specs=[pl.BlockSpec(memory_space=pltpu.VMEM)] * len(outs),
         scratch_shapes=[pltpu.VMEM(s, F32) for s in scratch],
         compiler_params=pltpu.CompilerParams(vmem_limit_bytes=limit),
+        cost_estimate=cost,
     )(*args)
 
 
@@ -612,51 +664,61 @@
     X1, Y1 = X // 2, -(-Y // 16) * 8 + 2 * BASE
     xb, yb = bx // 4, by // 4
 
-    strip = (bx + bx // 2, NEAR, bz)
-    outs = [(bx, by, bz), (bx, by, bz), (HALO, by, bz), (HALO, by, bz), strip, strip]
-    h, right, k_near, k_far, g_near, g_far = pl.pallas_call(
+    strip = (strip_tiles(whole_strips(bx)), NEAR, bz)
+    def ints(*shape):
+        return jax.ShapeDtypeStruct(shape, jnp.int32)
+
+    def floats(*shape):
+        return jax.ShapeDtypeStruct(shape, F32)
+
+    outs = [floats(bx, by, bz), ints(bx, by, bz), ints(HALO, by, bz), ints(HALO, by, bz), floats(*strip), floats(*strip)]
+    right, material, k_near, k_far, g_near, g_far = pl.pallas_call(
         start_kernel,
-        out_shape=[jax.ShapeDtypeStruct(s, F32) for s in outs],
-        in_specs=[pl.BlockSpec(memory_space=pl.ANY)] * 2 + [pl.BlockSpec(memory_space=pltpu.VMEM)],
+        out_shape=outs,
+        in_specs=[pl.BlockSpec(memory_space=pl.ANY)] * 2,
         out_specs=[pl.BlockSpec(memory_space=pltpu.VMEM)] * len(outs),
-        scratch_shapes=[
-            pltpu.VMEM((bx, by, bz), jnp.int32),
-            pltpu.VMEM((8, bz), F32),
-            pltpu.SemaphoreType.DMA((2,)),
-        ],
+        scratch_shapes=[pltpu.SemaphoreType.DMA((2,))],
         compiler_params=pltpu.CompilerParams(vmem_limit_bytes=START_LIMIT),
-    )(right_side, material, conductivity[None])
+    )(right_side, material)
     k_near, k_far = trade(k_near, k_far, "gx")
     g_near, g_far = trade(g_near, g_far, "gy")
+    table, h, h_near = kernel_call(
+        table_kernel, [(8, bz), (bx, by, bz), (HALO, by, bz)], [], [conductivity[None], material, k_near]
+    )
     strip = (plane_strips(Y)[1], 8, bz)
     g_wide, g_near, g_far = kernel_call(
         g_kernel, [(bx, YA, bz), strip, strip], [], [right, g_near, g_far]
     )
-    first, last = far_planes(X)
-    strip = (X + (last - first) // 2, NEAR, bz)
+    strip = (strip_tiles(diamond_strips(X)), NEAR, bz)
     k_wide, k_near, k_far = kernel_call(
-        k_kernel, [(X, by, bz), strip, strip], [], [h, k_near, k_far]
+        k_kernel, [(X, by, bz), strip, strip], [], [h, h_near, k_far, table]
     )
     g_near, g_far = trade(g_near, g_far, "gx")
     k_near, k_far = trade(k_near, k_far, "gy")
 
     pad0, full0, pad1, full1 = (X + 2, YB, bz), (X, YB, bz), (X1 + 2, Y1, bz), (X1, Y1, bz)
-    packed, g0, wx0, wy0, wz0, inv0, tot0, v0, wx1, wy1, wz1, inv1, v1, g1 = kernel_call(
+    wx0, wy0, wz0, inv0, tot0, wx1, wy1, wz1, inv1, h2 = kernel_call(
+        faces_kernel,
+        [pad0, full0, full0, full0, full0, pad1, full1, full1, full1, (xb, yb, bz)],
+        [(X + 2, YA, bz), pad1, (X1, Y, bz)],
+        [k_wide, k_near, k_far],
+        pl.CostEstimate(flops=0, bytes_accessed=8 << 20, transcendentals=0),
+    )
+    packed, g0, v0, v1, g1 = kernel_call(
         first_kernel,
-        [(devices, 2 * yb, bz), (X, YA, bz), pad0, full0, full0, full0, full0, pad0]
-        + [pad1, full1, full1, full1, pad1, full1],
-        [(X + 2, YA, bz), pad1, (X1, Y, bz), (xb, 8, bz)],
-        [k_wide, k_near, k_far, g_wide, g_near, g_far],
+        [(devices, 2 * yb, bz), (X, YA, bz), pad0, pad1, full1],
+        [(X1, Y, bz), (xb, 8, bz)],
+        [g_wide, g_near, g_far, wx0, wy0, wz0, inv0, wx1, wy1, wz1, inv1, h2],
     )
     got = everywhere(packed)
     level2 = (gx_count, gy_count * yb, bz)
     level3 = (gx_count, gy_count * yb // 2, bz)
     coarse_scratch = [
-        level2, (gx_count + 2, gy_count * yb + 16, bz), (3 * xb, 32, bz), pad1, (X1, by + 24, bz), pad0,
+        level2, (gx_count + 2, gy_count + 2, yb, bz), (3, 16, bz), (3 * xb, 32, bz), pad1, (X1, by + 24, bz), pad0,
     ]
     packed, v0n, v1n, g1n, *levels = kernel_call(
         second_kernel,
-        [(devices, yb, bz), pad0, pad1, full1] + [level2] * 4 + [level3] * 4,
+        [(devices, yb, bz), pad0, pad1, full1] + [level2] * 4 + [level3] * 7,
         [level2, level2] + coarse_scratch + [pad0, (X1, Y, bz), (xb, 8, bz)],
         [got, g0, wx0, wy0, wz0, inv0, tot0, v0, wx1, wy1, wz1, inv1, v1, g1],
     )

time: 47.3 us -> 45.7 us (0.966)
  waiting for transfers between devices: 5.49 us -> 2.98 us
  blocking collectives: 22.2 us -> 22.8 us
    ppermute x4, waiting for transfers between devices: 5.47 us -> 1.18 us  [trade(): from_far = lax.ppermute(to_far, ('gx', 'gy'), route(axis, True))]
    ppermute x4, waiting for transfers between devices: 0.01 us -> 1.8 us  [trade(): from_near = lax.ppermute(to_near, ('gx', 'gy'), route(axis, False))]
    all_to_all x2, blocking collectives: 22.2 us -> 22.8 us  [everywhere(): return lax.all_to_all(copies, ('gx', 'gy'), 0, 0)]
    pallas_call x5 -> x7, Pallas kernels: 7.25 us -> 7.67 us  [kernel_call(): pl.pallas_call(body, out_shape=[jax.ShapeDtypeStruct(s, F32) for s in out...]
  transfers between devices with their start and end apart: 8 -> 8, of which waited for: 2 -> 3; matrix products, arithmetic and copies ran while one was open for 0% -> 0% of each run, Pallas kernels for 0% -> 3%
where the time goes in v4:
time: 45.7 us; the launch traced here: 45.5 us
  blocking collectives  22.8 us (50%)
  starting transfers between devices  10.4 us (23%)
  Pallas kernels  8.67 us (19%)
  waiting for transfers between devices  2.98 us (7%)
  local copies, waits for them, and re-layouts  0.66 us (1%)
    all_to_all x2, blocking collectives, everywhere(): return lax.all_to_all(copies, ('gx', 'gy'), 0, 0)  22.8 us
    pallas_call x7, Pallas kernels, kernel_call(): pl.pallas_call(body, out_shape=[jax.ShapeDtypeStruct(s, F32) for s in out...  7.67 us
    ppermute x4, starting transfers between devices, trade(): from_far = lax.ppermute(to_far, ('gx', 'gy'), route(axis, True))  6.7 us
    ppermute x4, starting transfers between devices, trade(): from_near = lax.ppermute(to_near, ('gx', 'gy'), route(axis, False))  3.66 us
    ppermute x4, waiting for transfers between devices, trade(): from_near = lax.ppermute(to_near, ('gx', 'gy'), route(axis, False))  1.8 us
    ppermute x4, waiting for transfers between devices, trade(): from_far = lax.ppermute(to_far, ('gx', 'gy'), route(axis, True))  1.18 us
    pallas_call x1, Pallas kernels, local(): pl.pallas_call(start_kernel, out_shape=outs, in_specs=[pl.BlockSpec(memor...  1 us
  transfers between devices with their start and end apart: 8, of which 3 were waited for; matrix products, arithmetic and copies ran while one was open for 0% of the time, Pallas kernels for 3%

profile of v4, /device:TPU:0, one launch (start us, length us, event | category | flops | bytes accessed | tf_op | source)
XLA Modules:
  0.0 45.5 jit_solution(16639305330542227501)
XLA Ops:
  0.0 1.0 %shard_map.37 = (f32[16,16,128]{2,1,0:T(8,128)S(1)}, s32[16,16,128]{2,1,0:T(8,128)S(1)}, s32[12,16,128]{2,1,0:T(8,128)S(1)}, s32[12,16,128]{2,1,0:T(8,128)S(1)},...) custom-call(f32[16,16,128]{2,1,0:T(8,128)} %right_hbm.1, s32[16,16,128]{2,1,0:T(8,128)} %material_hbm.1), custom_call_target="tpu_custom_call" | custom-call | tf_op jit(solution)/shard_map/pallas_call | solution.py:675
  1.0 0.5 %collective-permute-start.4 = (s32[12,16,128]{2,1,0:T(8,128)S(1)}, s32[12,16,128]{2,1,0:T(8,128)S(1)}, u32[]{:S(2)}, u32[]{:S(2)}) collective-permute-start(s32[12,16,128]{2,1,0:T(8,128)S(1)} %get-tuple-element.57), channel_id=1, source_target_pairs={{0,4},{1,5},{2,6},{3,7},{4,0},{5,1},{6,2},{7,3},{8,12},{9,13},{10,... | collective-permute-start | bytes 294920 | tf_op jit(solution)/shard_map/ppermute | solution.py:52
  1.5 2.6 %collective-permute-start.5 = (s32[12,16,128]{2,1,0:T(8,128)S(1)}, s32[12,16,128]{2,1,0:T(8,128)S(1)}, u32[]{:S(2)}, u32[]{:S(2)}) collective-permute-start(s32[12,16,128]{2,1,0:T(8,128)S(1)} %get-tuple-element.60), channel_id=1, source_target_pairs={{0,1},{1,0},{2,3},{3,2},{4,8},{5,9},{6,10},{7,11},{8,4},{9,5},{10,... | collective-permute-start | bytes 294920 | tf_op jit(solution)/shard_map/ppermute | solution.py:51
  4.2 0.1 collective-permute-start
  4.3 1.2 %collective-permute-start.1 = (f32[24,8,128]{2,1,0:T(8,128)S(1)}, f32[24,8,128]{2,1,0:T(8,128)S(1)}, u32[]{:S(2)}, u32[]{:S(2)}) collective-permute-start(f32[24,8,128]{2,1,0:T(8,128)S(1)} %get-tuple-element.52), channel_id=1, source_target_pairs={{0,4},{1,2},{2,1},{3,7},{4,0},{5,6},{6,5},{7,3},{8,12},{9,10},{10,... | collective-permute-start | bytes 294920 | tf_op jit(solution)/shard_map/ppermute | solution.py:51
  5.5 0.0 collective-permute-done.4.near
  5.5 0.0 copy-start
  5.5 0.7 %copy-done = f32[16]{0:T(128)S(1)} copy-done((f32[16]{0:T(128)S(1)}, f32[16]{0:T(128)}, u32[]{:S(2)}) %copy-start) | copy-done | bytes 88
  6.2 0.2 shard_map.39
  6.4 0.4 collective-permute-done.5.far
  6.8 0.2 shard_map.40
  7.0 2.6 %collective-permute-start.6 = (f32[45,8,128]{2,1,0:T(8,128)S(1)}, f32[45,8,128]{2,1,0:T(8,128)S(1)}, u32[]{:S(2)}, u32[]{:S(2)}) collective-permute-start(f32[45,8,128]{2,1,0:T(8,128)S(1)} %get-tuple-element.63), channel_id=1, source_target_pairs={{0,1},{1,0},{2,3},{3,2},{4,5},{5,4},{6,7},{7,6},{8,9},{9,8},{10,11... | collective-permute-start | bytes 552968 | tf_op jit(solution)/shard_map/ppermute | solution.py:52
  9.5 0.1 collective-permute-start.7
  9.6 0.0 collective-permute-done.near
  9.6 0.0 collective-permute-done.1.far
  9.6 0.1 shard_map.38
  9.7 0.5 %collective-permute-start.2 = (f32[40,8,128]{2,1,0:T(8,128)S(1)}, f32[40,8,128]{2,1,0:T(8,128)S(1)}, u32[]{:S(2)}, u32[]{:S(2)}) collective-permute-start(f32[40,8,128]{2,1,0:T(8,128)S(1)} %get-tuple-element.54), channel_id=1, source_target_pairs={{0,4},{1,5},{2,6},{3,7},{4,0},{5,1},{6,2},{7,3},{8,12},{9,13},{10,... | collective-permute-start | bytes 491528 | tf_op jit(solution)/shard_map/ppermute | solution.py:52
  10.2 2.7 %collective-permute-start.3 = (f32[40,8,128]{2,1,0:T(8,128)S(1)}, f32[40,8,128]{2,1,0:T(8,128)S(1)}, u32[]{:S(2)}, u32[]{:S(2)}) collective-permute-start(f32[40,8,128]{2,1,0:T(8,128)S(1)} %get-tuple-element.55), channel_id=1, source_target_pairs={{0,1},{1,0},{2,3},{3,2},{4,8},{5,9},{6,10},{7,11},{8,4},{9,5},{10,... | collective-permute-start | bytes 491528 | tf_op jit(solution)/shard_map/ppermute | solution.py:51
  12.9 1.8 %collective-permute-done.6.k_near = f32[45,8,128]{2,1,0:T(8,128)S(1)} collective-permute-done((f32[45,8,128]{2,1,0:T(8,128)S(1)}, f32[45,8,128]{2,1,0:T(8,128)S(1)}, u32[]{:S(2)}, u32[]{:S(2)}) %collective-permute-start.6) | collective-permute-done | bytes 184352 | tf_op jit(solution)/shard_map/ppermute | solution.py:52
  14.7 0.0 collective-permute-done.7.k_far
  14.7 1.0 %shard_map.41 = (f32[42,56,128]{2,1,0:T(8,128)S(1)}, f32[40,56,128]{2,1,0:T(8,128)S(1)}, f32[40,56,128]{2,1,0:T(8,128)S(1)}, f32[40,56,128]{2,1,0:T(8,128)S(1)},...) custom-call(f32[40,16,128]{2,1,0:T(8,128)S(1)} %get-tuple-element.62, ...), custom_call_target="tpu_custom_call" | custom-call | bytes 8388608 | tf_op jit(solution)/shard_map/pallas_call | solution.py:645
  15.7 0.0 collective-permute-done.2.g_near
  15.7 0.8 %collective-permute-done.3.g_far = f32[40,8,128]{2,1,0:T(8,128)S(1)} collective-permute-done((f32[40,8,128]{2,1,0:T(8,128)S(1)}, f32[40,8,128]{2,1,0:T(8,128)S(1)}, u32[]{:S(2)}, u32[]{:S(2)}) %collective-permute-start.3) | collective-permute-done | bytes 163872 | tf_op jit(solution)/shard_map/ppermute | solution.py:51
  16.4 1.3 %shard_map.42 = (f32[32,8,128]{2,1,0:T(8,128)S(1)}, f32[40,48,128]{2,1,0:T(8,128)S(1)}, f32[42,56,128]{2,1,0:T(8,128)S(1)}, f32[22,40,128]{2,1,0:T(8,128)S(1)}, f32[20,40,128]{2,1,0:T(8,128)S(1)}) custom-call(f32[16,48,128]{2,1,0:T(8,128)S(1)} %get-tuple-element.53.g_wide, f32[40,8,128]{2,1,0:T(8,128)S(1)} %collective-permute-done.2.g_near, ...), custom_call_target="tpu_custom_call" | custom-call | tf_op jit(solution)/shard_map/pallas_call | solution.py:645
  17.7 13.6 %all_to_all.10.got = f32[32,8,128]{2,1,0:T(8,128)S(1)} all-to-all(f32[32,8,128]{2,1,0:T(8,128)S(1)} %get-tuple-element.74), channel_id=1, replica_groups=mesh['gx'=8,'gy'=4] {'gx','gy'}, dimensions={0} | all-to-all | bytes 262144 | tf_op jit(solution)/shard_map/all_to_all | solution.py:57
  31.4 3.1 %shard_map.43 = (f32[32,4,128]{2,1,0:T(4,128)S(1)}, f32[42,56,128]{2,1,0:T(8,128)S(1)}, f32[22,40,128]{2,1,0:T(8,128)S(1)}, f32[20,40,128]{2,1,0:T(8,128)S(1)}, ...) custom-call(f32[32,8,128]{2,1,0:T(8,128)S(1)} %all_to_all.10.got, ...), custom_call_target="tpu_custom_call" | custom-call | tf_op jit(solution)/shard_map/pallas_call | solution.py:645
  34.4 9.2 %all_to_all.11.got = f32[32,4,128]{2,1,0:T(4,128)S(1)} all-to-all(f32[32,4,128]{2,1,0:T(4,128)S(1)} %get-tuple-element.80), channel_id=1, replica_groups=mesh['gx'=8,'gy'=4] {'gx','gy'}, dimensions={0} | all-to-all | bytes 131072 | tf_op jit(solution)/shard_map/all_to_all | solution.py:57
  43.6 1.9 %shard_map.44 = f32[16,16,128]{2,1,0:T(8,128)} custom-call(f32[32,4,128]{2,1,0:T(4,128)S(1)} %all_to_all.11.got, f32[40,48,128]{2,1,0:T(8,128)S(1)} %get-tuple-element.75.g0, f32[42,56,128]{2,1,0:T(8,128)S(1)} %get-tuple-element.65.wx0, f32[40,56,128]{2,1,0:T(8,128)S(1)} %get-tuple-element.66.wy0, f32[40,56,128]{2,1,0:T(8,128)S(1)} %get-tuple-element.67.wz0, ...), custom_call_target="tpu_custom_call" | custom-call | tf_op jit(solution)/shard_map/pallas_call | solution.py:645
Async XLA Ops:
  1.0 4.5 %collective-permute-start.4 = (s32[12,16,128]{2,1,0:T(8,128)S(1)}, s32[12,16,128]{2,1,0:T(8,128)S(1)}, u32[]{:S(2)}, u32[]{:S(2)}) collective-permute-start(s32[12,16,128]{2,1,0:T(8,128)S(1)} %get-tuple-element.57), channel_id=1, source_target_pairs={{0,4},{1,5},{2,6},{3,7},{4,0},{5,1},{6,2},{7,3},{8,12},{9,13},{10,... | collective-permute-start | bytes 294920 | tf_op jit(solution)/shard_map/ppermute | solution.py:52
  1.5 5.3 %collective-permute-start.5 = (s32[12,16,128]{2,1,0:T(8,128)S(1)}, s32[12,16,128]{2,1,0:T(8,128)S(1)}, u32[]{:S(2)}, u32[]{:S(2)}) collective-permute-start(s32[12,16,128]{2,1,0:T(8,128)S(1)} %get-tuple-element.60), channel_id=1, source_target_pairs={{0,1},{1,0},{2,3},{3,2},{4,8},{5,9},{6,10},{7,11},{8,4},{9,5},{10,... | collective-permute-start | bytes 294920 | tf_op jit(solution)/shard_map/ppermute | solution.py:51
  4.2 5.4 %collective-permute-start = (f32[24,8,128]{2,1,0:T(8,128)S(1)}, f32[24,8,128]{2,1,0:T(8,128)S(1)}, u32[]{:S(2)}, u32[]{:S(2)}) collective-permute-start(f32[24,8,128]{2,1,0:T(8,128)S(1)} %get-tuple-element.51), channel_id=1, source_target_pairs={{0,1},{1,0},{2,3},{3,2},{4,5},{5,4},{6,7},{7,6},{8,9},{9,8},{10,11... | collective-permute-start | bytes 294920 | tf_op jit(solution)/shard_map/ppermute | solution.py:52
  4.3 5.4 %collective-permute-start.1 = (f32[24,8,128]{2,1,0:T(8,128)S(1)}, f32[24,8,128]{2,1,0:T(8,128)S(1)}, u32[]{:S(2)}, u32[]{:S(2)}) collective-permute-start(f32[24,8,128]{2,1,0:T(8,128)S(1)} %get-tuple-element.52), channel_id=1, source_target_pairs={{0,4},{1,2},{2,1},{3,7},{4,0},{5,6},{6,5},{7,3},{8,12},{9,10},{10,... | collective-permute-start | bytes 294920 | tf_op jit(solution)/shard_map/ppermute | solution.py:51
  5.5 0.7 %copy-start = (f32[16]{0:T(128)S(1)}, f32[16]{0:T(128)}, u32[]{:S(2)}) copy-start(f32[16]{0:T(128)} %param.5) | copy-start | bytes 196
  7.0 7.7 %collective-permute-start.6 = (f32[45,8,128]{2,1,0:T(8,128)S(1)}, f32[45,8,128]{2,1,0:T(8,128)S(1)}, u32[]{:S(2)}, u32[]{:S(2)}) collective-permute-start(f32[45,8,128]{2,1,0:T(8,128)S(1)} %get-tuple-element.63), channel_id=1, source_target_pairs={{0,1},{1,0},{2,3},{3,2},{4,5},{5,4},{6,7},{7,6},{8,9},{9,8},{10,11... | collective-permute-start | bytes 552968 | tf_op jit(solution)/shard_map/ppermute | solution.py:52
  9.5 5.2 %collective-permute-start.7 = (f32[45,8,128]{2,1,0:T(8,128)S(1)}, f32[45,8,128]{2,1,0:T(8,128)S(1)}, u32[]{:S(2)}, u32[]{:S(2)}) collective-permute-start(f32[45,8,128]{2,1,0:T(8,128)S(1)} %get-tuple-element.64), channel_id=1, source_target_pairs={{0,4},{1,2},{2,1},{3,7},{4,0},{5,6},{6,5},{7,3},{8,12},{9,10},{10,... | collective-permute-start | bytes 552968 | tf_op jit(solution)/shard_map/ppermute | solution.py:51
  9.7 6.0 %collective-permute-start.2 = (f32[40,8,128]{2,1,0:T(8,128)S(1)}, f32[40,8,128]{2,1,0:T(8,128)S(1)}, u32[]{:S(2)}, u32[]{:S(2)}) collective-permute-start(f32[40,8,128]{2,1,0:T(8,128)S(1)} %get-tuple-element.54), channel_id=1, source_target_pairs={{0,4},{1,5},{2,6},{3,7},{4,0},{5,1},{6,2},{7,3},{8,12},{9,13},{10,... | collective-permute-start | bytes 491528 | tf_op jit(solution)/shard_map/ppermute | solution.py:52
  10.2 6.3 %collective-permute-start.3 = (f32[40,8,128]{2,1,0:T(8,128)S(1)}, f32[40,8,128]{2,1,0:T(8,128)S(1)}, u32[]{:S(2)}, u32[]{:S(2)}) collective-permute-start(f32[40,8,128]{2,1,0:T(8,128)S(1)} %get-tuple-element.55), channel_id=1, source_target_pairs={{0,1},{1,0},{2,3},{3,2},{4,8},{5,9},{6,10},{7,11},{8,4},{9,5},{10,... | collective-permute-start | bytes 491528 | tf_op jit(solution)/shard_map/ppermute | solution.py:51

commit v5 on v4

--- a/solution.py
+++ b/solution.py
@@ -12,6 +12,7 @@
 NEAR = 8
 FAR = HALO - NEAR
 BASE = 8
+UNPACK = 8
 F32 = jnp.float32
 START_LIMIT = int(53.25 * 2**20)
 
@@ -209,6 +210,25 @@
     )
 
 
+def diamond(planes, rows, reach):
+    groups = {}
+    for distance in range(0, reach + 2, 2):
+        rest = reach - max(distance - 1, 0)
+        wide = -(-(rows - 2 * HALO + 2 * rest) // 8) * 8
+        top = HALO - (wide - (rows - 2 * HALO)) // 2
+        first, last = groups.get((top, wide), (distance, distance))
+        groups[(top, wide)] = (first, distance)
+    found = []
+    for (top, wide), (first, last) in groups.items():
+        if first == 0:
+            found.append((HALO - last, planes - 2 * HALO + 2 * last, top, wide))
+        else:
+            size = last - first + 2
+            found.append((HALO - last, size, top, wide))
+            found.append((planes - HALO + first - 2, size, top, wide))
+    return found
+
+
 def halve_rows(value, buffer):
     count, rows, _ = value.shape
     buffer[0:count, 0:rows, :] = value
@@ -244,9 +264,10 @@
         buffer[:, n * rows : (n + 1) * rows, :] = value
     used = rows * len(values)
     lane = lane_row(width)
+    first = (lane % span) * blocks
     packed = None
     for x in range(blocks):
-        picked = pick_lanes(buffer[x], (lane % span) * blocks)[:used]
+        picked = (pick_lanes(buffer[x], first) + pick_lanes(buffer[x], first + blocks // 2))[:used]
         packed = picked if packed is None else jnp.where(lanes_of(picked) // span == x, picked, packed)
     return packed
 
@@ -441,10 +462,12 @@
     rows = rows + 2 * HALO
 
     aH0, aWX0, aH1, aWX1 = (h0, 1, top), (wx0, 1, BASE), (h1, 1, BASE), (wx1, 1, BASE)
-    _, wx, wy, wz, total, inverse = faces(aH0, (0, planes, 0, rows), 1)
-    write(aWX0, 0, 0, wx)
-    for ref, value in ((wy0, wy), (wz0, wz), (tot0, total), (inv0, inverse)):
-        write((ref, 0, BASE), 0, 0, value)
+    for window in diamond(planes, rows, HALO - 1):
+        start, _, above_rows, _ = window
+        _, wx, wy, wz, total, inverse = faces(aH0, window, 1)
+        write(aWX0, start, above_rows, wx)
+        for ref, value in ((wy0, wy), (wz0, wz), (tot0, total), (inv0, inverse)):
+            write((ref, 0, BASE), start, above_rows, value)
     write(aH1, 0, 0, sum_blocks(read(aH0, 0, planes, 0, rows), buf0, 1) * (1.0 / 32.0))
 
     planes1, rows1 = planes // 2, -(-rows // 16) * 8
@@ -454,7 +477,7 @@
         write((ref, 0, BASE), 0, 0, value)
     low = HALO // 2
     own = read(aH1, low, planes1 - HALO, low, rows // 2 - HALO)
-    h2[...] = sum_blocks(own, buf0, 2) * (1.0 / 32.0)
+    h2[...] = halve_rows(halve_planes(own), buf0) * (1.0 / 32.0)
 
 
 def first_kernel(
@@ -475,10 +498,13 @@
     aG0, aV0, aV1, aG1 = (g0, 0, top), (v0, 1, BASE), (v1, 1, BASE), (g1, 0, BASE)
     w0 = (wx0, 1, BASE), (wy0, 0, BASE), (wz0, 0, BASE)
     w1 = (wx1, 1, BASE), (wy1, 0, BASE), (wz1, 0, BASE)
-    window = (0, planes, 0, rows)
-    write(aV0, 0, 0, read((inv0, 0, BASE), *window) * read(aG0, *window))
-    _, around = spread(aV0, w0, window, 1)
-    write(aG1, 0, 0, sum_blocks(KEEP * read(aG0, *window) + around, buf0, 1) * 0.125)
+    for window in diamond(planes, rows, HALO - 1):
+        write(aV0, window[0], window[2], read((inv0, 0, BASE), *window) * read(aG0, *window))
+    for window in diamond(planes, rows, HALO - 2):
+        start, _, above_rows, _ = window
+        _, around = spread(aV0, w0, window, 1)
+        r = KEEP * read(aG0, *window) + around
+        write(aG1, start // 2, above_rows // 2, sum_blocks(r, buf0.at[start // 2 :], 1) * 0.125)
 
     planes1, rows1 = planes // 2, -(-rows // 16) * 8
     window = (0, planes1, 0, rows1)
@@ -486,7 +512,7 @@
     low = HALO // 2
     window = (low, planes1 - HALO, low, rows // 2 - HALO)
     _, around = spread(aV1, w1, window, 2)
-    g2 = sum_blocks(KEEP * read(aG1, *window) + around, buf0, 2) * 0.125
+    g2 = halve_rows(halve_planes(KEEP * read(aG1, *window) + around), buf0) * 0.125
     send_to_all(packed, pack_block([g2, h2[...]], bufp))
 
 
@@ -499,14 +525,14 @@
     gy_count = lax.axis_size("gy")
     block2 = rows2 // gy_count
 
-    def unpack(i, carry):
-        for y in range(gy_count):
-            both = got[i * gy_count + y]
-            g2[i, y * block2 : (y + 1) * block2, :] = both[:block2]
-            h2[i, y * block2 : (y + 1) * block2, :] = both[block2:]
-        return carry
-
-    lax.fori_loop(0, count, unpack, 0)
+    def unpack(i):
+        for x in range(UNPACK):
+            for y in range(gy_count):
+                both = got[(i + x) * gy_count + y]
+                g2[i + x, y * block2 : (y + 1) * block2, :] = both[:block2]
+                h2[i + x, y * block2 : (y + 1) * block2, :] = both[block2:]
+
+    slabs(0, count, UNPACK, unpack)
 
     span = width // 4
     h = h2[...]
@@ -572,7 +598,8 @@
     write(aV1N, low - 2, low - 2, read(aINV1, *window) * read(aG1N, *window))
     window = (low, block1, low, block1)
     _, around = spread(aV1N, w1, window, 2)
-    send_to_all(packed, pack_block([sum_blocks(KEEP * read(aG1N, *window) + around, buf0, 2) * 0.125], bufp))
+    g2 = halve_rows(halve_planes(KEEP * read(aG1N, *window) + around), buf0) * 0.125
+    send_to_all(packed, pack_block([g2], bufp))
 
 
 def third_kernel(
@@ -583,12 +610,12 @@
     gy_count = lax.axis_size("gy")
     block2 = rows2 // gy_count
 
-    def unpack(i, carry):
-        for y in range(gy_count):
-            g2[i, y * block2 : (y + 1) * block2, :] = got[i * gy_count + y]
-        return carry
-
-    lax.fori_loop(0, count, unpack, 0)
+    def unpack(i):
+        for x in range(UNPACK):
+            for y in range(gy_count):
+                g2[i + x, y * block2 : (y + 1) * block2, :] = got[(i + x) * gy_count + y]
+
+    slabs(0, count, UNPACK, unpack)
     values = [ref[...] for ref in levels]
     spread_out(coarse_cycle(g2[...], values[:4], values[4:], buf2), wide, around, doubled, range(3, 9))
 

time: 45.7 us -> 45.4 us (level)
  no operation moved by 1% of the time
where the time goes in v5:
time: 45.4 us; the launch traced here: 45.2 us
  blocking collectives  22.7 us (50%)
  starting transfers between devices  10.4 us (23%)
  Pallas kernels  8.35 us (18%)
  waiting for transfers between devices  3.06 us (7%)
  local copies, waits for them, and re-layouts  0.66 us (1%)
    all_to_all x2, blocking collectives, everywhere(): return lax.all_to_all(copies, ('gx', 'gy'), 0, 0)  22.7 us
    pallas_call x7, Pallas kernels, kernel_call(): pl.pallas_call(body, out_shape=[jax.ShapeDtypeStruct(s, F32) for s in out...  7.34 us
    ppermute x4, starting transfers between devices, trade(): from_far = lax.ppermute(to_far, ('gx', 'gy'), route(axis, True))  6.7 us
    ppermute x4, starting transfers between devices, trade(): from_near = lax.ppermute(to_near, ('gx', 'gy'), route(axis, False))  3.66 us
    ppermute x4, waiting for transfers between devices, trade(): from_near = lax.ppermute(to_near, ('gx', 'gy'), route(axis, False))  1.8 us
    ppermute x4, waiting for transfers between devices, trade(): from_far = lax.ppermute(to_far, ('gx', 'gy'), route(axis, True))  1.27 us
    pallas_call x1, Pallas kernels, local(): pl.pallas_call(start_kernel, out_shape=outs, in_specs=[pl.BlockSpec(memor...  1 us
  transfers between devices with their start and end apart: 8, of which 3 were waited for; matrix products, arithmetic and copies ran while one was open for 0% of the time, Pallas kernels for 3%

profile of v5, /device:TPU:0, one launch (start us, length us, event | category | flops | bytes accessed | tf_op | source)
XLA Modules:
  0.0 45.2 jit_solution(14292606845705276468)
XLA Ops:
  0.0 1.0 %shard_map.37 = (f32[16,16,128]{2,1,0:T(8,128)S(1)}, s32[16,16,128]{2,1,0:T(8,128)S(1)}, s32[12,16,128]{2,1,0:T(8,128)S(1)}, s32[12,16,128]{2,1,0:T(8,128)S(1)},...) custom-call(f32[16,16,128]{2,1,0:T(8,128)} %right_hbm.1, s32[16,16,128]{2,1,0:T(8,128)} %material_hbm.1), custom_call_target="tpu_custom_call" | custom-call | tf_op jit(solution)/shard_map/pallas_call | solution.py:702
  1.0 0.5 %collective-permute-start.4 = (s32[12,16,128]{2,1,0:T(8,128)S(1)}, s32[12,16,128]{2,1,0:T(8,128)S(1)}, u32[]{:S(2)}, u32[]{:S(2)}) collective-permute-start(s32[12,16,128]{2,1,0:T(8,128)S(1)} %get-tuple-element.57), channel_id=1, source_target_pairs={{0,4},{1,5},{2,6},{3,7},{4,0},{5,1},{6,2},{7,3},{8,12},{9,13},{10,... | collective-permute-start | bytes 294920 | tf_op jit(solution)/shard_map/ppermute | solution.py:53
  1.5 2.6 %collective-permute-start.5 = (s32[12,16,128]{2,1,0:T(8,128)S(1)}, s32[12,16,128]{2,1,0:T(8,128)S(1)}, u32[]{:S(2)}, u32[]{:S(2)}) collective-permute-start(s32[12,16,128]{2,1,0:T(8,128)S(1)} %get-tuple-element.60), channel_id=1, source_target_pairs={{0,1},{1,0},{2,3},{3,2},{4,8},{5,9},{6,10},{7,11},{8,4},{9,5},{10,... | collective-permute-start | bytes 294920 | tf_op jit(solution)/shard_map/ppermute | solution.py:52
  4.2 0.1 collective-permute-start
  4.3 1.2 %collective-permute-start.1 = (f32[24,8,128]{2,1,0:T(8,128)S(1)}, f32[24,8,128]{2,1,0:T(8,128)S(1)}, u32[]{:S(2)}, u32[]{:S(2)}) collective-permute-start(f32[24,8,128]{2,1,0:T(8,128)S(1)} %get-tuple-element.52), channel_id=1, source_target_pairs={{0,4},{1,2},{2,1},{3,7},{4,0},{5,6},{6,5},{7,3},{8,12},{9,10},{10,... | collective-permute-start | bytes 294920 | tf_op jit(solution)/shard_map/ppermute | solution.py:52
  5.5 0.0 collective-permute-done.4.near
  5.5 0.0 copy-start
  5.5 0.7 %copy-done = f32[16]{0:T(128)S(1)} copy-done((f32[16]{0:T(128)S(1)}, f32[16]{0:T(128)}, u32[]{:S(2)}) %copy-start) | copy-done | bytes 88
  6.2 0.2 shard_map.39
  6.4 0.4 collective-permute-done.5.far
  6.8 0.2 shard_map.40
  7.0 2.6 %collective-permute-start.6 = (f32[45,8,128]{2,1,0:T(8,128)S(1)}, f32[45,8,128]{2,1,0:T(8,128)S(1)}, u32[]{:S(2)}, u32[]{:S(2)}) collective-permute-start(f32[45,8,128]{2,1,0:T(8,128)S(1)} %get-tuple-element.63), channel_id=1, source_target_pairs={{0,1},{1,0},{2,3},{3,2},{4,5},{5,4},{6,7},{7,6},{8,9},{9,8},{10,11... | collective-permute-start | bytes 552968 | tf_op jit(solution)/shard_map/ppermute | solution.py:53
  9.5 0.1 collective-permute-start.7
  9.6 0.0 collective-permute-done.near
  9.6 0.0 collective-permute-done.1.far
  9.6 0.1 shard_map.38
  9.7 0.5 %collective-permute-start.2 = (f32[40,8,128]{2,1,0:T(8,128)S(1)}, f32[40,8,128]{2,1,0:T(8,128)S(1)}, u32[]{:S(2)}, u32[]{:S(2)}) collective-permute-start(f32[40,8,128]{2,1,0:T(8,128)S(1)} %get-tuple-element.54), channel_id=1, source_target_pairs={{0,4},{1,5},{2,6},{3,7},{4,0},{5,1},{6,2},{7,3},{8,12},{9,13},{10,... | collective-permute-start | bytes 491528 | tf_op jit(solution)/shard_map/ppermute | solution.py:53
  10.2 2.7 %collective-permute-start.3 = (f32[40,8,128]{2,1,0:T(8,128)S(1)}, f32[40,8,128]{2,1,0:T(8,128)S(1)}, u32[]{:S(2)}, u32[]{:S(2)}) collective-permute-start(f32[40,8,128]{2,1,0:T(8,128)S(1)} %get-tuple-element.55), channel_id=1, source_target_pairs={{0,1},{1,0},{2,3},{3,2},{4,8},{5,9},{6,10},{7,11},{8,4},{9,5},{10,... | collective-permute-start | bytes 491528 | tf_op jit(solution)/shard_map/ppermute | solution.py:52
  12.9 1.8 %collective-permute-done.6.k_near = f32[45,8,128]{2,1,0:T(8,128)S(1)} collective-permute-done((f32[45,8,128]{2,1,0:T(8,128)S(1)}, f32[45,8,128]{2,1,0:T(8,128)S(1)}, u32[]{:S(2)}, u32[]{:S(2)}) %collective-permute-start.6) | collective-permute-done | bytes 184352 | tf_op jit(solution)/shard_map/ppermute | solution.py:53
  14.7 0.0 collective-permute-done.7.k_far
  14.7 0.9 %shard_map.41 = (f32[42,56,128]{2,1,0:T(8,128)S(1)}, f32[40,56,128]{2,1,0:T(8,128)S(1)}, f32[40,56,128]{2,1,0:T(8,128)S(1)}, f32[40,56,128]{2,1,0:T(8,128)S(1)},...) custom-call(f32[40,16,128]{2,1,0:T(8,128)S(1)} %get-tuple-element.62, ...), custom_call_target="tpu_custom_call" | custom-call | bytes 8388608 | tf_op jit(solution)/shard_map/pallas_call | solution.py:672
  15.6 0.0 collective-permute-done.2.g_near
  15.6 0.9 %collective-permute-done.3.g_far = f32[40,8,128]{2,1,0:T(8,128)S(1)} collective-permute-done((f32[40,8,128]{2,1,0:T(8,128)S(1)}, f32[40,8,128]{2,1,0:T(8,128)S(1)}, u32[]{:S(2)}, u32[]{:S(2)}) %collective-permute-start.3) | collective-permute-done | bytes 163872 | tf_op jit(solution)/shard_map/ppermute | solution.py:52
  16.4 1.1 %shard_map.42 = (f32[32,8,128]{2,1,0:T(8,128)S(1)}, f32[40,48,128]{2,1,0:T(8,128)S(1)}, f32[42,56,128]{2,1,0:T(8,128)S(1)}, f32[22,40,128]{2,1,0:T(8,128)S(1)}, f32[20,40,128]{2,1,0:T(8,128)S(1)}) custom-call(f32[16,48,128]{2,1,0:T(8,128)S(1)} %get-tuple-element.53.g_wide, f32[40,8,128]{2,1,0:T(8,128)S(1)} %collective-permute-done.2.g_near, ...), custom_call_target="tpu_custom_call" | custom-call | tf_op jit(solution)/shard_map/pallas_call | solution.py:672
  17.6 13.5 %all_to_all.10.got = f32[32,8,128]{2,1,0:T(8,128)S(1)} all-to-all(f32[32,8,128]{2,1,0:T(8,128)S(1)} %get-tuple-element.74), channel_id=1, replica_groups=mesh['gx'=8,'gy'=4] {'gx','gy'}, dimensions={0} | all-to-all | bytes 262144 | tf_op jit(solution)/shard_map/all_to_all | solution.py:58
  31.1 3.0 %shard_map.43 = (f32[32,4,128]{2,1,0:T(4,128)S(1)}, f32[42,56,128]{2,1,0:T(8,128)S(1)}, f32[22,40,128]{2,1,0:T(8,128)S(1)}, f32[20,40,128]{2,1,0:T(8,128)S(1)}, ...) custom-call(f32[32,8,128]{2,1,0:T(8,128)S(1)} %all_to_all.10.got, ...), custom_call_target="tpu_custom_call" | custom-call | tf_op jit(solution)/shard_map/pallas_call | solution.py:672
  34.1 9.2 %all_to_all.11.got = f32[32,4,128]{2,1,0:T(4,128)S(1)} all-to-all(f32[32,4,128]{2,1,0:T(4,128)S(1)} %get-tuple-element.80), channel_id=1, replica_groups=mesh['gx'=8,'gy'=4] {'gx','gy'}, dimensions={0} | all-to-all | bytes 131072 | tf_op jit(solution)/shard_map/all_to_all | solution.py:58
  43.3 1.9 %shard_map.44 = f32[16,16,128]{2,1,0:T(8,128)} custom-call(f32[32,4,128]{2,1,0:T(4,128)S(1)} %all_to_all.11.got, f32[40,48,128]{2,1,0:T(8,128)S(1)} %get-tuple-element.75.g0, f32[42,56,128]{2,1,0:T(8,128)S(1)} %get-tuple-element.65.wx0, f32[40,56,128]{2,1,0:T(8,128)S(1)} %get-tuple-element.66.wy0, f32[40,56,128]{2,1,0:T(8,128)S(1)} %get-tuple-element.67.wz0, ...), custom_call_target="tpu_custom_call" | custom-call | tf_op jit(solution)/shard_map/pallas_call | solution.py:672
Async XLA Ops:
  1.0 4.5 %collective-permute-start.4 = (s32[12,16,128]{2,1,0:T(8,128)S(1)}, s32[12,16,128]{2,1,0:T(8,128)S(1)}, u32[]{:S(2)}, u32[]{:S(2)}) collective-permute-start(s32[12,16,128]{2,1,0:T(8,128)S(1)} %get-tuple-element.57), channel_id=1, source_target_pairs={{0,4},{1,5},{2,6},{3,7},{4,0},{5,1},{6,2},{7,3},{8,12},{9,13},{10,... | collective-permute-start | bytes 294920 | tf_op jit(solution)/shard_map/ppermute | solution.py:53
  1.5 5.3 %collective-permute-start.5 = (s32[12,16,128]{2,1,0:T(8,128)S(1)}, s32[12,16,128]{2,1,0:T(8,128)S(1)}, u32[]{:S(2)}, u32[]{:S(2)}) collective-permute-start(s32[12,16,128]{2,1,0:T(8,128)S(1)} %get-tuple-element.60), channel_id=1, source_target_pairs={{0,1},{1,0},{2,3},{3,2},{4,8},{5,9},{6,10},{7,11},{8,4},{9,5},{10,... | collective-permute-start | bytes 294920 | tf_op jit(solution)/shard_map/ppermute | solution.py:52
  4.2 5.4 %collective-permute-start = (f32[24,8,128]{2,1,0:T(8,128)S(1)}, f32[24,8,128]{2,1,0:T(8,128)S(1)}, u32[]{:S(2)}, u32[]{:S(2)}) collective-permute-start(f32[24,8,128]{2,1,0:T(8,128)S(1)} %get-tuple-element.51), channel_id=1, source_target_pairs={{0,1},{1,0},{2,3},{3,2},{4,5},{5,4},{6,7},{7,6},{8,9},{9,8},{10,11... | collective-permute-start | bytes 294920 | tf_op jit(solution)/shard_map/ppermute | solution.py:53
  4.3 5.4 %collective-permute-start.1 = (f32[24,8,128]{2,1,0:T(8,128)S(1)}, f32[24,8,128]{2,1,0:T(8,128)S(1)}, u32[]{:S(2)}, u32[]{:S(2)}) collective-permute-start(f32[24,8,128]{2,1,0:T(8,128)S(1)} %get-tuple-element.52), channel_id=1, source_target_pairs={{0,4},{1,2},{2,1},{3,7},{4,0},{5,6},{6,5},{7,3},{8,12},{9,10},{10,... | collective-permute-start | bytes 294920 | tf_op jit(solution)/shard_map/ppermute | solution.py:52
  5.5 0.7 %copy-start = (f32[16]{0:T(128)S(1)}, f32[16]{0:T(128)}, u32[]{:S(2)}) copy-start(f32[16]{0:T(128)} %param.5) | copy-start | bytes 196
  7.0 7.7 %collective-permute-start.6 = (f32[45,8,128]{2,1,0:T(8,128)S(1)}, f32[45,8,128]{2,1,0:T(8,128)S(1)}, u32[]{:S(2)}, u32[]{:S(2)}) collective-permute-start(f32[45,8,128]{2,1,0:T(8,128)S(1)} %get-tuple-element.63), channel_id=1, source_target_pairs={{0,1},{1,0},{2,3},{3,2},{4,5},{5,4},{6,7},{7,6},{8,9},{9,8},{10,11... | collective-permute-start | bytes 552968 | tf_op jit(solution)/shard_map/ppermute | solution.py:53
  9.5 5.2 %collective-permute-start.7 = (f32[45,8,128]{2,1,0:T(8,128)S(1)}, f32[45,8,128]{2,1,0:T(8,128)S(1)}, u32[]{:S(2)}, u32[]{:S(2)}) collective-permute-start(f32[45,8,128]{2,1,0:T(8,128)S(1)} %get-tuple-element.64), channel_id=1, source_target_pairs={{0,4},{1,2},{2,1},{3,7},{4,0},{5,6},{6,5},{7,3},{8,12},{9,10},{10,... | collective-permute-start | bytes 552968 | tf_op jit(solution)/shard_map/ppermute | solution.py:52
  9.7 5.9 %collective-permute-start.2 = (f32[40,8,128]{2,1,0:T(8,128)S(1)}, f32[40,8,128]{2,1,0:T(8,128)S(1)}, u32[]{:S(2)}, u32[]{:S(2)}) collective-permute-start(f32[40,8,128]{2,1,0:T(8,128)S(1)} %get-tuple-element.54), channel_id=1, source_target_pairs={{0,4},{1,5},{2,6},{3,7},{4,0},{5,1},{6,2},{7,3},{8,12},{9,13},{10,... | collective-permute-start | bytes 491528 | tf_op jit(solution)/shard_map/ppermute | solution.py:53
  10.2 6.3 %collective-permute-start.3 = (f32[40,8,128]{2,1,0:T(8,128)S(1)}, f32[40,8,128]{2,1,0:T(8,128)S(1)}, u32[]{:S(2)}, u32[]{:S(2)}) collective-permute-start(f32[40,8,128]{2,1,0:T(8,128)S(1)} %get-tuple-element.55), channel_id=1, source_target_pairs={{0,1},{1,0},{2,3},{3,2},{4,8},{5,9},{6,10},{7,11},{8,4},{9,5},{10,... | collective-permute-start | bytes 491528 | tf_op jit(solution)/shard_map/ppermute | solution.py:52

commit v6 on v5

--- a/solution.py
+++ b/solution.py
@@ -14,7 +14,6 @@
 BASE = 8
 UNPACK = 8
 F32 = jnp.float32
-START_LIMIT = int(53.25 * 2**20)
 
 
 def near_partner(index, count):
@@ -337,10 +336,6 @@
     return to_near, to_far
 
 
-def whole_strips(planes):
-    return (0, planes), (0, 0, 0), (0, planes // 2, planes // 2)
-
-
 def diamond_strips(planes):
     full = (HALO - NEAR + 1, planes - HALO + NEAR - 1)
     far = HALO - FAR + 1
@@ -379,32 +374,13 @@
             at += count
 
 
-def start_kernel(
-    right_hbm, material_hbm, right, material, k_near, k_far, g_near, g_far, arrived,
-):
-    planes, rows, _ = right.shape
-    copies = [
-        pltpu.make_async_copy(material_hbm, material, arrived.at[0]),
-        pltpu.make_async_copy(right_hbm, right, arrived.at[1]),
-    ]
-    for copy in copies:
-        copy.start()
-    copies[0].wait()
-    odd = is_odd("gx")
-    k_near[...] = material[pl.ds(jnp.where(odd, 0, planes - HALO), HALO)]
-    k_far[...] = material[pl.ds(jnp.where(odd, planes - HALO, 0), HALO)]
-    copies[1].wait()
-    to_near, to_far = row_starts("gy", rows)
-    strips = whole_strips(planes)
-    pack_rows(right, to_near, strips, g_near)
-    pack_rows(right, to_far, strips, g_far)
-
-
-def table_kernel(cond, material, near, table, h, h_near):
+def own_kernel(cond, material, right_in, near, table, h, h_near, right):
     table[...] = jnp.zeros(table.shape, F32)
     table[0:1, 0 : cond.shape[1]] = 0.5 * cond[...]
     h[...] = look_up(material[...], table)
-    h_near[...] = look_up(near[...], table)
+    first = jnp.where(is_odd("gx"), near.shape[0] - HALO, 0)
+    h_near[...] = look_up(near[pl.ds(first, HALO)], table)
+    right[...] = right_in[...]
 
 
 def look_up(ids, table):
@@ -416,7 +392,8 @@
 
 def k_kernel(h, h_near, far, table, wide, k_near, k_far):
     block = h.shape[0]
-    h_far = look_up(far[...], table)
+    first = jnp.where(is_odd("gx"), 0, block - HALO)
+    h_far = look_up(far[pl.ds(first, HALO)], table)
     wide[0:HALO] = below(h_near[...], h_far, "gx")
     wide[HALO : HALO + block] = h[...]
     wide[HALO + block :] = above(h_near[...], h_far, "gx")
@@ -440,7 +417,8 @@
     block, rows, _ = right.shape
     top = BASE // 2
     wide[:, top + HALO : top + HALO + rows, :] = right[...]
-    unpack_rows(wide, 0, top + HALO, top + HALO + rows, whole_strips(block), near, far)
+    wide[:, top : top + HALO, :] = below(near[:, rows - HALO :], far[:, rows - HALO :], "gy")
+    wide[:, top + HALO + rows : top + 2 * HALO + rows, :] = above(near[:, :HALO], far[:, :HALO], "gy")
     odd = is_odd("gx")
     strips, _ = plane_strips(rows + 2 * HALO)
     for distance, cut, tiles, at in strips:
@@ -660,7 +638,7 @@
     slabs(HALO, planes - HALO, size, sweep)
 
 
-def kernel_call(body, outs, scratch, args, cost=None):
+def kernel_call(body, outs, scratch, args):
     def size(shape):
         total = 4
         for length in shape:
@@ -676,7 +654,6 @@
         out_specs=[pl.BlockSpec(memory_space=pltpu.VMEM)] * len(outs),
         scratch_shapes=[pltpu.VMEM(s, F32) for s in scratch],
         compiler_params=pltpu.CompilerParams(vmem_limit_bytes=limit),
-        cost_estimate=cost,
     )(*args)
 
 
@@ -691,26 +668,13 @@
     X1, Y1 = X // 2, -(-Y // 16) * 8 + 2 * BASE
     xb, yb = bx // 4, by // 4
 
-    strip = (strip_tiles(whole_strips(bx)), NEAR, bz)
-    def ints(*shape):
-        return jax.ShapeDtypeStruct(shape, jnp.int32)
-
-    def floats(*shape):
-        return jax.ShapeDtypeStruct(shape, F32)
-
-    outs = [floats(bx, by, bz), ints(bx, by, bz), ints(HALO, by, bz), ints(HALO, by, bz), floats(*strip), floats(*strip)]
-    right, material, k_near, k_far, g_near, g_far = pl.pallas_call(
-        start_kernel,
-        out_shape=outs,
-        in_specs=[pl.BlockSpec(memory_space=pl.ANY)] * 2,
-        out_specs=[pl.BlockSpec(memory_space=pltpu.VMEM)] * len(outs),
-        scratch_shapes=[pltpu.SemaphoreType.DMA((2,))],
-        compiler_params=pltpu.CompilerParams(vmem_limit_bytes=START_LIMIT),
-    )(right_side, material)
-    k_near, k_far = trade(k_near, k_far, "gx")
-    g_near, g_far = trade(g_near, g_far, "gy")
-    table, h, h_near = kernel_call(
-        table_kernel, [(8, bz), (bx, by, bz), (HALO, by, bz)], [], [conductivity[None], material, k_near]
+    k_near, k_far = trade(material, material, "gx")
+    g_near, g_far = trade(right_side, right_side, "gy")
+    table, h, h_near, right = kernel_call(
+        own_kernel,
+        [(8, bz), (bx, by, bz), (HALO, by, bz), (bx, by, bz)],
+        [],
+        [conductivity[None], material, right_side, k_near],
     )
     strip = (plane_strips(Y)[1], 8, bz)
     g_wide, g_near, g_far = kernel_call(
@@ -729,7 +693,6 @@
         [pad0, full0, full0, full0, full0, pad1, full1, full1, full1, (xb, yb, bz)],
         [(X + 2, YA, bz), pad1, (X1, Y, bz)],
         [k_wide, k_near, k_far],
-        pl.CostEstimate(flops=0, bytes_accessed=8 << 20, transcendentals=0),
     )
     packed, g0, v0, v1, g1 = kernel_call(
         first_kernel,

time: 45.4 us -> 45.3 us (level)
  local copies, waits for them, and re-layouts: 0.66 us -> 2.46 us
  starting transfers between devices: 10.4 us -> 9.36 us
  Pallas kernels: 8.35 us -> 7.39 us
  waiting for transfers between devices: 3.06 us -> 3.66 us
  blocking collectives: 22.7 us -> 22.1 us
    unnamed x2 -> x6, local copies, waits for them, and re-layouts: 0.66 us -> 2.46 us
    ppermute x4, starting transfers between devices: 6.7 us -> 5.65 us  [trade(): from_far = lax.ppermute(to_far, ('gx', 'gy'), route(axis, True))]
    pallas_call x1 -> x0, Pallas kernels: 1 us -> none  [local(): pl.pallas_call(start_kernel, out_shape=outs, in_specs=[pl.BlockSpec(memor...]
    ppermute x4, waiting for transfers between devices: 1.8 us -> 2.8 us  [trade(): from_near = lax.ppermute(to_near, ('gx', 'gy'), route(axis, False))]
    all_to_all x2, blocking collectives: 22.7 us -> 22.1 us  [everywhere(): return lax.all_to_all(copies, ('gx', 'gy'), 0, 0)]
where the time goes in v6:
time: 45.3 us; the launch traced here: 45.1 us
  blocking collectives  22.1 us (49%)
  starting transfers between devices  9.36 us (21%)
  Pallas kernels  7.39 us (16%)
  waiting for transfers between devices  3.66 us (8%)
  local copies, waits for them, and re-layouts  2.46 us (5%)
    all_to_all x2, blocking collectives, everywhere(): return lax.all_to_all(copies, ('gx', 'gy'), 0, 0)  22.1 us
    pallas_call x7, Pallas kernels, kernel_call(): pl.pallas_call(body, out_shape=[jax.ShapeDtypeStruct(s, F32) for s in out...  7.39 us
    ppermute x4, starting transfers between devices, trade(): from_far = lax.ppermute(to_far, ('gx', 'gy'), route(axis, True))  5.65 us
    ppermute x4, starting transfers between devices, trade(): from_near = lax.ppermute(to_near, ('gx', 'gy'), route(axis, False))  3.72 us
    ppermute x4, waiting for transfers between devices, trade(): from_near = lax.ppermute(to_near, ('gx', 'gy'), route(axis, False))  2.8 us
    unnamed x6, local copies, waits for them, and re-layouts  2.46 us
  transfers between devices with their start and end apart: 8, of which 3 were waited for; matrix products, arithmetic and copies ran while one was open for 0% of the time, Pallas kernels for 3%

profile of v6, /device:TPU:0, one launch (start us, length us, event | category | flops | bytes accessed | tf_op | source)
XLA Modules:
  0.0 45.1 jit_solution(4507876142048499544)
XLA Ops:
  0.0 0.5 %collective-permute-start = (s32[16,16,128]{2,1,0:T(8,128)}, s32[16,16,128]{2,1,0:T(8,128)S(1)}, u32[]{:S(2)}, u32[]{:S(2)}) collective-permute-start(s32[16,16,128]{2,1,0:T(8,128)} %material.1), channel_id=1, source_target_pairs={{0,4},{1,5},{2,6},{3,7},{4,0},{5,1},{6,2},{7,3},{8,12},{9,13},{10,... | collective-permute-start | bytes 393224 | tf_op jit(solution)/shard_map/ppermute | solution.py:52
  0.5 2.6 %collective-permute-start.5 = (s32[16,16,128]{2,1,0:T(8,128)}, s32[16,16,128]{2,1,0:T(8,128)S(1)}, u32[]{:S(2)}, u32[]{:S(2)}) collective-permute-start(s32[16,16,128]{2,1,0:T(8,128)} %material.1), channel_id=1, source_target_pairs={{0,1},{1,0},{2,3},{3,2},{4,8},{5,9},{6,10},{7,11},{8,4},{9,5},{10,... | collective-permute-start | bytes 393224 | tf_op jit(solution)/shard_map/ppermute | solution.py:51
  3.0 0.0 collective-permute-start.2
  3.1 3.1 %collective-permute-start.1 = (f32[16,16,128]{2,1,0:T(8,128)}, f32[16,16,128]{2,1,0:T(8,128)S(1)}, u32[]{:S(2)}, u32[]{:S(2)}) collective-permute-start(f32[16,16,128]{2,1,0:T(8,128)} %right_in.1), channel_id=1, source_target_pairs={{0,1},{1,0},{2,3},{3,2},{4,5},{5,4},{6,7},{7,6},{8,9},{9,8},{10,11... | collective-permute-start | bytes 393224 | tf_op jit(solution)/shard_map/ppermute | solution.py:52
  6.2 0.0 collective-permute-done.near
  6.2 0.0 copy-start
  6.2 0.9 %copy-done = s32[16,16,128]{2,1,0:T(8,128)S(1)} copy-done((s32[16,16,128]{2,1,0:T(8,128)S(1)}, s32[16,16,128]{2,1,0:T(8,128)}, u32[]{:S(2)}) %copy-start) | copy-done | bytes 131096
  7.1 0.0 copy-start.1
  7.1 0.9 %copy-done.1 = f32[16,16,128]{2,1,0:T(8,128)S(1)} copy-done((f32[16,16,128]{2,1,0:T(8,128)S(1)}, f32[16,16,128]{2,1,0:T(8,128)}, u32[]{:S(2)}) %copy-start.1) | copy-done | bytes 131096
  8.0 0.0 copy-start.2
  8.0 0.7 %copy-done.2 = f32[16]{0:T(128)S(1)} copy-done((f32[16]{0:T(128)S(1)}, f32[16]{0:T(128)}, u32[]{:S(2)}) %copy-start.2) | copy-done | bytes 88
  8.7 0.2 shard_map.37
  8.9 0.0 collective-permute-done.5.far
  8.9 0.2 shard_map.39
  9.1 0.1 collective-permute-start.6
  9.1 0.4 collective-permute-start.7
  9.5 0.0 collective-permute-done.2.far
  9.5 0.3 collective-permute-done.1.near
  9.8 0.1 shard_map.38
  9.9 0.1 collective-permute-start.3
  10.0 2.7 %collective-permute-start.4 = (f32[40,8,128]{2,1,0:T(8,128)S(1)}, f32[40,8,128]{2,1,0:T(8,128)S(1)}, u32[]{:S(2)}, u32[]{:S(2)}) collective-permute-start(f32[40,8,128]{2,1,0:T(8,128)S(1)} %get-tuple-element.48), channel_id=1, source_target_pairs={{0,1},{1,0},{2,3},{3,2},{4,8},{5,9},{6,10},{7,11},{8,4},{9,5},{10,... | collective-permute-start | bytes 491528 | tf_op jit(solution)/shard_map/ppermute | solution.py:51
  12.7 2.5 %collective-permute-done.6.k_near = f32[45,8,128]{2,1,0:T(8,128)S(1)} collective-permute-done((f32[45,8,128]{2,1,0:T(8,128)S(1)}, f32[45,8,128]{2,1,0:T(8,128)S(1)}, u32[]{:S(2)}, u32[]{:S(2)}) %collective-permute-start.6) | collective-permute-done | bytes 184352 | tf_op jit(solution)/shard_map/ppermute | solution.py:52
  15.1 0.0 collective-permute-done.7.k_far
  15.1 0.9 %shard_map.40 = (f32[42,56,128]{2,1,0:T(8,128)S(1)}, f32[40,56,128]{2,1,0:T(8,128)S(1)}, f32[40,56,128]{2,1,0:T(8,128)S(1)}, f32[40,56,128]{2,1,0:T(8,128)S(1)},...) custom-call(f32[40,16,128]{2,1,0:T(8,128)S(1)} %get-tuple-element.52, ...), custom_call_target="tpu_custom_call" | custom-call | tf_op jit(solution)/shard_map/pallas_call | solution.py:650
  16.0 0.0 collective-permute-done.3.g_near
  16.0 0.9 %collective-permute-done.4.g_far = f32[40,8,128]{2,1,0:T(8,128)S(1)} collective-permute-done((f32[40,8,128]{2,1,0:T(8,128)S(1)}, f32[40,8,128]{2,1,0:T(8,128)S(1)}, u32[]{:S(2)}, u32[]{:S(2)}) %collective-permute-start.4) | collective-permute-done | bytes 163872 | tf_op jit(solution)/shard_map/ppermute | solution.py:51
  16.9 1.1 %shard_map.41 = (f32[32,8,128]{2,1,0:T(8,128)S(1)}, f32[40,48,128]{2,1,0:T(8,128)S(1)}, f32[42,56,128]{2,1,0:T(8,128)S(1)}, f32[22,40,128]{2,1,0:T(8,128)S(1)}, f32[20,40,128]{2,1,0:T(8,128)S(1)}) custom-call(f32[16,48,128]{2,1,0:T(8,128)S(1)} %get-tuple-element.46.g_wide, f32[40,8,128]{2,1,0:T(8,128)S(1)} %collective-permute-done.3.g_near, ...), custom_call_target="tpu_custom_call" | custom-call | tf_op jit(solution)/shard_map/pallas_call | solution.py:650
  18.0 13.0 %all_to_all.10.got = f32[32,8,128]{2,1,0:T(8,128)S(1)} all-to-all(f32[32,8,128]{2,1,0:T(8,128)S(1)} %get-tuple-element.64), channel_id=1, replica_groups=mesh['gx'=8,'gy'=4] {'gx','gy'}, dimensions={0} | all-to-all | bytes 262144 | tf_op jit(solution)/shard_map/all_to_all | solution.py:57
  31.0 3.0 %shard_map.42 = (f32[32,4,128]{2,1,0:T(4,128)S(1)}, f32[42,56,128]{2,1,0:T(8,128)S(1)}, f32[22,40,128]{2,1,0:T(8,128)S(1)}, f32[20,40,128]{2,1,0:T(8,128)S(1)}, ...) custom-call(f32[32,8,128]{2,1,0:T(8,128)S(1)} %all_to_all.10.got, ...), custom_call_target="tpu_custom_call" | custom-call | tf_op jit(solution)/shard_map/pallas_call | solution.py:650
  34.0 9.2 %all_to_all.11.got = f32[32,4,128]{2,1,0:T(4,128)S(1)} all-to-all(f32[32,4,128]{2,1,0:T(4,128)S(1)} %get-tuple-element.70), channel_id=1, replica_groups=mesh['gx'=8,'gy'=4] {'gx','gy'}, dimensions={0} | all-to-all | bytes 131072 | tf_op jit(solution)/shard_map/all_to_all | solution.py:57
  43.2 1.9 %shard_map.43 = f32[16,16,128]{2,1,0:T(8,128)} custom-call(f32[32,4,128]{2,1,0:T(4,128)S(1)} %all_to_all.11.got, f32[40,48,128]{2,1,0:T(8,128)S(1)} %get-tuple-element.65.g0, f32[42,56,128]{2,1,0:T(8,128)S(1)} %get-tuple-element.55.wx0, f32[40,56,128]{2,1,0:T(8,128)S(1)} %get-tuple-element.56.wy0, f32[40,56,128]{2,1,0:T(8,128)S(1)} %get-tuple-element.57.wz0, ...), custom_call_target="tpu_custom_call" | custom-call | tf_op jit(solution)/shard_map/pallas_call | solution.py:650
Async XLA Ops:
  0.0 6.2 %collective-permute-start = (s32[16,16,128]{2,1,0:T(8,128)}, s32[16,16,128]{2,1,0:T(8,128)S(1)}, u32[]{:S(2)}, u32[]{:S(2)}) collective-permute-start(s32[16,16,128]{2,1,0:T(8,128)} %material.1), channel_id=1, source_target_pairs={{0,4},{1,5},{2,6},{3,7},{4,0},{5,1},{6,2},{7,3},{8,12},{9,13},{10,... | collective-permute-start | bytes 393224 | tf_op jit(solution)/shard_map/ppermute | solution.py:52
  0.5 8.4 %collective-permute-start.5 = (s32[16,16,128]{2,1,0:T(8,128)}, s32[16,16,128]{2,1,0:T(8,128)S(1)}, u32[]{:S(2)}, u32[]{:S(2)}) collective-permute-start(s32[16,16,128]{2,1,0:T(8,128)} %material.1), channel_id=1, source_target_pairs={{0,1},{1,0},{2,3},{3,2},{4,8},{5,9},{6,10},{7,11},{8,4},{9,5},{10,... | collective-permute-start | bytes 393224 | tf_op jit(solution)/shard_map/ppermute | solution.py:51
  3.0 6.5 %collective-permute-start.2 = (f32[16,16,128]{2,1,0:T(8,128)}, f32[16,16,128]{2,1,0:T(8,128)S(1)}, u32[]{:S(2)}, u32[]{:S(2)}) collective-permute-start(f32[16,16,128]{2,1,0:T(8,128)} %right_in.1), channel_id=1, source_target_pairs={{0,4},{1,2},{2,1},{3,7},{4,0},{5,6},{6,5},{7,3},{8,12},{9,10},{10,... | collective-permute-start | bytes 393224 | tf_op jit(solution)/shard_map/ppermute | solution.py:51
  3.1 6.8 %collective-permute-start.1 = (f32[16,16,128]{2,1,0:T(8,128)}, f32[16,16,128]{2,1,0:T(8,128)S(1)}, u32[]{:S(2)}, u32[]{:S(2)}) collective-permute-start(f32[16,16,128]{2,1,0:T(8,128)} %right_in.1), channel_id=1, source_target_pairs={{0,1},{1,0},{2,3},{3,2},{4,5},{5,4},{6,7},{7,6},{8,9},{9,8},{10,11... | collective-permute-start | bytes 393224 | tf_op jit(solution)/shard_map/ppermute | solution.py:52
  6.2 0.9 %copy-start = (s32[16,16,128]{2,1,0:T(8,128)S(1)}, s32[16,16,128]{2,1,0:T(8,128)}, u32[]{:S(2)}) copy-start(s32[16,16,128]{2,1,0:T(8,128)} %material.1) | copy-start | bytes 393220
  7.1 0.9 %copy-start.1 = (f32[16,16,128]{2,1,0:T(8,128)S(1)}, f32[16,16,128]{2,1,0:T(8,128)}, u32[]{:S(2)}) copy-start(f32[16,16,128]{2,1,0:T(8,128)} %right_in.1) | copy-start | bytes 393220
  8.0 0.7 %copy-start.2 = (f32[16]{0:T(128)S(1)}, f32[16]{0:T(128)}, u32[]{:S(2)}) copy-start(f32[16]{0:T(128)} %param.5) | copy-start | bytes 196
  9.1 6.1 %collective-permute-start.6 = (f32[45,8,128]{2,1,0:T(8,128)S(1)}, f32[45,8,128]{2,1,0:T(8,128)S(1)}, u32[]{:S(2)}, u32[]{:S(2)}) collective-permute-start(f32[45,8,128]{2,1,0:T(8,128)S(1)} %get-tuple-element.53), channel_id=1, source_target_pairs={{0,1},{1,0},{2,3},{3,2},{4,5},{5,4},{6,7},{7,6},{8,9},{9,8},{10,11... | collective-permute-start | bytes 552968 | tf_op jit(solution)/shard_map/ppermute | solution.py:52
  9.1 6.0 %collective-permute-start.7 = (f32[45,8,128]{2,1,0:T(8,128)S(1)}, f32[45,8,128]{2,1,0:T(8,128)S(1)}, u32[]{:S(2)}, u32[]{:S(2)}) collective-permute-start(f32[45,8,128]{2,1,0:T(8,128)S(1)} %get-tuple-element.54), channel_id=1, source_target_pairs={{0,4},{1,2},{2,1},{3,7},{4,0},{5,6},{6,5},{7,3},{8,12},{9,10},{10,... | collective-permute-start | bytes 552968 | tf_op jit(solution)/shard_map/ppermute | solution.py:51
  9.9 6.1 %collective-permute-start.3 = (f32[40,8,128]{2,1,0:T(8,128)S(1)}, f32[40,8,128]{2,1,0:T(8,128)S(1)}, u32[]{:S(2)}, u32[]{:S(2)}) collective-permute-start(f32[40,8,128]{2,1,0:T(8,128)S(1)} %get-tuple-element.47), channel_id=1, source_target_pairs={{0,4},{1,5},{2,6},{3,7},{4,0},{5,1},{6,2},{7,3},{8,12},{9,13},{10,... | collective-permute-start | bytes 491528 | tf_op jit(solution)/shard_map/ppermute | solution.py:52
  10.0 6.9 %collective-permute-start.4 = (f32[40,8,128]{2,1,0:T(8,128)S(1)}, f32[40,8,128]{2,1,0:T(8,128)S(1)}, u32[]{:S(2)}, u32[]{:S(2)}) collective-permute-start(f32[40,8,128]{2,1,0:T(8,128)S(1)} %get-tuple-element.48), channel_id=1, source_target_pairs={{0,1},{1,0},{2,3},{3,2},{4,8},{5,9},{6,10},{7,11},{8,4},{9,5},{10,... | collective-permute-start | bytes 491528 | tf_op jit(solution)/shard_map/ppermute | solution.py:51

commit v7 on v6

--- a/solution.py
+++ b/solution.py
@@ -54,7 +54,7 @@
 
 
 def everywhere(copies):
-    return lax.all_to_all(copies, ("gx", "gy"), 0, 0)
+    return lax.all_to_all(copies, ("gy", "gx"), 0, 0)
 
 
 def is_odd(axis):
@@ -506,7 +506,7 @@
     def unpack(i):
         for x in range(UNPACK):
             for y in range(gy_count):
-                both = got[(i + x) * gy_count + y]
+                both = got[y * count + i + x]
                 g2[i + x, y * block2 : (y + 1) * block2, :] = both[:block2]
                 h2[i + x, y * block2 : (y + 1) * block2, :] = both[block2:]
 
@@ -591,7 +591,7 @@
     def unpack(i):
         for x in range(UNPACK):
             for y in range(gy_count):
-                g2[i + x, y * block2 : (y + 1) * block2, :] = got[(i + x) * gy_count + y]
+                g2[i + x, y * block2 : (y + 1) * block2, :] = got[y * count + i + x]
 
     slabs(0, count, UNPACK, unpack)
     values = [ref[...] for ref in levels]

time: 45.3 us -> 45.1 us (level)
  no operation moved by 1% of the time
where the time goes in v7:
time: 45.1 us; the launch traced here: 44.9 us
  blocking collectives  22 us (49%)
  starting transfers between devices  9.36 us (21%)
  Pallas kernels  7.4 us (16%)
  waiting for transfers between devices  3.66 us (8%)
  local copies, waits for them, and re-layouts  2.46 us (5%)
    all_to_all x2, blocking collectives, everywhere(): return lax.all_to_all(copies, ('gy', 'gx'), 0, 0)  22 us
    pallas_call x7, Pallas kernels, kernel_call(): pl.pallas_call(body, out_shape=[jax.ShapeDtypeStruct(s, F32) for s in out...  7.4 us
    ppermute x4, starting transfers between devices, trade(): from_far = lax.ppermute(to_far, ('gx', 'gy'), route(axis, True))  5.65 us
    ppermute x4, starting transfers between devices, trade(): from_near = lax.ppermute(to_near, ('gx', 'gy'), route(axis, False))  3.72 us
    ppermute x4, waiting for transfers between devices, trade(): from_near = lax.ppermute(to_near, ('gx', 'gy'), route(axis, False))  2.8 us
    unnamed x6, local copies, waits for them, and re-layouts  2.46 us
  transfers between devices with their start and end apart: 8, of which 3 were waited for; matrix products, arithmetic and copies ran while one was open for 0% of the time, Pallas kernels for 3%

profile of v7, /device:TPU:0, one launch (start us, length us, event | category | flops | bytes accessed | tf_op | source)
XLA Modules:
  0.0 44.9 jit_solution(15603749727816128000)
XLA Ops:
  0.0 0.5 %collective-permute-start = (s32[16,16,128]{2,1,0:T(8,128)}, s32[16,16,128]{2,1,0:T(8,128)S(1)}, u32[]{:S(2)}, u32[]{:S(2)}) collective-permute-start(s32[16,16,128]{2,1,0:T(8,128)} %material.1), channel_id=1, source_target_pairs={{0,4},{1,5},{2,6},{3,7},{4,0},{5,1},{6,2},{7,3},{8,12},{9,13},{10,... | collective-permute-start | bytes 393224 | tf_op jit(solution)/shard_map/ppermute | solution.py:52
  0.5 2.6 %collective-permute-start.5 = (s32[16,16,128]{2,1,0:T(8,128)}, s32[16,16,128]{2,1,0:T(8,128)S(1)}, u32[]{:S(2)}, u32[]{:S(2)}) collective-permute-start(s32[16,16,128]{2,1,0:T(8,128)} %material.1), channel_id=1, source_target_pairs={{0,1},{1,0},{2,3},{3,2},{4,8},{5,9},{6,10},{7,11},{8,4},{9,5},{10,... | collective-permute-start | bytes 393224 | tf_op jit(solution)/shard_map/ppermute | solution.py:51
  3.0 0.0 collective-permute-start.2
  3.1 3.1 %collective-permute-start.1 = (f32[16,16,128]{2,1,0:T(8,128)}, f32[16,16,128]{2,1,0:T(8,128)S(1)}, u32[]{:S(2)}, u32[]{:S(2)}) collective-permute-start(f32[16,16,128]{2,1,0:T(8,128)} %right_in.1), channel_id=1, source_target_pairs={{0,1},{1,0},{2,3},{3,2},{4,5},{5,4},{6,7},{7,6},{8,9},{9,8},{10,11... | collective-permute-start | bytes 393224 | tf_op jit(solution)/shard_map/ppermute | solution.py:52
  6.2 0.0 collective-permute-done.near
  6.2 0.0 copy-start
  6.2 0.9 %copy-done = s32[16,16,128]{2,1,0:T(8,128)S(1)} copy-done((s32[16,16,128]{2,1,0:T(8,128)S(1)}, s32[16,16,128]{2,1,0:T(8,128)}, u32[]{:S(2)}) %copy-start) | copy-done | bytes 131096
  7.1 0.0 copy-start.1
  7.1 0.9 %copy-done.1 = f32[16,16,128]{2,1,0:T(8,128)S(1)} copy-done((f32[16,16,128]{2,1,0:T(8,128)S(1)}, f32[16,16,128]{2,1,0:T(8,128)}, u32[]{:S(2)}) %copy-start.1) | copy-done | bytes 131096
  8.0 0.0 copy-start.2
  8.0 0.7 %copy-done.2 = f32[16]{0:T(128)S(1)} copy-done((f32[16]{0:T(128)S(1)}, f32[16]{0:T(128)}, u32[]{:S(2)}) %copy-start.2) | copy-done | bytes 88
  8.7 0.2 shard_map.37
  8.9 0.0 collective-permute-done.5.far
  8.9 0.2 shard_map.39
  9.1 0.1 collective-permute-start.6
  9.1 0.4 collective-permute-start.7
  9.5 0.0 collective-permute-done.2.far
  9.5 0.3 collective-permute-done.1.near
  9.8 0.1 shard_map.38
  9.9 0.1 collective-permute-start.3
  10.0 2.7 %collective-permute-start.4 = (f32[40,8,128]{2,1,0:T(8,128)S(1)}, f32[40,8,128]{2,1,0:T(8,128)S(1)}, u32[]{:S(2)}, u32[]{:S(2)}) collective-permute-start(f32[40,8,128]{2,1,0:T(8,128)S(1)} %get-tuple-element.48), channel_id=1, source_target_pairs={{0,1},{1,0},{2,3},{3,2},{4,8},{5,9},{6,10},{7,11},{8,4},{9,5},{10,... | collective-permute-start | bytes 491528 | tf_op jit(solution)/shard_map/ppermute | solution.py:51
  12.7 2.5 %collective-permute-done.6.k_near = f32[45,8,128]{2,1,0:T(8,128)S(1)} collective-permute-done((f32[45,8,128]{2,1,0:T(8,128)S(1)}, f32[45,8,128]{2,1,0:T(8,128)S(1)}, u32[]{:S(2)}, u32[]{:S(2)}) %collective-permute-start.6) | collective-permute-done | bytes 184352 | tf_op jit(solution)/shard_map/ppermute | solution.py:52
  15.1 0.0 collective-permute-done.7.k_far
  15.1 0.9 %shard_map.40 = (f32[42,56,128]{2,1,0:T(8,128)S(1)}, f32[40,56,128]{2,1,0:T(8,128)S(1)}, f32[40,56,128]{2,1,0:T(8,128)S(1)}, f32[40,56,128]{2,1,0:T(8,128)S(1)},...) custom-call(f32[40,16,128]{2,1,0:T(8,128)S(1)} %get-tuple-element.52, ...), custom_call_target="tpu_custom_call" | custom-call | tf_op jit(solution)/shard_map/pallas_call | solution.py:650
  16.0 0.0 collective-permute-done.3.g_near
  16.0 0.9 %collective-permute-done.4.g_far = f32[40,8,128]{2,1,0:T(8,128)S(1)} collective-permute-done((f32[40,8,128]{2,1,0:T(8,128)S(1)}, f32[40,8,128]{2,1,0:T(8,128)S(1)}, u32[]{:S(2)}, u32[]{:S(2)}) %collective-permute-start.4) | collective-permute-done | bytes 163872 | tf_op jit(solution)/shard_map/ppermute | solution.py:51
  16.9 1.1 %shard_map.41 = (f32[32,8,128]{2,1,0:T(8,128)S(1)}, f32[40,48,128]{2,1,0:T(8,128)S(1)}, f32[42,56,128]{2,1,0:T(8,128)S(1)}, f32[22,40,128]{2,1,0:T(8,128)S(1)}, f32[20,40,128]{2,1,0:T(8,128)S(1)}) custom-call(f32[16,48,128]{2,1,0:T(8,128)S(1)} %get-tuple-element.46.g_wide, f32[40,8,128]{2,1,0:T(8,128)S(1)} %collective-permute-done.3.g_near, ...), custom_call_target="tpu_custom_call" | custom-call | tf_op jit(solution)/shard_map/pallas_call | solution.py:650
  18.0 12.8 %all_to_all.10.got = f32[32,8,128]{2,1,0:T(8,128)S(1)} all-to-all(f32[32,8,128]{2,1,0:T(8,128)S(1)} %get-tuple-element.64), channel_id=1, replica_groups=mesh['gx'=8,'gy'=4] {'gy','gx'}, dimensions={0} | all-to-all | bytes 262144 | tf_op jit(solution)/shard_map/all_to_all | solution.py:57
  30.8 3.0 %shard_map.42 = (f32[32,4,128]{2,1,0:T(4,128)S(1)}, f32[42,56,128]{2,1,0:T(8,128)S(1)}, f32[22,40,128]{2,1,0:T(8,128)S(1)}, f32[20,40,128]{2,1,0:T(8,128)S(1)}, ...) custom-call(f32[32,8,128]{2,1,0:T(8,128)S(1)} %all_to_all.10.got, ...), custom_call_target="tpu_custom_call" | custom-call | tf_op jit(solution)/shard_map/pallas_call | solution.py:650
  33.8 9.2 %all_to_all.11.got = f32[32,4,128]{2,1,0:T(4,128)S(1)} all-to-all(f32[32,4,128]{2,1,0:T(4,128)S(1)} %get-tuple-element.70), channel_id=1, replica_groups=mesh['gx'=8,'gy'=4] {'gy','gx'}, dimensions={0} | all-to-all | bytes 131072 | tf_op jit(solution)/shard_map/all_to_all | solution.py:57
  43.0 1.9 %shard_map.43 = f32[16,16,128]{2,1,0:T(8,128)} custom-call(f32[32,4,128]{2,1,0:T(4,128)S(1)} %all_to_all.11.got, f32[40,48,128]{2,1,0:T(8,128)S(1)} %get-tuple-element.65.g0, f32[42,56,128]{2,1,0:T(8,128)S(1)} %get-tuple-element.55.wx0, f32[40,56,128]{2,1,0:T(8,128)S(1)} %get-tuple-element.56.wy0, f32[40,56,128]{2,1,0:T(8,128)S(1)} %get-tuple-element.57.wz0, ...), custom_call_target="tpu_custom_call" | custom-call | tf_op jit(solution)/shard_map/pallas_call | solution.py:650
Async XLA Ops:
  0.0 6.2 %collective-permute-start = (s32[16,16,128]{2,1,0:T(8,128)}, s32[16,16,128]{2,1,0:T(8,128)S(1)}, u32[]{:S(2)}, u32[]{:S(2)}) collective-permute-start(s32[16,16,128]{2,1,0:T(8,128)} %material.1), channel_id=1, source_target_pairs={{0,4},{1,5},{2,6},{3,7},{4,0},{5,1},{6,2},{7,3},{8,12},{9,13},{10,... | collective-permute-start | bytes 393224 | tf_op jit(solution)/shard_map/ppermute | solution.py:52
  0.5 8.4 %collective-permute-start.5 = (s32[16,16,128]{2,1,0:T(8,128)}, s32[16,16,128]{2,1,0:T(8,128)S(1)}, u32[]{:S(2)}, u32[]{:S(2)}) collective-permute-start(s32[16,16,128]{2,1,0:T(8,128)} %material.1), channel_id=1, source_target_pairs={{0,1},{1,0},{2,3},{3,2},{4,8},{5,9},{6,10},{7,11},{8,4},{9,5},{10,... | collective-permute-start | bytes 393224 | tf_op jit(solution)/shard_map/ppermute | solution.py:51
  3.0 6.5 %collective-permute-start.2 = (f32[16,16,128]{2,1,0:T(8,128)}, f32[16,16,128]{2,1,0:T(8,128)S(1)}, u32[]{:S(2)}, u32[]{:S(2)}) collective-permute-start(f32[16,16,128]{2,1,0:T(8,128)} %right_in.1), channel_id=1, source_target_pairs={{0,4},{1,2},{2,1},{3,7},{4,0},{5,6},{6,5},{7,3},{8,12},{9,10},{10,... | collective-permute-start | bytes 393224 | tf_op jit(solution)/shard_map/ppermute | solution.py:51
  3.1 6.8 %collective-permute-start.1 = (f32[16,16,128]{2,1,0:T(8,128)}, f32[16,16,128]{2,1,0:T(8,128)S(1)}, u32[]{:S(2)}, u32[]{:S(2)}) collective-permute-start(f32[16,16,128]{2,1,0:T(8,128)} %right_in.1), channel_id=1, source_target_pairs={{0,1},{1,0},{2,3},{3,2},{4,5},{5,4},{6,7},{7,6},{8,9},{9,8},{10,11... | collective-permute-start | bytes 393224 | tf_op jit(solution)/shard_map/ppermute | solution.py:52
  6.2 0.9 %copy-start = (s32[16,16,128]{2,1,0:T(8,128)S(1)}, s32[16,16,128]{2,1,0:T(8,128)}, u32[]{:S(2)}) copy-start(s32[16,16,128]{2,1,0:T(8,128)} %material.1) | copy-start | bytes 393220
  7.1 0.9 %copy-start.1 = (f32[16,16,128]{2,1,0:T(8,128)S(1)}, f32[16,16,128]{2,1,0:T(8,128)}, u32[]{:S(2)}) copy-start(f32[16,16,128]{2,1,0:T(8,128)} %right_in.1) | copy-start | bytes 393220
  8.0 0.7 %copy-start.2 = (f32[16]{0:T(128)S(1)}, f32[16]{0:T(128)}, u32[]{:S(2)}) copy-start(f32[16]{0:T(128)} %param.5) | copy-start | bytes 196
  9.1 6.1 %collective-permute-start.6 = (f32[45,8,128]{2,1,0:T(8,128)S(1)}, f32[45,8,128]{2,1,0:T(8,128)S(1)}, u32[]{:S(2)}, u32[]{:S(2)}) collective-permute-start(f32[45,8,128]{2,1,0:T(8,128)S(1)} %get-tuple-element.53), channel_id=1, source_target_pairs={{0,1},{1,0},{2,3},{3,2},{4,5},{5,4},{6,7},{7,6},{8,9},{9,8},{10,11... | collective-permute-start | bytes 552968 | tf_op jit(solution)/shard_map/ppermute | solution.py:52
  9.1 6.0 %collective-permute-start.7 = (f32[45,8,128]{2,1,0:T(8,128)S(1)}, f32[45,8,128]{2,1,0:T(8,128)S(1)}, u32[]{:S(2)}, u32[]{:S(2)}) collective-permute-start(f32[45,8,128]{2,1,0:T(8,128)S(1)} %get-tuple-element.54), channel_id=1, source_target_pairs={{0,4},{1,2},{2,1},{3,7},{4,0},{5,6},{6,5},{7,3},{8,12},{9,10},{10,... | collective-permute-start | bytes 552968 | tf_op jit(solution)/shard_map/ppermute | solution.py:51
  9.9 6.1 %collective-permute-start.3 = (f32[40,8,128]{2,1,0:T(8,128)S(1)}, f32[40,8,128]{2,1,0:T(8,128)S(1)}, u32[]{:S(2)}, u32[]{:S(2)}) collective-permute-start(f32[40,8,128]{2,1,0:T(8,128)S(1)} %get-tuple-element.47), channel_id=1, source_target_pairs={{0,4},{1,5},{2,6},{3,7},{4,0},{5,1},{6,2},{7,3},{8,12},{9,13},{10,... | collective-permute-start | bytes 491528 | tf_op jit(solution)/shard_map/ppermute | solution.py:52
  10.0 6.9 %collective-permute-start.4 = (f32[40,8,128]{2,1,0:T(8,128)S(1)}, f32[40,8,128]{2,1,0:T(8,128)S(1)}, u32[]{:S(2)}, u32[]{:S(2)}) collective-permute-start(f32[40,8,128]{2,1,0:T(8,128)S(1)} %get-tuple-element.48), channel_id=1, source_target_pairs={{0,1},{1,0},{2,3},{3,2},{4,8},{5,9},{6,10},{7,11},{8,4},{9,5},{10,... | collective-permute-start | bytes 491528 | tf_op jit(solution)/shard_map/ppermute | solution.py:51

commit v8 on v7

--- a/solution.py
+++ b/solution.py
@@ -543,8 +543,8 @@
     rows = block + 16
     aU0 = (u0, 1, BASE - (HALO - 7))
     aE0 = (e0, 0, -(2 * low - 8))
-    aV0M = (v0m, 1, BASE - (HALO - 6))
-    aV0N = (v0n, 1, BASE - (HALO - 5))
+    aV0M = (v0m, 1, BASE // 2)
+    aV0N = (v0n, 1, BASE // 2)
     size = block + 16
 
     def correct(i):
@@ -554,17 +554,14 @@
 
     slabs(HALO - 8, planes - HALO + 8, size, correct)
 
-    def sweep(source, target, margin, size):
-        def body(i):
-            window = (i, size, HALO - margin, rows)
+    def sweep(source, target, margin):
+        for window in diamond(planes, planes, margin):
             here, around = spread(source, w0, window, 1)
             value = KEEP * here + read(aINV0, *window) * (read(aG0, *window) + around)
-            write(target, i, HALO - margin, value)
-
-        slabs(HALO - margin, planes - HALO + margin, size, body)
-
-    sweep(aU0, aV0M, 6, block + 12)
-    sweep(aV0M, aV0N, 5, block + 10)
+            write(target, window[0], window[2], value)
+
+    sweep(aU0, aV0M, 6)
+    sweep(aV0M, aV0N, 5)
 
     aG1N, aV1N = (g1n, 0, BASE - (low - 2)), (v1n, 1, BASE - (low - 2))
     window = (HALO - 4, block + 8, HALO - 4, block + 8)
@@ -606,7 +603,7 @@
     low, block1 = HALO // 2, block // 2
     aINV1 = (inv1, 0, BASE)
     aG1N, aV1N = (g1n, 0, BASE - (low - 2)), (v1n, 1, BASE - (low - 2))
-    aV0N = (v0n, 1, BASE - (HALO - 5))
+    aV0N = (v0n, 1, BASE // 2)
 
     aU1 = (u1, 1, BASE - (low - 2))
     window = (low - 2, block1 + 4, low - 2, block1 + 4)

time: 45.1 us -> 45 us (level)
  no operation moved by 1% of the time
where the time goes in v8:
time: 45 us; the launch traced here: 44.9 us
  blocking collectives  22 us (49%)
  starting transfers between devices  9.36 us (21%)
  Pallas kernels  7.34 us (16%)
  waiting for transfers between devices  3.66 us (8%)
  local copies, waits for them, and re-layouts  2.46 us (5%)
    all_to_all x2, blocking collectives, everywhere(): return lax.all_to_all(copies, ('gy', 'gx'), 0, 0)  22 us
    pallas_call x7, Pallas kernels, kernel_call(): pl.pallas_call(body, out_shape=[jax.ShapeDtypeStruct(s, F32) for s in out...  7.34 us
    ppermute x4, starting transfers between devices, trade(): from_far = lax.ppermute(to_far, ('gx', 'gy'), route(axis, True))  5.65 us
    ppermute x4, starting transfers between devices, trade(): from_near = lax.ppermute(to_near, ('gx', 'gy'), route(axis, False))  3.72 us
    ppermute x4, waiting for transfers between devices, trade(): from_near = lax.ppermute(to_near, ('gx', 'gy'), route(axis, False))  2.8 us
    unnamed x6, local copies, waits for them, and re-layouts  2.46 us
  transfers between devices with their start and end apart: 8, of which 3 were waited for; matrix products, arithmetic and copies ran while one was open for 0% of the time, Pallas kernels for 3%

profile of v8, /device:TPU:0, one launch (start us, length us, event | category | flops | bytes accessed | tf_op | source)
XLA Modules:
  0.0 44.9 jit_solution(10955632366652042007)
XLA Ops:
  0.0 0.5 %collective-permute-start = (s32[16,16,128]{2,1,0:T(8,128)}, s32[16,16,128]{2,1,0:T(8,128)S(1)}, u32[]{:S(2)}, u32[]{:S(2)}) collective-permute-start(s32[16,16,128]{2,1,0:T(8,128)} %material.1), channel_id=1, source_target_pairs={{0,4},{1,5},{2,6},{3,7},{4,0},{5,1},{6,2},{7,3},{8,12},{9,13},{10,... | collective-permute-start | bytes 393224 | tf_op jit(solution)/shard_map/ppermute | solution.py:52
  0.5 2.6 %collective-permute-start.5 = (s32[16,16,128]{2,1,0:T(8,128)}, s32[16,16,128]{2,1,0:T(8,128)S(1)}, u32[]{:S(2)}, u32[]{:S(2)}) collective-permute-start(s32[16,16,128]{2,1,0:T(8,128)} %material.1), channel_id=1, source_target_pairs={{0,1},{1,0},{2,3},{3,2},{4,8},{5,9},{6,10},{7,11},{8,4},{9,5},{10,... | collective-permute-start | bytes 393224 | tf_op jit(solution)/shard_map/ppermute | solution.py:51
  3.0 0.0 collective-permute-start.2
  3.1 3.1 %collective-permute-start.1 = (f32[16,16,128]{2,1,0:T(8,128)}, f32[16,16,128]{2,1,0:T(8,128)S(1)}, u32[]{:S(2)}, u32[]{:S(2)}) collective-permute-start(f32[16,16,128]{2,1,0:T(8,128)} %right_in.1), channel_id=1, source_target_pairs={{0,1},{1,0},{2,3},{3,2},{4,5},{5,4},{6,7},{7,6},{8,9},{9,8},{10,11... | collective-permute-start | bytes 393224 | tf_op jit(solution)/shard_map/ppermute | solution.py:52
  6.2 0.0 collective-permute-done.near
  6.2 0.0 copy-start
  6.2 0.9 %copy-done = s32[16,16,128]{2,1,0:T(8,128)S(1)} copy-done((s32[16,16,128]{2,1,0:T(8,128)S(1)}, s32[16,16,128]{2,1,0:T(8,128)}, u32[]{:S(2)}) %copy-start) | copy-done | bytes 131096
  7.1 0.0 copy-start.1
  7.1 0.9 %copy-done.1 = f32[16,16,128]{2,1,0:T(8,128)S(1)} copy-done((f32[16,16,128]{2,1,0:T(8,128)S(1)}, f32[16,16,128]{2,1,0:T(8,128)}, u32[]{:S(2)}) %copy-start.1) | copy-done | bytes 131096
  8.0 0.0 copy-start.2
  8.0 0.7 %copy-done.2 = f32[16]{0:T(128)S(1)} copy-done((f32[16]{0:T(128)S(1)}, f32[16]{0:T(128)}, u32[]{:S(2)}) %copy-start.2) | copy-done | bytes 88
  8.7 0.2 shard_map.37
  8.9 0.0 collective-permute-done.5.far
  8.9 0.2 shard_map.39
  9.1 0.1 collective-permute-start.6
  9.1 0.4 collective-permute-start.7
  9.5 0.0 collective-permute-done.2.far
  9.5 0.3 collective-permute-done.1.near
  9.8 0.1 shard_map.38
  9.9 0.1 collective-permute-start.3
  10.0 2.7 %collective-permute-start.4 = (f32[40,8,128]{2,1,0:T(8,128)S(1)}, f32[40,8,128]{2,1,0:T(8,128)S(1)}, u32[]{:S(2)}, u32[]{:S(2)}) collective-permute-start(f32[40,8,128]{2,1,0:T(8,128)S(1)} %get-tuple-element.48), channel_id=1, source_target_pairs={{0,1},{1,0},{2,3},{3,2},{4,8},{5,9},{6,10},{7,11},{8,4},{9,5},{10,... | collective-permute-start | bytes 491528 | tf_op jit(solution)/shard_map/ppermute | solution.py:51
  12.7 2.5 %collective-permute-done.6.k_near = f32[45,8,128]{2,1,0:T(8,128)S(1)} collective-permute-done((f32[45,8,128]{2,1,0:T(8,128)S(1)}, f32[45,8,128]{2,1,0:T(8,128)S(1)}, u32[]{:S(2)}, u32[]{:S(2)}) %collective-permute-start.6) | collective-permute-done | bytes 184352 | tf_op jit(solution)/shard_map/ppermute | solution.py:52
  15.1 0.0 collective-permute-done.7.k_far
  15.1 0.9 %shard_map.40 = (f32[42,56,128]{2,1,0:T(8,128)S(1)}, f32[40,56,128]{2,1,0:T(8,128)S(1)}, f32[40,56,128]{2,1,0:T(8,128)S(1)}, f32[40,56,128]{2,1,0:T(8,128)S(1)},...) custom-call(f32[40,16,128]{2,1,0:T(8,128)S(1)} %get-tuple-element.52, ...), custom_call_target="tpu_custom_call" | custom-call | tf_op jit(solution)/shard_map/pallas_call | solution.py:647
  16.0 0.0 collective-permute-done.3.g_near
  16.0 0.9 %collective-permute-done.4.g_far = f32[40,8,128]{2,1,0:T(8,128)S(1)} collective-permute-done((f32[40,8,128]{2,1,0:T(8,128)S(1)}, f32[40,8,128]{2,1,0:T(8,128)S(1)}, u32[]{:S(2)}, u32[]{:S(2)}) %collective-permute-start.4) | collective-permute-done | bytes 163872 | tf_op jit(solution)/shard_map/ppermute | solution.py:51
  16.9 1.1 %shard_map.41 = (f32[32,8,128]{2,1,0:T(8,128)S(1)}, f32[40,48,128]{2,1,0:T(8,128)S(1)}, f32[42,56,128]{2,1,0:T(8,128)S(1)}, f32[22,40,128]{2,1,0:T(8,128)S(1)}, f32[20,40,128]{2,1,0:T(8,128)S(1)}) custom-call(f32[16,48,128]{2,1,0:T(8,128)S(1)} %get-tuple-element.46.g_wide, f32[40,8,128]{2,1,0:T(8,128)S(1)} %collective-permute-done.3.g_near, ...), custom_call_target="tpu_custom_call" | custom-call | tf_op jit(solution)/shard_map/pallas_call | solution.py:647
  18.0 12.8 %all_to_all.10.got = f32[32,8,128]{2,1,0:T(8,128)S(1)} all-to-all(f32[32,8,128]{2,1,0:T(8,128)S(1)} %get-tuple-element.64), channel_id=1, replica_groups=mesh['gx'=8,'gy'=4] {'gy','gx'}, dimensions={0} | all-to-all | bytes 262144 | tf_op jit(solution)/shard_map/all_to_all | solution.py:57
  30.8 2.9 %shard_map.42 = (f32[32,4,128]{2,1,0:T(4,128)S(1)}, f32[42,56,128]{2,1,0:T(8,128)S(1)}, f32[22,40,128]{2,1,0:T(8,128)S(1)}, f32[20,40,128]{2,1,0:T(8,128)S(1)}, ...) custom-call(f32[32,8,128]{2,1,0:T(8,128)S(1)} %all_to_all.10.got, ...), custom_call_target="tpu_custom_call" | custom-call | tf_op jit(solution)/shard_map/pallas_call | solution.py:647
  33.7 9.2 %all_to_all.11.got = f32[32,4,128]{2,1,0:T(4,128)S(1)} all-to-all(f32[32,4,128]{2,1,0:T(4,128)S(1)} %get-tuple-element.70), channel_id=1, replica_groups=mesh['gx'=8,'gy'=4] {'gy','gx'}, dimensions={0} | all-to-all | bytes 131072 | tf_op jit(solution)/shard_map/all_to_all | solution.py:57
  42.9 1.9 %shard_map.43 = f32[16,16,128]{2,1,0:T(8,128)} custom-call(f32[32,4,128]{2,1,0:T(4,128)S(1)} %all_to_all.11.got, f32[40,48,128]{2,1,0:T(8,128)S(1)} %get-tuple-element.65.g0, f32[42,56,128]{2,1,0:T(8,128)S(1)} %get-tuple-element.55.wx0, f32[40,56,128]{2,1,0:T(8,128)S(1)} %get-tuple-element.56.wy0, f32[40,56,128]{2,1,0:T(8,128)S(1)} %get-tuple-element.57.wz0, ...), custom_call_target="tpu_custom_call" | custom-call | tf_op jit(solution)/shard_map/pallas_call | solution.py:647
Async XLA Ops:
  0.0 6.2 %collective-permute-start = (s32[16,16,128]{2,1,0:T(8,128)}, s32[16,16,128]{2,1,0:T(8,128)S(1)}, u32[]{:S(2)}, u32[]{:S(2)}) collective-permute-start(s32[16,16,128]{2,1,0:T(8,128)} %material.1), channel_id=1, source_target_pairs={{0,4},{1,5},{2,6},{3,7},{4,0},{5,1},{6,2},{7,3},{8,12},{9,13},{10,... | collective-permute-start | bytes 393224 | tf_op jit(solution)/shard_map/ppermute | solution.py:52
  0.5 8.4 %collective-permute-start.5 = (s32[16,16,128]{2,1,0:T(8,128)}, s32[16,16,128]{2,1,0:T(8,128)S(1)}, u32[]{:S(2)}, u32[]{:S(2)}) collective-permute-start(s32[16,16,128]{2,1,0:T(8,128)} %material.1), channel_id=1, source_target_pairs={{0,1},{1,0},{2,3},{3,2},{4,8},{5,9},{6,10},{7,11},{8,4},{9,5},{10,... | collective-permute-start | bytes 393224 | tf_op jit(solution)/shard_map/ppermute | solution.py:51
  3.0 6.5 %collective-permute-start.2 = (f32[16,16,128]{2,1,0:T(8,128)}, f32[16,16,128]{2,1,0:T(8,128)S(1)}, u32[]{:S(2)}, u32[]{:S(2)}) collective-permute-start(f32[16,16,128]{2,1,0:T(8,128)} %right_in.1), channel_id=1, source_target_pairs={{0,4},{1,2},{2,1},{3,7},{4,0},{5,6},{6,5},{7,3},{8,12},{9,10},{10,... | collective-permute-start | bytes 393224 | tf_op jit(solution)/shard_map/ppermute | solution.py:51
  3.1 6.8 %collective-permute-start.1 = (f32[16,16,128]{2,1,0:T(8,128)}, f32[16,16,128]{2,1,0:T(8,128)S(1)}, u32[]{:S(2)}, u32[]{:S(2)}) collective-permute-start(f32[16,16,128]{2,1,0:T(8,128)} %right_in.1), channel_id=1, source_target_pairs={{0,1},{1,0},{2,3},{3,2},{4,5},{5,4},{6,7},{7,6},{8,9},{9,8},{10,11... | collective-permute-start | bytes 393224 | tf_op jit(solution)/shard_map/ppermute | solution.py:52
  6.2 0.9 %copy-start = (s32[16,16,128]{2,1,0:T(8,128)S(1)}, s32[16,16,128]{2,1,0:T(8,128)}, u32[]{:S(2)}) copy-start(s32[16,16,128]{2,1,0:T(8,128)} %material.1) | copy-start | bytes 393220
  7.1 0.9 %copy-start.1 = (f32[16,16,128]{2,1,0:T(8,128)S(1)}, f32[16,16,128]{2,1,0:T(8,128)}, u32[]{:S(2)}) copy-start(f32[16,16,128]{2,1,0:T(8,128)} %right_in.1) | copy-start | bytes 393220
  8.0 0.7 %copy-start.2 = (f32[16]{0:T(128)S(1)}, f32[16]{0:T(128)}, u32[]{:S(2)}) copy-start(f32[16]{0:T(128)} %param.5) | copy-start | bytes 196
  9.1 6.1 %collective-permute-start.6 = (f32[45,8,128]{2,1,0:T(8,128)S(1)}, f32[45,8,128]{2,1,0:T(8,128)S(1)}, u32[]{:S(2)}, u32[]{:S(2)}) collective-permute-start(f32[45,8,128]{2,1,0:T(8,128)S(1)} %get-tuple-element.53), channel_id=1, source_target_pairs={{0,1},{1,0},{2,3},{3,2},{4,5},{5,4},{6,7},{7,6},{8,9},{9,8},{10,11... | collective-permute-start | bytes 552968 | tf_op jit(solution)/shard_map/ppermute | solution.py:52
  9.1 6.0 %collective-permute-start.7 = (f32[45,8,128]{2,1,0:T(8,128)S(1)}, f32[45,8,128]{2,1,0:T(8,128)S(1)}, u32[]{:S(2)}, u32[]{:S(2)}) collective-permute-start(f32[45,8,128]{2,1,0:T(8,128)S(1)} %get-tuple-element.54), channel_id=1, source_target_pairs={{0,4},{1,2},{2,1},{3,7},{4,0},{5,6},{6,5},{7,3},{8,12},{9,10},{10,... | collective-permute-start | bytes 552968 | tf_op jit(solution)/shard_map/ppermute | solution.py:51
  9.9 6.1 %collective-permute-start.3 = (f32[40,8,128]{2,1,0:T(8,128)S(1)}, f32[40,8,128]{2,1,0:T(8,128)S(1)}, u32[]{:S(2)}, u32[]{:S(2)}) collective-permute-start(f32[40,8,128]{2,1,0:T(8,128)S(1)} %get-tuple-element.47), channel_id=1, source_target_pairs={{0,4},{1,5},{2,6},{3,7},{4,0},{5,1},{6,2},{7,3},{8,12},{9,13},{10,... | collective-permute-start | bytes 491528 | tf_op jit(solution)/shard_map/ppermute | solution.py:52
  10.0 6.9 %collective-permute-start.4 = (f32[40,8,128]{2,1,0:T(8,128)S(1)}, f32[40,8,128]{2,1,0:T(8,128)S(1)}, u32[]{:S(2)}, u32[]{:S(2)}) collective-permute-start(f32[40,8,128]{2,1,0:T(8,128)S(1)} %get-tuple-element.48), channel_id=1, source_target_pairs={{0,1},{1,0},{2,3},{3,2},{4,8},{5,9},{6,10},{7,11},{8,4},{9,5},{10,... | collective-permute-start | bytes 491528 | tf_op jit(solution)/shard_map/ppermute | solution.py:51
